TPU v7x, 128 devices: a whole 4x4x4 slice. The times are simulated.
128 devices in a mesh: section: 2 (over z_lo), seq: 16 (over y, z_hi, core), tensor: 4 (over x).
Axes of the slice: x: 4, y: 4, z: 4 (z_hi: 2, z_lo: 2; z = z_hi * 2 + z_lo), core: 2. Of those that a mesh axis runs over, the one named last changes fastest.
Arguments:
- tokens: bfloat16 [8192, 8192], P(('section', 'seq')), may hold values from -6 to 6
- w_query: bfloat16 [8192, 4096], P(('section', 'seq'), 'tensor'), may hold values from -0.0625 to 0.0625
- query_gain: float32 [8192], replicated, may hold values from 0.125 to 2
- state_kv: bfloat16 [8192, 1792], P('tensor'), may hold values from -0.0625 to 0.0625
- neighbours: bfloat16 [2, 64, 2, 128, 896], P('section', ('seq', 'tensor')), may hold values from -6 to 6
- enc_gain: float32 [896], replicated, may hold values from 0.5 to 2
- enc_query: bfloat16 [896, 896], replicated, may hold values from -0.1875 to 0.1875
- enc_out: bfloat16 [896, 896], replicated, may hold values from -0.1875 to 0.1875
- w_key: bfloat16 [896, 4096], P(None, 'tensor'), may hold values from -0.1875 to 0.1875
- w_value: bfloat16 [896, 4096], P(None, 'tensor'), may hold values from -0.1875 to 0.1875
- counts: int32 [128], P(('section', 'seq')), may hold values from 0 to 2
- d_context: bfloat16 [8192, 4096], P(('section', 'seq'), 'tensor'), may hold values from -1.5 to 1.5
Outputs:
- context: bfloat16 [8192, 4096], P(('section', 'seq'), 'tensor')
- d_hidden: bfloat16 [8192, 8192], P(('section', 'seq'), 'tensor')
- d_query_weight: float32 [8192, 4096], P(('section', 'seq'), 'tensor')
- d_encoded: bfloat16 [2, 64, 2, 128, 896], P('section', ('seq', 'tensor'))
- row_dots: float32 [8192], P(('section', 'seq'))
Inputs may be any that keep to these rules, and one draw needn't show every extreme that they name: `counts`: slots of a block from its count on hold padding.
All inputs are finite; a program needn't handle non-finite values.
Results may differ from a plain program's by a relative error of at most 0.039.
Values may be sent and summed in bfloat16 or wider, within the bound.
A program may use at most 192 MiB of HBM per device.

v0:
```python
import math

import jax
import jax.numpy as jnp
from jax import lax
from jax.sharding import PartitionSpec as P

HD = 128
E = 896
EHD = 64
BLOCK = 64
NBR = 2
RLEN = 128


EPSILON = 1e-05
NEG_LARGE = -1e30


def swapped(value, axis, distance):
    mask = 2**distance
    pairs = [(source, source ^ mask) for source in range(lax.axis_size(axis))]
    return lax.ppermute(value, axis, pairs)


def encode(enc_in, block_states, enc_gain, enc_query, enc_out):
    block_count = enc_in.shape[0]
    heads_enc = E // EHD
    enc_rows = enc_in.astype(jnp.float32).reshape(-1, E)
    enc_scale = lax.rsqrt(jnp.mean(enc_rows * enc_rows, axis=-1, keepdims=True) + EPSILON)
    enc_normed = (enc_rows * enc_scale * enc_gain).astype(jnp.bfloat16)
    enc_queries = jnp.dot(enc_normed, enc_query, preferred_element_type=jnp.float32).astype(
        jnp.bfloat16
    )
    query_heads = enc_queries.reshape(block_count, NBR * RLEN, heads_enc, EHD)
    state_rows = block_states.reshape(block_count, BLOCK, 2 * E)
    key_heads = state_rows[:, :, :E].reshape(block_count, BLOCK, heads_enc, EHD)
    value_heads = state_rows[:, :, E:].reshape(block_count, BLOCK, heads_enc, EHD)
    scores = jnp.einsum(
        "cqhd,ckhd->chqk", query_heads, key_heads, preferred_element_type=jnp.float32
    ) / math.sqrt(EHD)
    row_top = jnp.max(scores, axis=-1, keepdims=True)
    weights = jnp.exp(scores - row_top)
    enc_weights = (weights / jnp.sum(weights, axis=-1, keepdims=True)).astype(jnp.bfloat16)
    enc_context = (
        jnp.einsum("chqk,ckhd->cqhd", enc_weights, value_heads, preferred_element_type=jnp.float32)
        .astype(jnp.bfloat16)
        .reshape(-1, E)
    )
    mixed = enc_rows + jnp.dot(enc_context, enc_out, preferred_element_type=jnp.float32)
    return mixed.astype(jnp.bfloat16).reshape(block_count, NBR, RLEN, E)


def shards(
    tokens,
    w_query,
    query_gain,
    state_kv,
    neighbours,
    enc_gain,
    enc_query,
    enc_out,
    w_key,
    w_value,
    counts,
    d_context,
):
    tensor_count = lax.axis_size("tensor")
    tensor_rank = lax.axis_index("tensor")
    tok_rows, width = tokens.shape
    blocks_here = counts.shape[0]
    local_width = w_query.shape[1]
    heads_here = local_width // HD
    width_share = width // tensor_count
    hidden = tokens.astype(jnp.float32)
    inverse = lax.rsqrt(jnp.mean(hidden * hidden, axis=-1, keepdims=True) + EPSILON)
    unit_full = hidden * inverse
    unit_rows = unit_full.astype(jnp.bfloat16)
    normed = (unit_full * query_gain).astype(jnp.bfloat16)
    unit_share = lax.dynamic_slice_in_dim(unit_rows, tensor_rank * width_share, width_share, 1)
    state_part = jnp.dot(unit_share, state_kv, preferred_element_type=jnp.float32)
    block_states = lax.psum_scatter(
        state_part.astype(jnp.bfloat16), "tensor", scatter_dimension=0, tiled=True
    )
    partner_states = swapped(block_states, "section", 0)
    encoded_there = encode(neighbours[0], partner_states, enc_gain, enc_query, enc_out)
    encoded_home = swapped(encoded_there, "section", 0)
    encoded_all = lax.all_gather(encoded_home, "tensor", axis=0, tiled=True)
    w_full = lax.all_gather(w_query, ("section", "seq"), axis=0, tiled=True)
    queries = jnp.dot(normed, w_full, preferred_element_type=jnp.float32).astype(jnp.bfloat16)
    enc_flat = encoded_all.reshape(-1, E)
    key_rows = jnp.dot(enc_flat, w_key, preferred_element_type=jnp.float32).astype(jnp.bfloat16)
    value_rows = jnp.dot(enc_flat, w_value, preferred_element_type=jnp.float32).astype(jnp.bfloat16)
    query_heads = queries.reshape(blocks_here, BLOCK, heads_here, HD)
    key_heads = key_rows.reshape(blocks_here, NBR * RLEN, heads_here, HD)
    value_heads = value_rows.reshape(blocks_here, NBR * RLEN, heads_here, HD)
    score_scale = 1.0 / math.sqrt(HD)
    scores = (
        jnp.einsum("cqhd,ckhd->chqk", query_heads, key_heads, preferred_element_type=jnp.float32)
        * score_scale
    )
    slot_index = jnp.arange(NBR * RLEN, dtype=jnp.int32) // RLEN
    valid_keys = (slot_index[None, :] < counts[:, None])[:, None, None, :]
    row_top = jnp.max(jnp.where(valid_keys, scores, NEG_LARGE), axis=-1, keepdims=True)
    weights = jnp.where(valid_keys, jnp.exp(scores - row_top), 0.0)
    empty_rows = (counts == 0).astype(jnp.float32)[:, None, None, None]
    attn_probs = weights / (jnp.sum(weights, axis=-1, keepdims=True) + empty_rows)
    attn_weights = attn_probs.astype(jnp.bfloat16)
    context = (
        jnp.einsum("chqk,ckhd->cqhd", attn_weights, value_heads, preferred_element_type=jnp.float32)
        .astype(jnp.bfloat16)
        .reshape(tok_rows, local_width)
    )
    grad_heads = d_context.reshape(blocks_here, BLOCK, heads_here, HD)
    d_values = jnp.einsum(
        "chqk,cqhd->ckhd", attn_weights, grad_heads, preferred_element_type=jnp.float32
    ).astype(jnp.bfloat16)
    d_probs = jnp.einsum(
        "cqhd,ckhd->chqk", grad_heads, value_heads, preferred_element_type=jnp.float32
    )
    d_scores = (
        attn_probs * (d_probs - jnp.sum(attn_probs * d_probs, axis=-1, keepdims=True)) * score_scale
    ).astype(jnp.bfloat16)
    d_queries = (
        jnp.einsum("chqk,ckhd->cqhd", d_scores, key_heads, preferred_element_type=jnp.float32)
        .astype(jnp.bfloat16)
        .reshape(tok_rows, local_width)
    )
    d_keys = jnp.einsum(
        "chqk,cqhd->ckhd", d_scores, query_heads, preferred_element_type=jnp.float32
    ).astype(jnp.bfloat16)
    grad_part = jnp.dot(
        d_keys.reshape(-1, local_width), w_key.T, preferred_element_type=jnp.float32
    )
    grad_part = grad_part + jnp.dot(
        d_values.reshape(-1, local_width), w_value.T, preferred_element_type=jnp.float32
    )
    grad_part = grad_part.reshape(blocks_here, NBR, RLEN, E)
    crossed = swapped(grad_part.astype(jnp.bfloat16), "section", 0)
    d_encoded = lax.psum_scatter(
        crossed.astype(jnp.float32).astype(jnp.bfloat16), "tensor", scatter_dimension=0, tiled=True
    )
    d_encoded = d_encoded[None]
    contract_rows = (((0,), (0,)), ((), ()))
    full_term = lax.dot_general(
        normed, d_queries, contract_rows, preferred_element_type=jnp.float32
    )
    sectioned = full_term.reshape(lax.axis_size("section"), -1, local_width)
    by_seq = lax.psum_scatter(
        sectioned.astype(jnp.bfloat16), "seq", scatter_dimension=1, tiled=True
    )
    d_query_weight = lax.psum_scatter(by_seq, "section", scatter_dimension=0, tiled=True).astype(
        jnp.float32
    )[0]
    normed_part = jnp.dot(d_queries, w_full.T, preferred_element_type=jnp.float32)
    d_normed = lax.psum_scatter(
        normed_part.astype(jnp.bfloat16), "tensor", scatter_dimension=1, tiled=True
    ).astype(jnp.float32)
    gain_share = lax.dynamic_slice_in_dim(query_gain, tensor_rank * width_share, width_share, 0)
    unit_slice = lax.dynamic_slice_in_dim(unit_full, tensor_rank * width_share, width_share, 1)
    d_unit = d_normed * gain_share
    row_sums = lax.psum(jnp.sum(d_unit * unit_slice, axis=-1, keepdims=True), "tensor")
    row_dots = row_sums[:, 0] / math.sqrt(width)
    d_hidden = (inverse * (d_unit - unit_slice * (row_sums / width))).astype(jnp.bfloat16)
    return (context, d_hidden, d_query_weight, d_encoded, row_dots)


def solution(mesh):
    return jax.shard_map(
        shards,
        mesh=mesh,
        in_specs=(
            P(("section", "seq"), None),
            P(("section", "seq"), "tensor"),
            P(),
            P("tensor", None),
            P("section", ("seq", "tensor"), None, None, None),
            P(),
            P(),
            P(),
            P(None, "tensor"),
            P(None, "tensor"),
            P(("section", "seq")),
            P(("section", "seq"), "tensor"),
        ),
        out_specs=(
            P(("section", "seq"), "tensor"),
            P(("section", "seq"), "tensor"),
            P(("section", "seq"), "tensor"),
            P("section", ("seq", "tensor"), None, None, None),
            P(("section", "seq")),
        ),
        check_vma=False,
    )
```

profile of v0, /device:TPU:1, one launch (start us, length us, event | category | flops | bytes accessed | tf_op | source)
XLA Modules:
  0.0 507.1 jit_solution(8647647718983678939)
XLA Ops:
  7.2 3.2 fusion.3
  10.5 8.2 %fusion.25 = (bf16[8192,256]{0,1:T(8,128)(2,1)}, f32[256,8192]{1,0:T(8,128)}) fusion(f32[8192]{0:T(1024)S(1)} %copy-done.7, f32[256]{0:T(256)S(1)} %add_rsqrt_fusion, bf16[256,8192]{1,0:T(8,128)(2,1)} %param.12), kind=kLoop, calls=%fused_computation.42 | loop fusion | flops 8388608 | bytes 16811008 | tf_op jit(solution)/shard_map/dot_general | solution.py:145
  18.7 6.7 %convolution_convert_fusion.2 = bf16[256,1792]{1,0:T(8,128)(2,1)} fusion(bf16[2048,1792]{1,0:T(8,128)(2,1)} %param.15, f32[256,8192]{1,0:T(8,128)} %get-tuple-element.6, s32[]{:T(128)S(6)} %select_n.21), kind=kOutput, calls=%fused_computation.10 | convolution fusion | flops 1879506944 | bytes 9306116 | tf_op jit(solution)/shard_map/dot_general | solution.py:81
  25.9 24.5 %reduce-scatter.6.cloned.1.call-done = bf16[64,1792]{1,0:T(8,128)(2,1)} async-done(((bf16[256,1792]{1,0:T(8,128)(2,1)}), bf16[64,1792]{1,0:T(8,128)(2,1)}) %reduce-scatter.6.cloned.1.call-update) | async-done | bytes 229392 | tf_op jit(solution)/shard_map/reduce_scatter | solution.py:82
  62.9 7.4 %collective-permute-done.1 = bf16[1,2,128,896]{3,2,1,0:T(8,128)(2,1)S(1)} collective-permute-done((bf16[1,2,128,896]{3,2,1,0:T(8,128)(2,1)S(1)}, bf16[1,2,128,896]{3,2,1,0:T(8,128)(2,1)S(1)}, u32[]{:S(2)}, u32[]{:S(2)}) %collective-permute-start.1) | collective-permute-done | bytes 458784 | tf_op jit(solution)/shard_map/ppermute | solution.py:23
  72.1 6.5 %copy.62 = bf16[8192,256]{1,0:T(8,128)(2,1)} copy(bf16[8192,256]{0,1:T(8,128)(2,1)} %get-tuple-element.5) | data formatting | bytes 8388608 | tf_op jit(solution)/shard_map/dot_general | solution.py:145
  78.7 24.4 %all-gather.3.cloned.1.call-done = bf16[4,2,128,896]{3,2,1,0:T(8,128)(2,1)} async-done(((bf16[1,2,128,896]{3,2,1,0:T(8,128)(2,1)}), bf16[4,2,128,896]{3,2,1,0:T(8,128)(2,1)}) %all-gather.3.cloned.1.call-update) | async-done | bytes 1835024 | tf_op jit(solution)/shard_map/all_gather | solution.py:88
  103.1 3.8 convert_bitcast_fusion.3
  115.5 87.0 %all-gather.5.cloned.1.call-done = bf16[8192,1024]{1,0:T(8,128)(2,1)} async-done(((bf16[256,1024]{1,0:T(8,128)(2,1)}), bf16[8192,1024]{1,0:T(8,128)(2,1)}) %all-gather.5.cloned.1.call-update) | async-done | bytes 16777232 | tf_op jit(solution)/shard_map/all_gather | solution.py:89
  202.5 11.7 %fusion.45 = bf16[32,8,8,128]{3,1,2,0:T(8,128)(2,1)S(1)} fusion(bf16[8192,1024]{1,0:T(8,128)(2,1)} %all-gather.5.cloned.1.call-done, f32[8192]{0:T(1024)S(1)} %copy-done.7, bf16[256,8192]{1,0:T(8,128)(2,1)} %param.12, f32[256]{0:T(256)S(1)} %add_rsqrt_fusion), kind=kOutput, calls=%fused_computation.56 | convolution fusion | flops 4303618048 | bytes 21529600 | tf_op jit(solution)/shard_map/dot_general | solution.py:90
  217.3 16.3 %fusion.42 = bf16[4,64,8,128]{3,1,2,0:T(8,128)(2,1)} fusion(bf16[4,256,8,128]{3,2,1,0:T(8,128)(2,1)} %bitcast.118, f32[4,8,256,64]{2,3,1,0:T(8,128)} %fusion.17, f32[4,8,64,256]{3,2,1,0:T(8,128)} %get-tuple-element.12, f32[4,8,64]{2,1,0:T(8,128)S(1)} %broadcast_add_fusion), kind=kOutput, calls=%fused_computation.55 | convolution fusion | flops 138152192 | bytes 6823936 | tf_op jit(solution)/shard_map/chqk,ckhd->cqhd/dot_general | solution.py:125
  235.9 12.5 %convolution_convert_fusion = bf16[2,4096,1024]{2,1,0:T(8,128)(2,1)} fusion(bf16[2,4096,256]{2,1,0:T(8,128)(2,1)} %bitcast.115, bf16[256,1024,1]{1,0,2:T(8,128)(2,1)} %reshape.184), kind=kOutput, calls=%fused_computation.3 | convolution fusion | flops 4303355904 | bytes 21495808 | tf_op jit(solution)/shard_map/dot_general | solution.py:145
  248.5 9.5 %convolution_convert_fusion.1 = bf16[256,8192]{1,0:T(8,128)(2,1)} fusion(bf16[8192,1024]{1,0:T(8,128)(2,1)} %all-gather.5.cloned.1.call-done, bf16[32,8,8,128]{3,2,1,0:T(8,128)(2,1)S(1)} %bitcast.127), kind=kOutput, calls=%fused_computation.6 | convolution fusion | flops 4297064448 | bytes 21495808 | tf_op jit(solution)/shard_map/dot_general | solution.py:155
  263.9 18.1 %convert_bitcast_fusion.1 = bf16[4,256,8,128]{1,3,2,0:T(8,128)(2,1)} fusion(f32[4,8,256,64]{2,3,1,0:T(8,128)} %fusion.17, bf16[4,64,8,128]{3,2,1,0:T(8,128)(2,1)S(1)} %bitcast.124, f32[4,8,64,256]{3,2,1,0:T(8,128)} %get-tuple-element.12, f32[4,8,64]{2,1,0:T(8,128)S(1)} %broadcast_add_fusion), kind=kOutput, calls=%fused_computation.23 | convolution fusion | flops 138938624 | bytes 6823936 | tf_op jit(solution)/shard_map/chqk,cqhd->ckhd/dot_general | solution.py:129
  282.0 4.3 copy.58
  286.3 5.9 %fusion.4 = f32[1024,896]{1,0:T(8,128)} fusion(bf16[896,1024]{1,0:T(8,128)(2,1)S(1)} %copy-done, bf16[128,8,8,128]{3,2,1,0:T(8,128)(2,1)} %bitcast.126), kind=kOutput, calls=%fused_computation.11 | convolution fusion | flops 1879048192 | bytes 7602176 | tf_op jit(solution)/shard_map/dot_general | solution.py:135
  292.1 103.7 %reduce-scatter.10.cloned.1.call-done = bf16[2,256,1024]{2,1,0:T(8,128)(2,1)} async-done(((bf16[2,4096,1024]{2,1,0:T(8,128)(2,1)}), bf16[2,256,1024]{2,1,0:T(8,128)(2,1)}) %reduce-scatter.10.cloned.1.call-update) | async-done | bytes 1048592 | tf_op jit(solution)/shard_map/reduce_scatter | solution.py:149
  395.9 5.6 %add_convert_fusion = bf16[1024,896]{1,0:T(8,128)(2,1)S(1)} fusion(f32[1024,896]{1,0:T(8,128)} %fusion.4, bf16[896,1024]{1,0:T(8,128)(2,1)} %param.20, bf16[128,8,8,128]{3,2,1,0:T(8,128)(2,1)} %bitcast.125), kind=kOutput, calls=%fused_computation.9 | convolution fusion | flops 1880883200 | bytes 9437184 | tf_op jit(solution)/shard_map/dot_general | solution.py:132
  401.9 40.0 %collective-permute-done.2 = bf16[4,2,128,896]{3,2,1,0:T(8,128)(2,1)} collective-permute-done((bf16[4,2,128,896]{3,2,1,0:T(8,128)(2,1)S(1)}, bf16[4,2,128,896]{3,2,1,0:T(8,128)(2,1)}, u32[]{:S(2)}, u32[]{:S(2)}) %collective-permute-start.2) | collective-permute-done | bytes 1835040 | tf_op jit(solution)/shard_map/ppermute | solution.py:23
  442.0 2.9 fusion.39
  448.5 8.2 %psum.7 = f32[256,1]{0,1:T(1,128)S(1)} all-reduce(f32[256,1]{0,1:T(1,128)S(1)} %bitcast.137), channel_id=1, replica_groups=mesh['section'=2,'seq'=16,'tensor'=4] {'tensor'}, use_global_device_ids=true, to_apply=%region_10.11 | all-reduce | flops 256 | bytes 2048 | tf_op jit(solution)/shard_map/psum | solution.py:162
  457.3 3.1 multiply_convert_fusion.1
  460.4 7.7 %reduce-scatter.12.cloned.1.call-done = bf16[1,256,1024]{2,1,0:T(8,128)(2,1)} async-done(((bf16[2,256,1024]{2,1,0:T(8,128)(2,1)}), bf16[1,256,1024]{2,1,0:T(8,128)(2,1)}) %reduce-scatter.12.cloned.1.call-update) | async-done | bytes 524304 | tf_op jit(solution)/shard_map/reduce_scatter | solution.py:152
  470.2 29.5 %reduce-scatter.14.cloned.1.call-done = bf16[1,2,128,896]{3,2,1,0:T(8,128)(2,1)} async-done(((bf16[4,2,128,896]{3,2,1,0:T(8,128)(2,1)}), bf16[1,2,128,896]{3,2,1,0:T(8,128)(2,1)}) %reduce-scatter.14.cloned.1.call-update) | async-done | bytes 458768 | tf_op jit(solution)/shard_map/reduce_scatter | solution.py:140
  (78 shorter events, 41.3 us)
Async XLA Ops:
  7.2 96.0 %copy-start = (bf16[896,1024]{1,0:T(8,128)(2,1)S(1)}, bf16[896,1024]{1,0:T(8,128)(2,1)}, u32[]{:S(2)}) copy-start(bf16[896,1024]{1,0:T(8,128)(2,1)} %param.21) | copy-start | bytes 5505028
  7.2 43.2 %reduce-scatter.6.cloned.1.call-start = ((), (), s32[]{:S(2)}) async-start(), calls=%async_computation.5 | async-start | bytes 1146880 | tf_op jit(solution)/shard_map/reduce_scatter | solution.py:82
  7.2 3.3 copy-start.7
  18.7 6.8 %copy-start.4 = (bf16[1,1,2,128,896]{4,3,2,1,0:T(8,128)(2,1)S(1)}, bf16[1,1,2,128,896]{4,3,2,1,0:T(8,128)(2,1)}, u32[]{:S(2)}) copy-start(bf16[1,1,2,128,896]{4,3,2,1,0:T(8,128)(2,1)} %param.16) | copy-start | bytes 1376260
  18.7 7.0 %copy-start.8 = (f32[896]{0:T(1024)S(1)}, f32[896]{0:T(1024)}, u32[]{:S(2)}) copy-start(f32[896]{0:T(1024)} %param.17) | copy-start | bytes 10756
  25.5 77.6 %all-gather.3.cloned.1.call-start = ((), (), s32[]{:S(2)}) async-start(), calls=%async_computation.6 | async-start | bytes 2293760 | tf_op jit(solution)/shard_map/all_gather | solution.py:88
  50.4 5.1 %collective-permute-start = (bf16[64,1792]{1,0:T(8,128)(2,1)}, bf16[64,1792]{1,0:T(8,128)(2,1)S(1)}, u32[]{:S(2)}, u32[]{:S(2)}) collective-permute-start(bf16[64,1792]{1,0:T(8,128)(2,1)} %reduce-scatter.6.cloned.1.call-done), channel_id=1, source_target_pairs={{0,64},{64,0},{1,65},{65,1},{2,66},{66,2},{3,67},{67,3},{4,68},{68... | collective-permute-start | bytes 688136 | tf_op jit(solution)/shard_map/ppermute | solution.py:23
  59.4 12.6 %copy-start.5 = (bf16[256,1024]{1,0:T(8,128)(2,1)S(1)}, bf16[256,1024]{1,0:T(8,128)(2,1)}, u32[]{:S(2)}) copy-start(bf16[256,1024]{1,0:T(8,128)(2,1)} %param.23) | copy-start | bytes 1572868
  61.6 8.8 %collective-permute-start.1 = (bf16[1,2,128,896]{3,2,1,0:T(8,128)(2,1)S(1)}, bf16[1,2,128,896]{3,2,1,0:T(8,128)(2,1)S(1)}, u32[]{:S(2)}, u32[]{:S(2)}) collective-permute-start(bf16[1,2,128,896]{3,2,1,0:T(8,128)(2,1)S(1)} %bitcast.133), channel_id=1, source_target_pairs={{0,64},{64,0},{1,65},{65,1},{2,66},{66,2},{3,67},{67,3},{4,68},{68... | collective-permute-start | bytes 1376264 | tf_op jit(solution)/shard_map/ppermute | solution.py:23
  70.4 0.8 copy-start.6
  71.2 131.3 %all-gather.5.cloned.1.call-start = ((), (), s32[]{:S(2)}) async-start(), calls=%async_computation.7 | async-start | bytes 17301504 | tf_op jit(solution)/shard_map/all_gather | solution.py:89
  71.9 323.9 %reduce-scatter.10.cloned.1.call-start = ((), (), s32[]{:S(2)}) async-start(), calls=%async_computation.9 | async-start | bytes 17825792 | tf_op jit(solution)/shard_map/reduce_scatter | solution.py:149
  72.1 6.6 %copy-start.9 = (s32[4]{0:T(128)S(1)}, s32[4]{0:T(128)}, u32[]{:S(2)}) copy-start(s32[4]{0:T(128)} %param.22) | copy-start | bytes 52
  107.0 1.5 copy-start.10
  107.0 2.0 copy-start.11
  109.0 4.3 copy-start.1
  202.5 11.8 %copy-start.2 = (bf16[128,8,8,128]{3,2,1,0:T(8,128)(2,1)S(1)}, bf16[128,8,8,128]{3,2,1,0:T(8,128)(2,1)}, u32[]{:S(2)}) copy-start(bf16[128,8,8,128]{3,2,1,0:T(8,128)(2,1)} %copy.64) | copy-start | bytes 6291460
  248.5 197.6 %reduce-scatter.8.cloned.1.call-start = ((), (), s32[]{:S(2)}) async-start(), calls=%async_computation.8 | async-start | bytes 5242880 | tf_op jit(solution)/shard_map/reduce_scatter | solution.py:156
  258.1 210.0 %reduce-scatter.12.cloned.1.call-start = ((), (), s32[]{:S(2)}) async-start(), calls=%async_computation.10 | async-start | bytes 1572864 | tf_op jit(solution)/shard_map/reduce_scatter | solution.py:152
  395.8 103.9 %reduce-scatter.14.cloned.1.call-start = ((), (), s32[]{:S(2)}) async-start(), calls=%async_computation.11 | async-start | bytes 2293760 | tf_op jit(solution)/shard_map/reduce_scatter | solution.py:140
  401.5 40.5 %collective-permute-start.2 = (bf16[4,2,128,896]{3,2,1,0:T(8,128)(2,1)S(1)}, bf16[4,2,128,896]{3,2,1,0:T(8,128)(2,1)}, u32[]{:S(2)}, u32[]{:S(2)}) collective-permute-start(bf16[4,2,128,896]{3,2,1,0:T(8,128)(2,1)S(1)} %bitcast.142), channel_id=1, source_target_pairs={{0,64},{64,0},{1,65},{65,1},{2,66},{66,2},{3,67},{67,3},{4,68},{68... | collective-permute-start | bytes 5505032 | tf_op jit(solution)/shard_map/ppermute | solution.py:23
  446.1 11.2 %copy-start.3 = (bf16[256,2048]{1,0:T(8,128)(2,1)S(1)}, bf16[256,2048]{1,0:T(8,128)(2,1)}, u32[]{:S(2)}) copy-start(bf16[256,2048]{1,0:T(8,128)(2,1)} %reduce-scatter.8.cloned.1.call-done) | copy-start | bytes 3145732
Sparse Core Ops, SparseCore 0:
  25.6 24.7 reduce-scatter.5
  71.3 31.7 all-gather.2
  104.8 97.5 all-gather.4
  248.6 147.1 reduce-scatter.9
  398.2 44.9 reduce-scatter.7
  445.4 22.6 reduce-scatter.11
  471.2 28.5 reduce-scatter.13
where the time goes:
time: 514 us; the launch traced here: 507 us
  waiting for transfers between devices  327 us (64%)
  matrix products  109 us (21%)
  local copies, waits for them, and re-layouts  22.8 us (4%)
  other arithmetic  22.2 us (4%)
  between operations  14.9 us (3%)
  blocking collectives  8.24 us (2%)
    reduce_scatter x1, waiting for transfers between devices, shards(): lax.psum_scatter(sectioned.astype(jnp.bfloat16), 'seq', scatter_dimension...  104 us
    all_gather x1, waiting for transfers between devices, shards(): w_full = lax.all_gather(w_query, ('section', 'seq'), axis=0, tiled=True)  87 us
    ppermute x3, waiting for transfers between devices, swapped(): return lax.ppermute(value, axis, pairs)  48.9 us
    reduce_scatter x1, waiting for transfers between devices, shards(): lax.psum_scatter(crossed.astype(jnp.float32).astype(jnp.bfloat16), 'tenso...  29.5 us
    reduce_scatter x1, waiting for transfers between devices, shards(): lax.psum_scatter(state_part.astype(jnp.bfloat16), 'tensor', scatter_dimen...  24.5 us
    all_gather x1, waiting for transfers between devices, shards(): encoded_all = lax.all_gather(encoded_home, 'tensor', axis=0, tiled=True)  24.4 us
    dot_general x1, matrix products, shards(): jnp.einsum('chqk,cqhd->ckhd', d_scores, query_heads, preferred_element_ty...  18.1 us
    dot_general x1, matrix products, shards(): jnp.einsum('chqk,ckhd->cqhd', d_scores, key_heads, preferred_element_type...  16.3 us
  transfers between devices with their start and end apart: 10, of which 9 were waited for; matrix products, arithmetic and copies ran while one was open for 16% of the time, Pallas kernels for 0%

commit v1 on v0

v1 whole, which is shorter than its diff:
```python
import functools
import math

import jax
import jax.numpy as jnp
from jax import lax
from jax.experimental import pallas as pl
from jax.experimental.pallas import tpu as pltpu
from jax.sharding import PartitionSpec as P

HD = 128
E = 896
EHD = 64
BLOCK = 64
NBR = 2
RLEN = 128
KEYS = NBR * RLEN

EPSILON = 1e-05
NEG_LARGE = -1e30
MESH = pl.DeviceIdType.MESH
F32 = jnp.float32
BF16 = jnp.bfloat16
LAST = (((1,), (1,)), ((), ()))
FIRST = (((0,), (0,)), ((), ()))


def dot(a, b, dims=(((1,), (0,)), ((), ()))):
    return lax.dot_general(a, b, dims, preferred_element_type=F32)


def swapped(value, axis, distance):
    mask = 2**distance
    pairs = [(source, source ^ mask) for source in range(lax.axis_size(axis))]
    return lax.ppermute(value, axis, pairs)


def encode(enc_in, block_states, enc_gain, enc_query, enc_out):
    block_count = enc_in.shape[0]
    heads_enc = E // EHD
    enc_rows = enc_in.astype(jnp.float32).reshape(-1, E)
    enc_scale = lax.rsqrt(jnp.mean(enc_rows * enc_rows, axis=-1, keepdims=True) + EPSILON)
    enc_normed = (enc_rows * enc_scale * enc_gain).astype(jnp.bfloat16)
    enc_queries = jnp.dot(enc_normed, enc_query, preferred_element_type=jnp.float32).astype(
        jnp.bfloat16
    )
    query_heads = enc_queries.reshape(block_count, NBR * RLEN, heads_enc, EHD)
    state_rows = block_states.reshape(block_count, BLOCK, 2 * E)
    key_heads = state_rows[:, :, :E].reshape(block_count, BLOCK, heads_enc, EHD)
    value_heads = state_rows[:, :, E:].reshape(block_count, BLOCK, heads_enc, EHD)
    scores = jnp.einsum(
        "cqhd,ckhd->chqk", query_heads, key_heads, preferred_element_type=jnp.float32
    ) / math.sqrt(EHD)
    row_top = jnp.max(scores, axis=-1, keepdims=True)
    weights = jnp.exp(scores - row_top)
    enc_weights = (weights / jnp.sum(weights, axis=-1, keepdims=True)).astype(jnp.bfloat16)
    enc_context = (
        jnp.einsum("chqk,ckhd->cqhd", enc_weights, value_heads, preferred_element_type=jnp.float32)
        .astype(jnp.bfloat16)
        .reshape(-1, E)
    )
    mixed = enc_rows + jnp.dot(enc_context, enc_out, preferred_element_type=jnp.float32)
    return mixed.astype(jnp.bfloat16).reshape(block_count, NBR, RLEN, E)


def attend_kernel(
    counts, q_ref, enc_ref, wk_ref, wv_ref, do_ref,
    ctx_ref, dq_ref, grad_ref, sums_ref,
    k_s, v_s, dk_s, dv_s,
):
    count = counts[pl.program_id(0)]
    enc = enc_ref[...]
    k_s[...] = dot(enc, wk_ref[...]).astype(BF16)
    v_s[...] = dot(enc, wv_ref[...]).astype(BF16)
    valid = lax.broadcasted_iota(jnp.int32, (BLOCK, KEYS), 1) < count * RLEN
    empty = jnp.where(count == 0, 1.0, 0.0).astype(F32)
    scale = 1.0 / math.sqrt(HD)
    total = jnp.zeros((BLOCK, HD), F32)
    for head in range(q_ref.shape[1] // HD):
        cols = slice(head * HD, (head + 1) * HD)
        q, k, v, do = q_ref[:, cols], k_s[:, cols], v_s[:, cols], do_ref[:, cols]
        scores = dot(q, k, LAST) * scale
        top = jnp.max(jnp.where(valid, scores, NEG_LARGE), axis=-1, keepdims=True)
        weights = jnp.where(valid, jnp.exp(scores - top), 0.0)
        probs = weights / (jnp.sum(weights, axis=-1, keepdims=True) + empty)
        rounded = probs.astype(BF16)
        ctx_ref[:, cols] = dot(rounded, v).astype(BF16)
        dv_s[:, cols] = dot(rounded, do, FIRST).astype(BF16)
        d_probs = dot(do, v, LAST)
        inner = jnp.sum(probs * d_probs, axis=-1, keepdims=True)
        d_scores = (probs * (d_probs - inner) * scale).astype(BF16)
        dq = dot(d_scores, k)
        dq_ref[:, cols] = dq.astype(BF16)
        total = total + dq * q.astype(F32)
        dk_s[:, cols] = dot(d_scores, q, FIRST).astype(BF16)
    grad = dot(dk_s[...], wk_ref[...], LAST) + dot(dv_s[...], wv_ref[...], LAST)
    grad_ref[0] = grad.astype(BF16)
    sums_ref[...] = jnp.broadcast_to(jnp.sum(total, axis=-1, keepdims=True), (BLOCK, HD))


def attend(counts, queries, encoded, w_key, w_value, d_context):
    blocks = counts.shape[0]
    rows, width = queries.shape
    row_block = pl.BlockSpec((BLOCK, width), lambda b: (b, 0))
    weight = pl.BlockSpec((E, width), lambda b: (0, 0))
    flops = 2 * (4 * rows * 4 * E * width + 6 * rows * KEYS * width)
    return pl.pallas_call(
        attend_kernel,
        grid=(blocks,),
        in_specs=[
            pl.BlockSpec(memory_space=pltpu.SMEM),
            row_block,
            pl.BlockSpec((KEYS, E), lambda b: (b, 0)),
            weight,
            weight,
            row_block,
        ],
        out_specs=[
            row_block,
            row_block,
            pl.BlockSpec((1, KEYS, E), lambda b: (b, 0, 0)),
            pl.BlockSpec((BLOCK, HD), lambda b: (b, 0)),
        ],
        out_shape=[
            jax.ShapeDtypeStruct((rows, width), BF16),
            jax.ShapeDtypeStruct((rows, width), BF16),
            jax.ShapeDtypeStruct((blocks, KEYS, E), BF16),
            jax.ShapeDtypeStruct((rows, HD), F32),
        ],
        scratch_shapes=[pltpu.VMEM((KEYS, width), BF16)] * 4,
        compiler_params=pltpu.CompilerParams(vmem_limit_bytes=50 * 2**20),
        cost_estimate=pl.CostEstimate(
            flops=flops, bytes_accessed=14 * 2**20, transcendentals=rows * 8 * KEYS
        ),
    )(counts, queries, encoded, w_key, w_value, d_context)


class Place:
    def __init__(self):
        self.section = lax.axis_index("section")
        seq = lax.axis_index("seq")
        self.x = lax.axis_index("tensor")
        self.core = seq % 2
        self.y = seq // 4
        self.z = 2 * ((seq // 2) % 2) + self.section

    def along(self, dim, off):
        if dim == "x":
            return (self.section, self.seq_of(self.y, self.z), (self.x + off) % 4)
        if dim == "y":
            return (self.section, self.seq_of((self.y + off) % 4, self.z), self.x)
        z = (self.z + off) % 4
        return (z % 2, self.seq_of(self.y, z), self.x)

    def seq_of(self, y, z):
        return y * 4 + (z // 2) * 2 + self.core

    def sibling(self):
        return (self.section, self.y * 4 + (self.z // 2) * 2 + 1 - self.core, self.x)

    def partner(self):
        return (1 - self.section, self.seq_of(self.y, self.z), self.x)

    def chunk(self, dy, dz):
        y, z = (self.y + dy) % 4, (self.z + dz) % 4
        return (z % 2) * 8 + y * 2 + z // 2


def greet(devices):
    barrier = pltpu.get_barrier_semaphore()
    for device in devices:
        pl.semaphore_signal(barrier, inc=1, device_id=device, device_id_type=MESH)
    pl.semaphore_wait(barrier, len(devices))


LINES = (2, 1, 3, 0)


def backward_kernel(
    dq_ref, mine_ref, sib_ref, w_ref, grad_ref, sums_ref, tokens_ref, inverse_ref, gain_ref,
    dw_ref, dh_ref, de_ref, dots_ref,
    dq2, dq_t, nrm, wc, prod, ra1, ra2, rb1, rb2, part, rn1, rn2, out_sib, in_sib,
    g1, gs, g2, gfin, gin, sums_in, tok, dh_s, column,
    load_sem, dh_sem, send_sem, recv_sem,
):
    at = Place()
    width = tokens_ref.shape[1]
    share = width // 4
    loads = [
        pltpu.make_async_copy(mine_ref, nrm.at[:, 0:256], load_sem.at[0]),
        pltpu.make_async_copy(sib_ref, nrm.at[:, 256:512], load_sem.at[1]),
        pltpu.make_async_copy(w_ref.at[:, at.core], wc, load_sem.at[2]),
    ]
    for i in range(8):
        first = pl.multiple_of(at.x * share + i * 256, 256)
        loads.append(
            pltpu.make_async_copy(tokens_ref.at[:, pl.ds(first, 256)], tok.at[i], load_sem.at[3 + i])
        )
    for load in loads:
        load.start()
    greet(
        [at.along("x", 1), at.along("x", 2), at.along("x", 3), at.along("y", 1), at.along("y", 3),
         at.along("z", 1), at.along("z", 3), at.sibling()]
    )

    copies = []

    def send(src, dst, device):
        index = len(copies)
        copy = pltpu.make_async_remote_copy(
            src_ref=src, dst_ref=dst, send_sem=send_sem.at[index], recv_sem=recv_sem.at[index],
            device_id=device, device_id_type=MESH,
        )
        copy.start()
        copies.append(copy)
        return copy

    def added(dst, first, second):
        dst[...] = (first[...].astype(F32) + second[...].astype(F32)).astype(BF16)

    c_dq = send(dq_ref, dq2.at[256:512], at.sibling())
    far = (at.x + 2) % 4
    up, down = (at.x + 1) % 4, (at.x + 3) % 4
    c_g1 = [
        send(grad_ref.at[far, 0:128], g1.at[0], at.along("x", 1)),
        send(grad_ref.at[far, 128:256], g1.at[1], at.along("x", 3)),
    ]
    c_sums = [send(sums_ref, sums_in.at[i], at.along("x", i + 1)) for i in range(3)]
    dq2[0:256] = dq_ref[...]
    for j in range(4):
        dq_t[256 * j : 256 * j + 256, 0:256] = jnp.transpose(dq_ref[:, 256 * j : 256 * j + 256])
    c_dq.wait_recv()
    for j in range(4):
        dq_t[256 * j : 256 * j + 256, 256:512] = jnp.transpose(
            dq2[256:512, 256 * j : 256 * j + 256]
        )
    loads[0].wait()
    loads[1].wait()

    def product(dy, dz):
        k = at.chunk(dy, dz)

        @pl.loop(0, 4)
        def _(i):
            rows = pl.ds(pl.multiple_of(i * 256, 256), 256)
            prod[k, rows, :] = dot(dq_t[rows, :], nrm[k]).astype(BF16)

    dims = (("z", "y"), ("y", "z"))

    def block(half, line, off, low=0, high=512):
        dy, dz = (line, off) if half == 0 else (off, line)
        return prod.at[at.chunk(dy, dz), half * 512 + low : half * 512 + high]

    c1 = {}

    def first_hop(half, line):
        dim = dims[half][0]
        slot = LINES.index(line)
        c1[half, line] = (
            send(block(half, line, 2, 0, 256), ra1.at[half, slot, 0], at.along(dim, 1)),
            send(block(half, line, 2, 256, 512), ra1.at[half, slot, 1], at.along(dim, 3)),
        )

    product(2, 2)
    first_hop(0, 2)
    first_hop(1, 2)
    for line in (1, 3, 0):
        product(line, 2)
        first_hop(0, line)
        product(2, line)
        first_hop(1, line)
    for dy in (1, 3, 0):
        for dz in (1, 3, 0):
            product(dy, dz)

    c_g1[0].wait_recv()
    c_g1[1].wait_recv()
    gs[0, 0:128] = (grad_ref[up, 0:128].astype(F32) + g1[0].astype(F32)).astype(BF16)
    gs[0, 128:256] = grad_ref[up, 128:256]
    gs[1, 0:128] = grad_ref[down, 0:128]
    gs[1, 128:256] = (grad_ref[down, 128:256].astype(F32) + g1[1].astype(F32)).astype(BF16)
    c_g2 = [
        send(gs.at[0], g2.at[0], at.along("x", 1)),
        send(gs.at[1], g2.at[1], at.along("x", 3)),
    ]

    c2 = {}

    def second_hop(half, line):
        dim = dims[half][0]
        slot = LINES.index(line)
        for way, off in ((0, 1), (1, 3)):
            c1[half, line][way].wait_recv()
            piece = block(half, line, off, 256 * way, 256 * way + 256)
            added(piece, piece, ra1.at[half, slot, way])
        c2[half, line] = (
            send(block(half, line, 1), ra2.at[half, slot, 0], at.along(dim, 1)),
            send(block(half, line, 3), ra2.at[half, slot, 1], at.along(dim, 3)),
        )

    def partial(k):
        @pl.loop(0, 2)
        def _(i):
            rows = pl.ds(pl.multiple_of(i * 256, 256), 256)
            part[k, rows, :] = dot(dq2[rows, :], wc[k], LAST).astype(BF16)

    n1, n2 = [], []
    loads[2].wait()
    second_hop(0, 2)
    second_hop(1, 2)
    for m in range(4):
        partial(far * 4 + m)
        n1.append(
            (
                send(part.at[far * 4 + m, 0:256], rn1.at[m, 0], at.along("x", 1)),
                send(part.at[far * 4 + m, 256:512], rn1.at[m, 1], at.along("x", 3)),
            )
        )
        if m > 0:
            second_hop(0, LINES[m])
            second_hop(1, LINES[m])

    for copy in c_sums:
        copy.wait_recv()
    sums = sums_ref[...] + sums_in[0] + sums_in[1] + sums_in[2]
    dots_ref[...] = sums * (1.0 / math.sqrt(width))
    column[...] = jnp.transpose(jnp.broadcast_to(sums[0:1], (128, 256)))

    for m in range(4):
        partial(up * 4 + m)
        partial(down * 4 + m)
        partial(at.x * 4 + m)
    for m in range(4):
        n1[m][0].wait_recv()
        piece = part.at[up * 4 + m, 0:256]
        added(piece, piece, rn1.at[m, 0])
        n1[m][1].wait_recv()
        piece = part.at[down * 4 + m, 256:512]
        added(piece, piece, rn1.at[m, 1])
        n2.append(
            (
                send(part.at[up * 4 + m], rn2.at[m, 0], at.along("x", 1)),
                send(part.at[down * 4 + m], rn2.at[m, 1], at.along("x", 3)),
            )
        )

    for copy in c_g2:
        copy.wait_recv()
    gfin[...] = (grad_ref[at.x].astype(F32) + g2[0].astype(F32) + g2[1].astype(F32)).astype(BF16)
    c_swap = send(gfin, gin, at.partner())

    def gathered(half, line):
        for way in (0, 1):
            c2[half, line][way].wait_recv()
        slot = LINES.index(line)
        piece = block(half, line, 0)
        total = piece[...].astype(F32) + ra2[half, slot, 0].astype(F32)
        piece[...] = (total + ra2[half, slot, 1].astype(F32)).astype(BF16)

    for load in loads[3:]:
        load.wait()
    stores = []

    def finish(i, d_normed):
        unit = tok[i].astype(F32) * inverse_ref[...]
        rows = jnp.concatenate([column[...], column[...]], axis=1)
        grads = d_normed * gain_ref[at.x * 8 + i]
        result = inverse_ref[...] * (grads - unit * (rows * (1.0 / width)))
        dh_s[i] = result.astype(BF16)
        first = pl.multiple_of(i * 256, 256)
        store = pltpu.make_async_copy(
            dh_s.at[i], dh_ref.at[:, pl.ds(first, 256)], dh_sem.at[len(stores)]
        )
        store.start()
        stores.append(store)

    c_sib = []

    def normed_sum(m):
        for copy in n2[m]:
            copy.wait_recv()

        def summed(low):
            rows = slice(low, low + 256)
            total = part[at.x * 4 + m, rows].astype(F32) + rn2[m, 0, rows].astype(F32)
            return total + rn2[m, 1, rows].astype(F32)

        out_sib[m] = summed(256).astype(BF16)
        c_sib.append(send(out_sib.at[m], in_sib.at[m], at.sibling()))
        finish(2 * m + at.core, summed(0))

    d1, d2 = {}, {}

    def turn(half):
        dim = dims[half][1]
        d1[half] = (
            send(block(half, 2, 0, 0, 256), rb1.at[half, 0], at.along(dim, 1)),
            send(block(half, 2, 0, 256, 512), rb1.at[half, 1], at.along(dim, 3)),
        )

    def turned(half):
        dim = dims[half][1]
        for way, off in ((0, 1), (1, 3)):
            d1[half][way].wait_recv()
            piece = block(half, off, 0, 256 * way, 256 * way + 256)
            added(piece, piece, rb1.at[half, way])
        d2[half] = (
            send(block(half, 1, 0), rb2.at[half, 0], at.along(dim, 1)),
            send(block(half, 3, 0), rb2.at[half, 1], at.along(dim, 3)),
        )

    def result(half):
        for way in (0, 1):
            c2[half, 0][way].wait_recv()
            d2[half][way].wait_recv()
        for low in (0, 256):
            rows = slice(low, low + 256)
            total = block(half, 0, 0)[rows].astype(F32)
            for extra in (ra2.at[half, 3, 0], ra2.at[half, 3, 1], rb2.at[half, 0], rb2.at[half, 1]):
                total = total + extra[rows].astype(F32)
            first = half * 512 + low
            dw_ref[:, first : first + 256] = jnp.transpose(total)

    for half in (0, 1):
        gathered(half, 2)
        turn(half)
    normed_sum(0)
    for half in (0, 1):
        gathered(half, 1)
    normed_sum(1)
    for half in (0, 1):
        gathered(half, 3)
    for half in (0, 1):
        turned(half)
    normed_sum(2)
    for half in (0, 1):
        result(half)
    normed_sum(3)
    for m in range(4):
        c_sib[m].wait_recv()
        finish(2 * m + 1 - at.core, in_sib[m].astype(F32))
    c_swap.wait_recv()
    de_ref[...] = gin[...]
    for copy in copies:
        copy.wait_send()
    for store in stores:
        store.wait()


SENDS = 1 + 2 + 3 + 16 + 2 + 16 + 8 + 8 + 1 + 4 + 8


def backward(d_queries, mine, theirs, w_all, grad, sums, tokens, inverse, gain):
    rows, width = d_queries.shape
    full = tokens.shape[1]
    vmem = pl.BlockSpec(memory_space=pltpu.VMEM)
    anywhere = pl.BlockSpec(memory_space=pl.ANY)

    def buffer(*shape, kind=BF16):
        return pltpu.VMEM(shape, kind)

    return pl.pallas_call(
        backward_kernel,
        in_specs=[vmem, anywhere, anywhere, anywhere, vmem, vmem, anywhere, vmem, vmem],
        out_specs=[vmem, anywhere, vmem, vmem],
        out_shape=[
            jax.ShapeDtypeStruct((256, width), F32),
            jax.ShapeDtypeStruct((rows, full // 4), BF16),
            jax.ShapeDtypeStruct((KEYS, E), BF16),
            jax.ShapeDtypeStruct((8, rows), F32),
        ],
        scratch_shapes=[
            buffer(512, 1024),
            buffer(1024, 512),
            buffer(16, 512, 256),
            buffer(16, 256, 1024),
            buffer(16, 1024, 256),
            buffer(2, 4, 2, 256, 256),
            buffer(2, 4, 2, 512, 256),
            buffer(2, 2, 256, 256),
            buffer(2, 2, 512, 256),
            buffer(16, 512, 256),
            buffer(4, 2, 256, 256),
            buffer(4, 2, 512, 256),
            buffer(4, 256, 256),
            buffer(4, 256, 256),
            buffer(2, 128, E),
            buffer(2, 256, E),
            buffer(2, 256, E),
            buffer(256, E),
            buffer(256, E),
            buffer(3, 8, 256, kind=F32),
            buffer(8, 256, 256),
            buffer(8, 256, 256),
            buffer(256, 128, kind=F32),
            pltpu.SemaphoreType.DMA((11,)),
            pltpu.SemaphoreType.DMA((8,)),
            pltpu.SemaphoreType.DMA((SENDS,)),
            pltpu.SemaphoreType.DMA((SENDS,)),
        ],
        compiler_params=pltpu.CompilerParams(
            collective_id=1, has_side_effects=True, vmem_limit_bytes=60 * 2**20
        ),
        cost_estimate=pl.CostEstimate(
            flops=4 * 512 * 1024 * 4096, bytes_accessed=20 * 2**20, transcendentals=0
        ),
    )(d_queries, mine, theirs, w_all, grad, sums, tokens, inverse, gain)


def shards(
    tokens,
    w_query,
    query_gain,
    state_kv,
    neighbours,
    enc_gain,
    enc_query,
    enc_out,
    w_key,
    w_value,
    counts,
    d_context,
):
    tensor_count = lax.axis_size("tensor")
    tensor_rank = lax.axis_index("tensor")
    core = lax.axis_index("seq") % 2
    tok_rows, width = tokens.shape
    width_share = width // tensor_count
    enc_in = swapped(neighbours[0], "section", 0)
    hidden = tokens.astype(jnp.float32)
    inverse = lax.rsqrt(jnp.mean(hidden * hidden, axis=-1, keepdims=True) + EPSILON)
    unit_full = hidden * inverse
    unit_rows = unit_full.astype(jnp.bfloat16)
    normed = (unit_full * query_gain).astype(jnp.bfloat16)
    unit_share = lax.dynamic_slice_in_dim(unit_rows, tensor_rank * width_share, width_share, 1)
    state_part = jnp.dot(unit_share, state_kv, preferred_element_type=jnp.float32)
    block_states = lax.psum_scatter(
        state_part.astype(jnp.bfloat16), "tensor", scatter_dimension=0, tiled=True
    )
    encoded_home = encode(enc_in, block_states, enc_gain, enc_query, enc_out)
    encoded_all = lax.all_gather(encoded_home, "tensor", axis=0, tiled=True)
    w_full = lax.all_gather(w_query, ("section", "seq"), axis=0, tiled=True)
    queries = jnp.dot(normed, w_full, preferred_element_type=jnp.float32).astype(jnp.bfloat16)
    context, d_queries, grad, sums = attend(
        counts, queries, encoded_all.reshape(-1, E), w_key, w_value, d_context
    )
    chunks = jnp.transpose(normed.reshape(tok_rows, 16, 2, 256), (2, 1, 0, 3))
    mine = lax.dynamic_index_in_dim(chunks, core, 0, keepdims=False)
    theirs = swapped(lax.dynamic_index_in_dim(chunks, 1 - core, 0, keepdims=False), "seq", 0)
    d_query_weight, d_hidden, d_encoded, row_dots = backward(
        d_queries,
        mine,
        theirs,
        w_full.reshape(16, 2, 256, -1),
        grad,
        jnp.broadcast_to(sums[:, 0][None], (8, tok_rows)),
        tokens,
        inverse,
        query_gain.reshape(32, 1, 256),
    )
    return (
        context,
        d_hidden,
        d_query_weight,
        d_encoded.reshape(1, 1, NBR, RLEN, E),
        row_dots[0],
    )


def solution(mesh):
    return jax.shard_map(
        shards,
        mesh=mesh,
        in_specs=(
            P(("section", "seq"), None),
            P(("section", "seq"), "tensor"),
            P(),
            P("tensor", None),
            P("section", ("seq", "tensor"), None, None, None),
            P(),
            P(),
            P(),
            P(None, "tensor"),
            P(None, "tensor"),
            P(("section", "seq")),
            P(("section", "seq"), "tensor"),
        ),
        out_specs=(
            P(("section", "seq"), "tensor"),
            P(("section", "seq"), "tensor"),
            P(("section", "seq"), "tensor"),
            P("section", ("seq", "tensor"), None, None, None),
            P(("section", "seq")),
        ),
        check_vma=False,
    )
```

time: 514 us -> 286 us (0.56); the launches traced: 507 us -> 285 us
  waiting for transfers between devices: 327 us -> 96.1 us
  Pallas kernels: 0 us -> 105 us
  matrix products: 109 us -> 22.7 us
  other arithmetic: 22.2 us -> 11.6 us
  blocking collectives: 8.24 us -> 0 us
  local copies, waits for them, and re-layouts: 22.8 us -> 29.4 us
    reduce_scatter x4 -> x0, waiting for transfers between devices: 141 us -> none  [the longest x1 104 us: shards(): lax.psum_scatter(sectioned.astype(jnp.bfloat16), 'seq', scatter_dimension...]
    pallas_call x0 -> x2, Pallas kernels: none -> 105 us  [the longest x1 73.3 us: backward(): pl.pallas_call(backward_kernel, in_specs=[vmem, anywhere, anywhere, anywh...]
    dot_general x12 -> x0, matrix products: 82.7 us -> none  [the longest x1 18.1 us: shards(): jnp.einsum('chqk,cqhd->ckhd', d_scores, query_heads, preferred_element_ty...]
    ppermute x3 -> x2, waiting for transfers between devices: 48.9 us -> 10.2 us  [swapped(): return lax.ppermute(value, axis, pairs)]
    all_gather x1, waiting for transfers between devices: 87 us -> 55.8 us  [shards(): w_full = lax.all_gather(w_query, ('section', 'seq'), axis=0, tiled=True)]
    unnamed x29 -> x28, local copies, waits for them, and re-layouts: 5.9 us -> 22.3 us
    reduce_scatter x1, waiting for transfers between devices: 24.5 us -> 10.2 us  [shards(): lax.psum_scatter(state_part.astype(jnp.bfloat16), 'tensor', scatter_dimen...]
    convert_element_type x4 -> x0, local copies, waits for them, and re-layouts: 8.72 us -> none  [the longest x1 4.29 us: shards(): d_keys = jnp.einsum('chqk,cqhd->ckhd', d_scores, query_heads, preferred_e...]
  transfers between devices with their start and end apart: 10 -> 5, of which waited for: 9 -> 4; matrix products, arithmetic and copies ran while one was open for 16% -> 11% of each run, Pallas kernels for 0% -> 11%
where the time goes in v1:
time: 286 us; the launch traced here: 285 us
  Pallas kernels  105 us (37%)
  waiting for transfers between devices  96.1 us (34%)
  local copies, waits for them, and re-layouts  29.4 us (10%)
  matrix products  22.7 us (8%)
  between operations  15.7 us (5%)
  other arithmetic  11.6 us (4%)
  starting transfers between devices  4.74 us (2%)
    pallas_call x1, Pallas kernels, backward(): pl.pallas_call(backward_kernel, in_specs=[vmem, anywhere, anywhere, anywh...  73.3 us
    all_gather x1, waiting for transfers between devices, shards(): w_full = lax.all_gather(w_query, ('section', 'seq'), axis=0, tiled=True)  55.8 us
    pallas_call x1, Pallas kernels, attend(): pl.pallas_call(attend_kernel, grid=(blocks,), in_specs=[pl.BlockSpec(memo...  31.6 us
    unnamed x28, local copies, waits for them, and re-layouts  22.3 us
    all_gather x1, waiting for transfers between devices, shards(): encoded_all = lax.all_gather(encoded_home, 'tensor', axis=0, tiled=True)  19.4 us
    dot_general x1, matrix products, shards(): jnp.dot(normed, w_full, preferred_element_type=jnp.float32)  11.6 us
    ppermute x2, waiting for transfers between devices, swapped(): return lax.ppermute(value, axis, pairs)  10.2 us
    reduce_scatter x1, waiting for transfers between devices, shards(): lax.psum_scatter(state_part.astype(jnp.bfloat16), 'tensor', scatter_dimen...  10.2 us
  transfers between devices with their start and end apart: 5, of which 4 were waited for; matrix products, arithmetic and copies ran while one was open for 11% of the time, Pallas kernels for 11%

profile of v1, /device:TPU:1, one launch (start us, length us, event | category | flops | bytes accessed | tf_op | source)
XLA Modules:
  0.0 285.0 jit_solution(5249956381626882921)
XLA Ops:
  8.1 6.5 %copy.27 = bf16[256,8192]{0,1:T(8,128)(2,1)} copy(bf16[256,8192]{1,0:T(8,128)(2,1)} %tokens_ref.1) | data formatting | bytes 8388608 | tf_op args[0]
  14.6 3.3 %fusion.1 = f32[256]{0:T(256)S(1)} fusion(bf16[256,8192]{0,1:T(8,128)(2,1)} %copy.27), kind=kLoop, calls=%fused_computation.3 | loop fusion | flops 6291200 | bytes 4195328 | tf_op jit(solution)/shard_map/reduce_sum | solution.py:531
  17.9 5.0 %convert_multiply_fusion = bf16[256,8192]{0,1:T(8,128)(2,1)} fusion(bf16[256,8192]{0,1:T(8,128)(2,1)} %copy.27, f32[256]{0:T(256)S(1)} %add_rsqrt_fusion), kind=kLoop, calls=%fused_computation.1 | loop fusion | flops 6291456 | bytes 8389632 | tf_op jit(solution)/shard_map/mul | solution.py:532
  22.8 6.5 %convolution_convert_fusion = bf16[256,1792]{1,0:T(8,128)(2,1)} fusion(bf16[2048,1792]{1,0:T(8,128)(2,1)} %param.15, bf16[256,8192]{0,1:T(8,128)(2,1)} %convert_multiply_fusion, s32[]{:T(128)S(6)} %select_n.17), kind=kOutput, calls=%fused_computation.5 | convolution fusion | flops 1879506944 | bytes 9306116 | tf_op jit(solution)/shard_map/dot_general | solution.py:536
  30.0 2.5 collective-permute-start
  32.5 10.2 %collective-permute-done = bf16[1,2,128,896]{3,2,1,0:T(8,128)(2,1)S(1)} collective-permute-done((bf16[1,2,128,896]{3,2,1,0:T(8,128)(2,1)S(1)}, bf16[1,2,128,896]{3,2,1,0:T(8,128)(2,1)S(1)}, u32[]{:S(2)}, u32[]{:S(2)}) %collective-permute-start) | collective-permute-done | bytes 458784 | tf_op jit(solution)/shard_map/ppermute | solution.py:35
  44.0 10.2 %reduce-scatter.2.cloned.1.call-done = bf16[64,1792]{1,0:T(8,128)(2,1)} async-done(((bf16[256,1792]{1,0:T(8,128)(2,1)}), bf16[64,1792]{1,0:T(8,128)(2,1)}) %reduce-scatter.2.cloned.1.call-update) | async-done | bytes 229392 | tf_op jit(solution)/shard_map/reduce_scatter | solution.py:537
  54.2 1.0 fusion.14
  56.7 2.9 %fusion.4 = bf16[256,896]{1,0:T(8,128)(2,1)} fusion(bf16[256,896]{0,1:T(8,128)(2,1)S(1)} %bitcast.52, bf16[896,896]{1,0:T(8,128)(2,1)} %param.19, bf16[256,896]{1,0:T(8,128)(2,1)S(1)} %bitcast.45), kind=kOutput, calls=%fused_computation.12 | convolution fusion | flops 411729920 | bytes 2981888 | tf_op jit(solution)/shard_map/dot_general | solution.py:62
  59.6 2.9 %multiply_convert_fusion = bf16[256,8192]{0,1:T(8,128)(2,1)S(1)} fusion(f32[8192]{0:T(1024)S(1)} %copy-done.8, f32[256]{0:T(256)S(1)} %add_rsqrt_fusion, bf16[256,8192]{0,1:T(8,128)(2,1)} %copy.27), kind=kLoop, calls=%fused_computation.4 | loop fusion | flops 8388608 | bytes 8422400 | tf_op jit(solution)/shard_map/convert_element_type | solution.py:534
  62.6 2.7 constant_dynamic-slice_fusion
  65.8 4.0 %copy.36 = bf16[256,16,1,256]{3,0,1,2:T(8,128)(2,1)} copy(bf16[256,16,1,256]{0,3,2,1:T(8,128)(2,1)} %get-tuple-element.21) | data formatting | bytes 4194304
  69.8 2.1 collective-permute-start.1
  71.8 3.9 %copy.35 = bf16[256,16,1,256]{3,0,1,2:T(8,128)(2,1)} copy(bf16[256,16,1,256]{0,3,2,1:T(8,128)(2,1)} %get-tuple-element.22) | data formatting | bytes 4194304
  75.8 0.8 copy.33.inverse_ref
  76.6 55.8 %all-gather.3.cloned.1.call-done = bf16[8192,1024]{1,0:T(8,128)(2,1)} async-done(((bf16[256,1024]{1,0:T(8,128)(2,1)}), bf16[8192,1024]{1,0:T(8,128)(2,1)}) %all-gather.3.cloned.1.call-update) | async-done | bytes 16777232 | tf_op jit(solution)/shard_map/all_gather | solution.py:542
  132.3 11.6 %convolution_convert_fusion.1.q_ref = bf16[256,1024]{1,0:T(8,128)(2,1)S(1)} fusion(bf16[256,8192]{0,1:T(8,128)(2,1)} %copy-done.6, bf16[8192,1024]{1,0:T(8,128)(2,1)} %all-gather.3.cloned.1.call-done), kind=kOutput, calls=%fused_computation.11 | convolution fusion | flops 4295229440 | bytes 21495808 | tf_op jit(solution)/shard_map/dot_general | solution.py:543
  143.9 19.4 %all-gather.5.cloned.1.call-done = bf16[4,2,128,896]{3,2,1,0:T(8,128)(2,1)} async-done(((bf16[1,2,128,896]{3,2,1,0:T(8,128)(2,1)}), bf16[4,2,128,896]{3,2,1,0:T(8,128)(2,1)}) %all-gather.5.cloned.1.call-update) | async-done | bytes 1835024 | tf_op jit(solution)/shard_map/all_gather | solution.py:541
  163.3 31.6 %shard_map.155 = (bf16[256,1024]{1,0:T(8,128)(2,1)}, bf16[256,1024]{1,0:T(8,128)(2,1)S(1)}, bf16[4,256,896]{2,1,0:T(8,128)(2,1)S(1)}, f32[256,128]{1,0:T(8,128)S(1)}) custom-call(s32[4]{0:T(128)S(1)} %copy-done.3, bf16[256,1024]{1,0:T(8,128)(2,1)S(1)} %convolution_convert_fusion.1.q_ref, bf16[1024,896]{1,0:T(8,128)(2,1)} %bitcast.58, ...), custom_call_target="tpu_custom_call" | custom-call | flops 8321499136 | bytes 14680064 | tf_op jit(solution)/shard_map/pallas_call | solution.py:107
  194.9 1.2 copy-done.4
  197.6 73.3 %shard_map.156 = (f32[256,1024]{1,0:T(8,128)}, bf16[256,2048]{1,0:T(8,128)(2,1)}, bf16[256,896]{1,0:T(8,128)(2,1)}, f32[8,256]{1,0:T(8,128)}) custom-call(bf16[256,1024]{1,0:T(8,128)(2,1)} %copy-done.5, bf16[16,256,256]{2,1,0:T(8,128)(2,1)} %bitcast.46, bf16[16,256,256]{2,1,0:T(8,128)(2,1)} %collective-permute-done.1.sib_ref, ...), custom_call_target="tpu_custom_call" | custom-call | flops 8589934592 | bytes 20971520 | tf_op jit(solution)/shard_map/pallas_call | solution.py:462
  270.9 1.3 slice.15
  272.2 2.3 copy.46
  274.5 2.3 copy.47
  (42 shorter events, 6.2 us)
Async XLA Ops:
  8.0 35.1 %copy-start = (bf16[896,896]{1,0:T(8,128)(2,1)S(1)}, bf16[896,896]{1,0:T(8,128)(2,1)}, u32[]{:S(2)}) copy-start(bf16[896,896]{1,0:T(8,128)(2,1)} %param.18) | copy-start | bytes 4816900
  8.0 46.2 %reduce-scatter.2.cloned.1.call-start = ((), (), s32[]{:S(2)}) async-start(), calls=%async_computation.2 | async-start | bytes 1146880 | tf_op jit(solution)/shard_map/reduce_scatter | solution.py:537
  22.8 7.1 %copy-start.10 = (bf16[1,1,2,128,896]{4,3,2,1,0:T(8,128)(2,1)S(1)}, bf16[1,1,2,128,896]{4,3,2,1,0:T(8,128)(2,1)}, u32[]{:S(2)}) copy-start(bf16[1,1,2,128,896]{4,3,2,1,0:T(8,128)(2,1)} %param.16) | copy-start | bytes 1376260
  22.8 20.1 %copy-start.9 = (f32[896]{0:T(1024)S(1)}, f32[896]{0:T(1024)}, u32[]{:S(2)}) copy-start(f32[896]{0:T(1024)} %param.17) | copy-start | bytes 10756
  29.3 103.0 %all-gather.3.cloned.1.call-start = ((), (), s32[]{:S(2)}) async-start(), calls=%async_computation.1 | async-start | bytes 17301504 | tf_op jit(solution)/shard_map/all_gather | solution.py:542
  29.9 133.4 %all-gather.5.cloned.1.call-start = ((), (), s32[]{:S(2)}) async-start(), calls=%async_computation.3 | async-start | bytes 2293760 | tf_op jit(solution)/shard_map/all_gather | solution.py:541
  30.0 12.8 %collective-permute-start = (bf16[1,2,128,896]{3,2,1,0:T(8,128)(2,1)S(1)}, bf16[1,2,128,896]{3,2,1,0:T(8,128)(2,1)S(1)}, u32[]{:S(2)}, u32[]{:S(2)}) collective-permute-start(bf16[1,2,128,896]{3,2,1,0:T(8,128)(2,1)S(1)} %bitcast.59), channel_id=1, source_target_pairs={{0,64},{64,0},{1,65},{65,1},{2,66},{66,2},{3,67},{67,3},{4,68},{68... | collective-permute-start | bytes 1376264 | tf_op jit(solution)/shard_map/ppermute | solution.py:35
  56.3 3.3 %copy-start.8 = (f32[8192]{0:T(1024)S(1)}, f32[8192]{0:T(1024)}, u32[]{:S(2)}) copy-start(f32[8192]{0:T(1024)} %param.14) | copy-start | bytes 98308
  62.6 3.2 %copy-start.6 = (bf16[256,8192]{0,1:T(8,128)(2,1)}, bf16[256,8192]{0,1:T(8,128)(2,1)S(1)}, u32[]{:S(2)}) copy-start(bf16[256,8192]{0,1:T(8,128)(2,1)S(1)} %multiply_convert_fusion) | copy-start | bytes 12582916
  69.8 127.3 %collective-permute-start.1 = (bf16[16,256,256]{2,1,0:T(8,128)(2,1)}, bf16[16,256,256]{2,1,0:T(8,128)(2,1)}, u32[]{:S(2)}, u32[]{:S(2)}) collective-permute-start(bf16[16,256,256]{2,1,0:T(8,128)(2,1)} %bitcast.47), channel_id=1, source_target_pairs={{0,4},{4,0},{8,12},{12,8},{16,20},{20,16},{24,28},{28,24},{32,36},... | collective-permute-start | bytes 6291464 | tf_op jit(solution)/shard_map/ppermute | solution.py:35
  76.6 86.7 %copy-start.2 = (bf16[256,1024]{1,0:T(8,128)(2,1)S(1)}, bf16[256,1024]{1,0:T(8,128)(2,1)}, u32[]{:S(2)}) copy-start(bf16[256,1024]{1,0:T(8,128)(2,1)} %do_ref.1) | copy-start | bytes 1572868
  76.6 86.7 %copy-start.3 = (s32[4]{0:T(128)S(1)}, s32[4]{0:T(128)}, u32[]{:S(2)}) copy-start(s32[4]{0:T(128)} %counts.1) | copy-start | bytes 52
  194.9 1.3 copy-start.4
  196.1 0.8 copy-start.5
  197.6 80.0 %copy-start.1 = (bf16[896,896]{1,0:T(8,128)(2,1)S(1)}, bf16[896,896]{1,0:T(8,128)(2,1)}, u32[]{:S(2)}) copy-start(bf16[896,896]{1,0:T(8,128)(2,1)} %param.18) | copy-start | bytes 4816900
  270.9 5.9 %copy-start.7 = (bf16[256,896]{1,0:T(8,128)(2,1)S(1)}, bf16[256,896]{1,0:T(8,128)(2,1)}, u32[]{:S(2)}) copy-start(bf16[256,896]{1,0:T(8,128)(2,1)} %get-tuple-element.19) | copy-start | bytes 1376260
Sparse Core Ops, SparseCore 0:
  29.4 24.7 reduce-scatter.1
Sparse Core Ops, SparseCore 1:
  31.5 100.7 all-gather.2
  134.4 28.8 all-gather.4

commit v2 on v1

--- a/solution.py
+++ b/solution.py
@@ -29,88 +29,58 @@
     return lax.dot_general(a, b, dims, preferred_element_type=F32)
 
 
-def swapped(value, axis, distance):
-    mask = 2**distance
-    pairs = [(source, source ^ mask) for source in range(lax.axis_size(axis))]
-    return lax.ppermute(value, axis, pairs)
-
-
-def encode(enc_in, block_states, enc_gain, enc_query, enc_out):
-    block_count = enc_in.shape[0]
-    heads_enc = E // EHD
-    enc_rows = enc_in.astype(jnp.float32).reshape(-1, E)
-    enc_scale = lax.rsqrt(jnp.mean(enc_rows * enc_rows, axis=-1, keepdims=True) + EPSILON)
-    enc_normed = (enc_rows * enc_scale * enc_gain).astype(jnp.bfloat16)
-    enc_queries = jnp.dot(enc_normed, enc_query, preferred_element_type=jnp.float32).astype(
-        jnp.bfloat16
-    )
-    query_heads = enc_queries.reshape(block_count, NBR * RLEN, heads_enc, EHD)
-    state_rows = block_states.reshape(block_count, BLOCK, 2 * E)
-    key_heads = state_rows[:, :, :E].reshape(block_count, BLOCK, heads_enc, EHD)
-    value_heads = state_rows[:, :, E:].reshape(block_count, BLOCK, heads_enc, EHD)
-    scores = jnp.einsum(
-        "cqhd,ckhd->chqk", query_heads, key_heads, preferred_element_type=jnp.float32
-    ) / math.sqrt(EHD)
-    row_top = jnp.max(scores, axis=-1, keepdims=True)
-    weights = jnp.exp(scores - row_top)
-    enc_weights = (weights / jnp.sum(weights, axis=-1, keepdims=True)).astype(jnp.bfloat16)
-    enc_context = (
-        jnp.einsum("chqk,ckhd->cqhd", enc_weights, value_heads, preferred_element_type=jnp.float32)
-        .astype(jnp.bfloat16)
-        .reshape(-1, E)
-    )
-    mixed = enc_rows + jnp.dot(enc_context, enc_out, preferred_element_type=jnp.float32)
-    return mixed.astype(jnp.bfloat16).reshape(block_count, NBR, RLEN, E)
-
-
 def attend_kernel(
-    counts, q_ref, enc_ref, wk_ref, wv_ref, do_ref,
+    counts, q_ref, k_ref, v_ref, wk_ref, wv_ref, do_ref,
     ctx_ref, dq_ref, grad_ref, sums_ref,
-    k_s, v_s, dk_s, dv_s,
+    score_s, dprob_s, weight_s, dscore_s, dk_s, dv_s,
 ):
     count = counts[pl.program_id(0)]
-    enc = enc_ref[...]
-    k_s[...] = dot(enc, wk_ref[...]).astype(BF16)
-    v_s[...] = dot(enc, wv_ref[...]).astype(BF16)
+    heads = q_ref.shape[1] // HD
     valid = lax.broadcasted_iota(jnp.int32, (BLOCK, KEYS), 1) < count * RLEN
     empty = jnp.where(count == 0, 1.0, 0.0).astype(F32)
     scale = 1.0 / math.sqrt(HD)
-    total = jnp.zeros((BLOCK, HD), F32)
-    for head in range(q_ref.shape[1] // HD):
-        cols = slice(head * HD, (head + 1) * HD)
-        q, k, v, do = q_ref[:, cols], k_s[:, cols], v_s[:, cols], do_ref[:, cols]
-        scores = dot(q, k, LAST) * scale
+    spans = [slice(head * HD, (head + 1) * HD) for head in range(heads)]
+    for head, cols in enumerate(spans):
+        score_s[head] = dot(q_ref[:, cols], k_ref[:, cols], LAST) * scale
+        dprob_s[head] = dot(do_ref[:, cols], v_ref[:, cols], LAST)
+    for head in range(heads):
+        scores = score_s[head]
         top = jnp.max(jnp.where(valid, scores, NEG_LARGE), axis=-1, keepdims=True)
         weights = jnp.where(valid, jnp.exp(scores - top), 0.0)
         probs = weights / (jnp.sum(weights, axis=-1, keepdims=True) + empty)
-        rounded = probs.astype(BF16)
-        ctx_ref[:, cols] = dot(rounded, v).astype(BF16)
-        dv_s[:, cols] = dot(rounded, do, FIRST).astype(BF16)
-        d_probs = dot(do, v, LAST)
+        weight_s[head] = probs.astype(BF16)
+        d_probs = dprob_s[head]
         inner = jnp.sum(probs * d_probs, axis=-1, keepdims=True)
-        d_scores = (probs * (d_probs - inner) * scale).astype(BF16)
-        dq = dot(d_scores, k)
+        dscore_s[head] = (probs * (d_probs - inner) * scale).astype(BF16)
+    total = jnp.zeros((BLOCK, HD), F32)
+    for head, cols in enumerate(spans):
+        ctx_ref[:, cols] = dot(weight_s[head], v_ref[:, cols]).astype(BF16)
+        dq = dot(dscore_s[head], k_ref[:, cols])
         dq_ref[:, cols] = dq.astype(BF16)
-        total = total + dq * q.astype(F32)
-        dk_s[:, cols] = dot(d_scores, q, FIRST).astype(BF16)
+        total = total + dq * q_ref[:, cols].astype(F32)
+        dv_s[:, cols] = dot(weight_s[head], do_ref[:, cols], FIRST).astype(BF16)
+        dk_s[:, cols] = dot(dscore_s[head], q_ref[:, cols], FIRST).astype(BF16)
     grad = dot(dk_s[...], wk_ref[...], LAST) + dot(dv_s[...], wv_ref[...], LAST)
     grad_ref[0] = grad.astype(BF16)
     sums_ref[...] = jnp.broadcast_to(jnp.sum(total, axis=-1, keepdims=True), (BLOCK, HD))
 
 
-def attend(counts, queries, encoded, w_key, w_value, d_context):
+def attend(counts, queries, keys, values, w_key, w_value, d_context):
     blocks = counts.shape[0]
     rows, width = queries.shape
+    heads = width // HD
     row_block = pl.BlockSpec((BLOCK, width), lambda b: (b, 0))
+    key_block = pl.BlockSpec((KEYS, width), lambda b: (b, 0))
     weight = pl.BlockSpec((E, width), lambda b: (0, 0))
-    flops = 2 * (4 * rows * 4 * E * width + 6 * rows * KEYS * width)
+    flops = 2 * (4 * rows * 2 * E * width + 6 * rows * KEYS * width)
     return pl.pallas_call(
         attend_kernel,
         grid=(blocks,),
         in_specs=[
             pl.BlockSpec(memory_space=pltpu.SMEM),
             row_block,
-            pl.BlockSpec((KEYS, E), lambda b: (b, 0)),
+            key_block,
+            key_block,
             weight,
             weight,
             row_block,
@@ -127,12 +97,14 @@
             jax.ShapeDtypeStruct((blocks, KEYS, E), BF16),
             jax.ShapeDtypeStruct((rows, HD), F32),
         ],
-        scratch_shapes=[pltpu.VMEM((KEYS, width), BF16)] * 4,
+        scratch_shapes=[pltpu.VMEM((heads, BLOCK, KEYS), F32)] * 2
+        + [pltpu.VMEM((heads, BLOCK, KEYS), BF16)] * 2
+        + [pltpu.VMEM((KEYS, width), BF16)] * 2,
         compiler_params=pltpu.CompilerParams(vmem_limit_bytes=50 * 2**20),
         cost_estimate=pl.CostEstimate(
             flops=flops, bytes_accessed=14 * 2**20, transcendentals=rows * 8 * KEYS
         ),
-    )(counts, queries, encoded, w_key, w_value, d_context)
+    )(counts, queries, keys, values, w_key, w_value, d_context)
 
 
 class Place:
@@ -173,11 +145,342 @@
     pl.semaphore_wait(barrier, len(devices))
 
 
+class Sender:
+    def __init__(self, send_sem, recv_sem):
+        self.send_sem, self.recv_sem, self.copies = send_sem, recv_sem, []
+
+    def __call__(self, src, dst, device):
+        index = len(self.copies)
+        copy = pltpu.make_async_remote_copy(
+            src_ref=src, dst_ref=dst, send_sem=self.send_sem.at[index],
+            recv_sem=self.recv_sem.at[index], device_id=device, device_id_type=MESH,
+        )
+        copy.start()
+        self.copies.append(copy)
+        return copy
+
+
+Y_FIRST = 96
+CHUNK = 256
+
+
+def wide(column):
+    return jnp.concatenate([column, column], axis=1)
+
+
+def forward_kernel(
+    tokens_ref, w_ref, gain_ref, state_ref, near_ref, egain_ref, equery_ref, eout_ref, wk_ref, wv_ref,
+    q_ref, w_out, nrm_out, k_out, v_out, inv_ref,
+    tok, wc, nrm, theirs, skv, unit, acc, q_send, q_in,
+    sp, sr1, sr2, enc_in, eq_s, ectx, escore, equery, eout, enc, wk, wv, ks, vs,
+    load_sem, out_sem, send_sem, recv_sem,
+):
+    at = Place()
+    share = tok.shape[1] // 4
+    send = Sender(send_sem, recv_sem)
+    me = at.chunk(0, 0)
+    pairs = (
+        (w_ref, wc.at[me]), (tokens_ref, tok), (state_ref, skv), (equery_ref, equery),
+        (eout_ref, eout), (wk_ref, wk), (wv_ref, wv),
+    )
+    loads = [pltpu.make_async_copy(src, dst, load_sem.at[i]) for i, (src, dst) in enumerate(pairs)]
+    for load in loads:
+        load.start()
+    greet(
+        [at.along("x", 1), at.along("x", 3), at.along("y", 1), at.along("y", 3),
+         at.along("z", 1), at.along("z", 3), at.sibling()]
+    )
+
+    dims = (("y", "z"), ("z", "y"))
+    spans = ((0, Y_FIRST), (Y_FIRST, CHUNK))
+
+    def piece(half, first, second, part=None):
+        dy, dz = (first, second) if half == 0 else (second, first)
+        low, high = spans[half]
+        middle = (low + high) // 2
+        low, high = (low, high) if part is None else ((low, middle), (middle, high))[part]
+        return wc.at[at.chunk(dy, dz), low:high]
+
+    def pass_on(ref, dim, off):
+        return send(ref, ref, at.along(dim, off))
+
+    near, relay, cross, last = {}, {}, {}, {}
+
+    def across(half, line):
+        dim = dims[half][1]
+        block = piece(half, line, 0)
+        cross[half, line] = (pass_on(block, dim, 1), pass_on(block, dim, 3))
+
+    def first_round(half):
+        dim = dims[half][0]
+        near[half][0].wait_recv()
+        relay[half] = [pass_on(piece(half, 3, 0, 0), dim, 1)]
+        across(half, 3)
+        near[half][1].wait_recv()
+        relay[half].append(pass_on(piece(half, 1, 0, 1), dim, 3))
+        across(half, 1)
+
+    def second_round(half):
+        relay[half][0].wait_recv()
+        relay[half][1].wait_recv()
+        across(half, 2)
+
+    def crossed(half, line):
+        dim = dims[half][1]
+        cross[half, line][0].wait_recv()
+        first = pass_on(piece(half, line, 3, 0), dim, 1)
+        cross[half, line][1].wait_recv()
+        last[half, line] = (first, pass_on(piece(half, line, 1, 1), dim, 3))
+
+    def landed(half, line):
+        last[half, line][0].wait_recv()
+        last[half, line][1].wait_recv()
+
+    outs = []
+
+    def write(src, dst):
+        copy = pltpu.make_async_copy(src, dst, out_sem.at[len(outs)])
+        copy.start()
+        outs.append(copy)
+
+    def accumulate(offsets, begin=False):
+        chunks = [at.chunk(dy, dz) for dy, dz in offsets]
+        for k in chunks:
+            write(wc.at[k], w_out.at[k])
+
+        @pl.loop(0, 4)
+        def _(i):
+            rows = pl.ds(pl.multiple_of((i // 2) * 256, 256), 256)
+            cols = pl.ds(pl.multiple_of((i % 2) * 512, 512), 512)
+            total = dot(nrm[chunks[0], rows, :], wc[chunks[0], :, cols])
+            for k in chunks[1:]:
+                total = total + dot(nrm[k, rows, :], wc[k, :, cols])
+            acc[rows, cols] = total if begin else acc[rows, cols] + total
+
+    loads[0].wait()
+    for half in (0, 1):
+        block = piece(half, 0, 0)
+        near[half] = (pass_on(block, dims[half][0], 1), pass_on(block, dims[half][0], 3))
+    c_near = send(near_ref, enc_in, at.partner())
+    for half in (0, 1):
+        across(half, 0)
+
+    loads[1].wait()
+
+    @pl.loop(0, 16)
+    def _(i):
+        rows = pl.ds(pl.multiple_of(i * 16, 16), 16)
+        values = tok[rows, :].astype(F32)
+        square = jnp.sum(values * values, axis=-1, keepdims=True)
+        inverse = lax.rsqrt(square * (1.0 / tok.shape[1]) + EPSILON)
+        inv_ref[rows, :] = jnp.broadcast_to(inverse, (16, 128))
+
+    @pl.loop(0, 8)
+    def _(i):
+        source = pl.ds(pl.multiple_of(at.x * share + i * 256, 256), 256)
+        target = pl.ds(pl.multiple_of(i * 256, 256), 256)
+        unit[:, target] = (tok[:, source].astype(F32) * wide(inv_ref[...])).astype(BF16)
+
+    loads[2].wait()
+
+    @pl.loop(0, 7)
+    def _(i):
+        cols = pl.ds(pl.multiple_of(i * 256, 256), 256)
+        part = dot(unit[...], skv[:, cols]).astype(BF16)
+        for j in range(4):
+            sp[j, :, cols] = part[64 * j : 64 * j + 64]
+
+    far, up, down = (at.x + 2) % 4, (at.x + 1) % 4, (at.x + 3) % 4
+    c_s1 = (
+        send(sp.at[far, 0:32], sr1.at[0], at.along("x", 1)),
+        send(sp.at[far, 32:64], sr1.at[1], at.along("x", 3)),
+    )
+    first_round(0)
+    first_round(1)
+
+    @pl.loop(0, 16)
+    def _(k):
+        def chunk(g):
+            cols = pl.ds(pl.multiple_of(g * CHUNK, CHUNK), CHUNK)
+            return (tok[:, cols].astype(F32) * wide(inv_ref[...]) * gain_ref[g]).astype(BF16)
+
+        nrm[k, 0:256] = chunk(2 * k + at.core)
+        theirs[k] = chunk(2 * k + 1 - at.core)
+
+    c_nrm = send(theirs, nrm.at[:, 256:512], at.sibling())
+
+    for way, block in ((0, up), (1, down)):
+        c_s1[way].wait_recv()
+        rows = slice(32 * way, 32 * way + 32)
+        sp[block, rows] = (sp[block, rows].astype(F32) + sr1[way].astype(F32)).astype(BF16)
+    c_s2 = (
+        send(sp.at[up], sr2.at[0], at.along("x", 1)),
+        send(sp.at[down], sr2.at[1], at.along("x", 3)),
+    )
+    second_round(0)
+    second_round(1)
+
+    loads[3].wait()
+    c_near.wait_recv()
+    enc_rows = enc_in[...].astype(F32)
+    mean = jnp.sum(enc_rows * enc_rows, axis=-1, keepdims=True) * (1.0 / E)
+    enc_normed = (enc_rows * lax.rsqrt(mean + EPSILON) * egain_ref[...]).astype(BF16)
+    eq_s[...] = dot(enc_normed, equery[...]).astype(BF16)
+    for half in (0, 1):
+        crossed(half, 0)
+
+    c_s2[0].wait_recv()
+    c_s2[1].wait_recv()
+    states = (sp[at.x].astype(F32) + sr2[0].astype(F32) + sr2[1].astype(F32)).astype(BF16)
+    states = states.astype(F32)
+    left = lax.broadcasted_iota(jnp.int32, (BLOCK, 128), 1) < EHD
+    left_wide = lax.broadcasted_iota(jnp.int32, (KEYS, 128), 1) < EHD
+
+    def doubled(cols):
+        both = states[:, cols]
+        return jnp.concatenate(
+            [jnp.where(left, both, 0.0), jnp.where(left, 0.0, both)], axis=0
+        ).astype(BF16)
+
+    for j in range(7):
+        keys = doubled(slice(128 * j, 128 * j + 128))
+        escore[j] = dot(eq_s[:, 128 * j : 128 * j + 128], keys, LAST) * (1.0 / math.sqrt(EHD))
+    for j in range(7):
+        scores = escore[j]
+        top_left = jnp.max(jnp.where(left_wide, scores, NEG_LARGE), axis=-1, keepdims=True)
+        top_right = jnp.max(jnp.where(left_wide, NEG_LARGE, scores), axis=-1, keepdims=True)
+        weights = jnp.exp(scores - jnp.where(left_wide, top_left, top_right))
+        sum_left = jnp.sum(jnp.where(left_wide, weights, 0.0), axis=-1, keepdims=True)
+        sum_right = jnp.sum(jnp.where(left_wide, 0.0, weights), axis=-1, keepdims=True)
+        escore[j] = weights / jnp.where(left_wide, sum_left, sum_right)
+    for j in range(7):
+        values = doubled(slice(E + 128 * j, E + 128 * j + 128))
+        ectx[:, 128 * j : 128 * j + 128] = dot(escore[j].astype(BF16), values).astype(BF16)
+    loads[4].wait()
+    enc[at.x] = (enc_in[...].astype(F32) + dot(ectx[...], eout[...])).astype(BF16)
+    c_e1 = (
+        send(enc.at[at.x], enc.at[at.x], at.along("x", 1)),
+        send(enc.at[at.x], enc.at[at.x], at.along("x", 3)),
+    )
+    loads[5].wait()
+    loads[6].wait()
+
+    def project(block):
+        @pl.loop(0, 4)
+        def _(i):
+            cols = pl.ds(pl.multiple_of(i * 256, 256), 256)
+            ks[block, :, cols] = dot(enc[block], wk[:, cols]).astype(BF16)
+            vs[block, :, cols] = dot(enc[block], wv[:, cols]).astype(BF16)
+
+        write(ks.at[block], k_out.at[block])
+        write(vs.at[block], v_out.at[block])
+
+    c_nrm.wait_recv()
+    write(nrm, nrm_out)
+    accumulate([(0, 0), (1, 0), (3, 0), (0, 1), (0, 3)], begin=True)
+    for line in (3, 1):
+        for half in (0, 1):
+            crossed(half, line)
+    project(at.x)
+    c_e1[0].wait_recv()
+    c_e2 = [send(enc.at[down, 0:128], enc.at[down, 0:128], at.along("x", 1))]
+    c_e1[1].wait_recv()
+    c_e2.append(send(enc.at[up, 128:256], enc.at[up, 128:256], at.along("x", 3)))
+    project(down)
+    project(up)
+    accumulate([(1, 1), (1, 3), (3, 1), (3, 3)])
+    for half in (0, 1):
+        crossed(half, 2)
+    landed(0, 0)
+    landed(1, 0)
+    accumulate([(2, 0), (0, 2)])
+    c_e2[0].wait_recv()
+    c_e2[1].wait_recv()
+    project(far)
+    for line in (3, 1):
+        landed(0, line)
+        landed(1, line)
+    accumulate([(2, 1), (2, 3), (1, 2), (3, 2)])
+    landed(0, 2)
+    landed(1, 2)
+    accumulate([(2, 2)])
+    q_send[...] = acc[256:512].astype(BF16)
+    c_q = send(q_send, q_in, at.sibling())
+    c_q.wait_recv()
+    q_ref[...] = (acc[0:256] + q_in[...].astype(F32)).astype(BF16)
+    for copy in send.copies:
+        copy.wait_send()
+    for copy in outs:
+        copy.wait()
+
+
+FORWARD_SENDS = 4 + 1 + 4 + 2 * 6 + 2 * 2 + 16 + 2 + 2 + 1 + 2 + 2 + 1
+
+
+def forward(tokens, w_query, gain, state_kv, near, enc_gain, enc_query, enc_out, w_key, w_value):
+    rows, full = tokens.shape
+    width = w_query.shape[1]
+    vmem = pl.BlockSpec(memory_space=pltpu.VMEM)
+    anywhere = pl.BlockSpec(memory_space=pl.ANY)
+
+    def buffer(*shape, kind=BF16):
+        return pltpu.VMEM(shape, kind)
+
+    return pl.pallas_call(
+        forward_kernel,
+        in_specs=[anywhere, anywhere, vmem, anywhere, anywhere, vmem] + [anywhere] * 4,
+        out_specs=[vmem] + [anywhere] * 4 + [vmem],
+        out_shape=[
+            jax.ShapeDtypeStruct((rows, width), BF16),
+            jax.ShapeDtypeStruct((16, CHUNK, width), BF16),
+            jax.ShapeDtypeStruct((16, 2 * rows, CHUNK), BF16),
+            jax.ShapeDtypeStruct((4, KEYS, width), BF16),
+            jax.ShapeDtypeStruct((4, KEYS, width), BF16),
+            jax.ShapeDtypeStruct((rows, 128), F32),
+        ],
+        scratch_shapes=[
+            buffer(rows, full),
+            buffer(16, CHUNK, width),
+            buffer(16, 2 * rows, CHUNK),
+            buffer(16, rows, CHUNK),
+            buffer(full // 4, 2 * E),
+            buffer(rows, full // 4),
+            buffer(2 * rows, width, kind=F32),
+            buffer(rows, width),
+            buffer(rows, width),
+            buffer(4, BLOCK, 2 * E),
+            buffer(2, BLOCK // 2, 2 * E),
+            buffer(2, BLOCK, 2 * E),
+            buffer(KEYS, E),
+            buffer(KEYS, E),
+            buffer(KEYS, E),
+            buffer(7, KEYS, 128, kind=F32),
+            buffer(E, E),
+            buffer(E, E),
+            buffer(4, KEYS, E),
+            buffer(E, width),
+            buffer(E, width),
+            buffer(4, KEYS, width),
+            buffer(4, KEYS, width),
+            pltpu.SemaphoreType.DMA((7,)),
+            pltpu.SemaphoreType.DMA((25,)),
+            pltpu.SemaphoreType.DMA((FORWARD_SENDS,)),
+            pltpu.SemaphoreType.DMA((FORWARD_SENDS,)),
+        ],
+        compiler_params=pltpu.CompilerParams(
+            collective_id=2, has_side_effects=True, vmem_limit_bytes=60 * 2**20
+        ),
+        cost_estimate=pl.CostEstimate(
+            flops=2 * 5400 * 2**20, bytes_accessed=40 * 2**20, transcendentals=0
+        ),
+    )(tokens, w_query, gain, state_kv, near, enc_gain, enc_query, enc_out, w_key, w_value)
+
+
 LINES = (2, 1, 3, 0)
 
 
 def backward_kernel(
-    dq_ref, mine_ref, sib_ref, w_ref, grad_ref, sums_ref, tokens_ref, inverse_ref, gain_ref,
+    dq_ref, nrm_ref, w_ref, grad_ref, sums_ref, tokens_ref, inverse_ref, gain_ref,
     dw_ref, dh_ref, de_ref, dots_ref,
     dq2, dq_t, nrm, wc, prod, ra1, ra2, rb1, rb2, part, rn1, rn2, out_sib, in_sib,
     g1, gs, g2, gfin, gin, sums_in, tok, dh_s, column,
@@ -187,14 +490,13 @@
     width = tokens_ref.shape[1]
     share = width // 4
     loads = [
-        pltpu.make_async_copy(mine_ref, nrm.at[:, 0:256], load_sem.at[0]),
-        pltpu.make_async_copy(sib_ref, nrm.at[:, 256:512], load_sem.at[1]),
-        pltpu.make_async_copy(w_ref.at[:, at.core], wc, load_sem.at[2]),
+        pltpu.make_async_copy(nrm_ref, nrm, load_sem.at[0]),
+        pltpu.make_async_copy(w_ref, wc, load_sem.at[1]),
     ]
     for i in range(8):
         first = pl.multiple_of(at.x * share + i * 256, 256)
         loads.append(
-            pltpu.make_async_copy(tokens_ref.at[:, pl.ds(first, 256)], tok.at[i], load_sem.at[3 + i])
+            pltpu.make_async_copy(tokens_ref.at[:, pl.ds(first, 256)], tok.at[i], load_sem.at[2 + i])
         )
     for load in loads:
         load.start()
@@ -203,17 +505,7 @@
          at.along("z", 1), at.along("z", 3), at.sibling()]
     )
 
-    copies = []
-
-    def send(src, dst, device):
-        index = len(copies)
-        copy = pltpu.make_async_remote_copy(
-            src_ref=src, dst_ref=dst, send_sem=send_sem.at[index], recv_sem=recv_sem.at[index],
-            device_id=device, device_id_type=MESH,
-        )
-        copy.start()
-        copies.append(copy)
-        return copy
+    send = Sender(send_sem, recv_sem)
 
     def added(dst, first, second):
         dst[...] = (first[...].astype(F32) + second[...].astype(F32)).astype(BF16)
@@ -235,7 +527,6 @@
             dq2[256:512, 256 * j : 256 * j + 256]
         )
     loads[0].wait()
-    loads[1].wait()
 
     def product(dy, dz):
         k = at.chunk(dy, dz)
@@ -305,7 +596,7 @@
             part[k, rows, :] = dot(dq2[rows, :], wc[k], LAST).astype(BF16)
 
     n1, n2 = [], []
-    loads[2].wait()
+    loads[1].wait()
     second_hop(0, 2)
     second_hop(1, 2)
     for m in range(4):
@@ -357,15 +648,16 @@
         total = piece[...].astype(F32) + ra2[half, slot, 0].astype(F32)
         piece[...] = (total + ra2[half, slot, 1].astype(F32)).astype(BF16)
 
-    for load in loads[3:]:
+    for load in loads[2:]:
         load.wait()
     stores = []
 
     def finish(i, d_normed):
-        unit = tok[i].astype(F32) * inverse_ref[...]
-        rows = jnp.concatenate([column[...], column[...]], axis=1)
+        inverse = wide(inverse_ref[...])
+        unit = tok[i].astype(F32) * inverse
+        rows = wide(column[...])
         grads = d_normed * gain_ref[at.x * 8 + i]
-        result = inverse_ref[...] * (grads - unit * (rows * (1.0 / width)))
+        result = inverse * (grads - unit * (rows * (1.0 / width)))
         dh_s[i] = result.astype(BF16)
         first = pl.multiple_of(i * 256, 256)
         store = pltpu.make_async_copy(
@@ -441,7 +733,7 @@
         finish(2 * m + 1 - at.core, in_sib[m].astype(F32))
     c_swap.wait_recv()
     de_ref[...] = gin[...]
-    for copy in copies:
+    for copy in send.copies:
         copy.wait_send()
     for store in stores:
         store.wait()
@@ -450,7 +742,7 @@
 SENDS = 1 + 2 + 3 + 16 + 2 + 16 + 8 + 8 + 1 + 4 + 8
 
 
-def backward(d_queries, mine, theirs, w_all, grad, sums, tokens, inverse, gain):
+def backward(d_queries, normed, w_all, grad, sums, tokens, inverse, gain):
     rows, width = d_queries.shape
     full = tokens.shape[1]
     vmem = pl.BlockSpec(memory_space=pltpu.VMEM)
@@ -461,7 +753,7 @@
 
     return pl.pallas_call(
         backward_kernel,
-        in_specs=[vmem, anywhere, anywhere, anywhere, vmem, vmem, anywhere, vmem, vmem],
+        in_specs=[vmem, anywhere, anywhere, vmem, vmem, anywhere, vmem, vmem],
         out_specs=[vmem, anywhere, vmem, vmem],
         out_shape=[
             jax.ShapeDtypeStruct((256, width), F32),
@@ -493,7 +785,7 @@
             buffer(8, 256, 256),
             buffer(8, 256, 256),
             buffer(256, 128, kind=F32),
-            pltpu.SemaphoreType.DMA((11,)),
+            pltpu.SemaphoreType.DMA((10,)),
             pltpu.SemaphoreType.DMA((8,)),
             pltpu.SemaphoreType.DMA((SENDS,)),
             pltpu.SemaphoreType.DMA((SENDS,)),
@@ -504,7 +796,7 @@
         cost_estimate=pl.CostEstimate(
             flops=4 * 512 * 1024 * 4096, bytes_accessed=20 * 2**20, transcendentals=0
         ),
-    )(d_queries, mine, theirs, w_all, grad, sums, tokens, inverse, gain)
+    )(d_queries, normed, w_all, grad, sums, tokens, inverse, gain)
 
 
 def shards(
@@ -521,42 +813,20 @@
     counts,
     d_context,
 ):
-    tensor_count = lax.axis_size("tensor")
-    tensor_rank = lax.axis_index("tensor")
-    core = lax.axis_index("seq") % 2
-    tok_rows, width = tokens.shape
-    width_share = width // tensor_count
-    enc_in = swapped(neighbours[0], "section", 0)
-    hidden = tokens.astype(jnp.float32)
-    inverse = lax.rsqrt(jnp.mean(hidden * hidden, axis=-1, keepdims=True) + EPSILON)
-    unit_full = hidden * inverse
-    unit_rows = unit_full.astype(jnp.bfloat16)
-    normed = (unit_full * query_gain).astype(jnp.bfloat16)
-    unit_share = lax.dynamic_slice_in_dim(unit_rows, tensor_rank * width_share, width_share, 1)
-    state_part = jnp.dot(unit_share, state_kv, preferred_element_type=jnp.float32)
-    block_states = lax.psum_scatter(
-        state_part.astype(jnp.bfloat16), "tensor", scatter_dimension=0, tiled=True
-    )
-    encoded_home = encode(enc_in, block_states, enc_gain, enc_query, enc_out)
-    encoded_all = lax.all_gather(encoded_home, "tensor", axis=0, tiled=True)
-    w_full = lax.all_gather(w_query, ("section", "seq"), axis=0, tiled=True)
-    queries = jnp.dot(normed, w_full, preferred_element_type=jnp.float32).astype(jnp.bfloat16)
+    tok_rows = tokens.shape[0]
+    gain = query_gain.reshape(32, 1, 256)
+    queries, w_part, normed, keys, values, inverse = forward(
+        tokens, w_query, gain, state_kv, neighbours.reshape(KEYS, E), enc_gain.reshape(1, E),
+        enc_query, enc_out, w_key, w_value,
+    )
     context, d_queries, grad, sums = attend(
-        counts, queries, encoded_all.reshape(-1, E), w_key, w_value, d_context
-    )
-    chunks = jnp.transpose(normed.reshape(tok_rows, 16, 2, 256), (2, 1, 0, 3))
-    mine = lax.dynamic_index_in_dim(chunks, core, 0, keepdims=False)
-    theirs = swapped(lax.dynamic_index_in_dim(chunks, 1 - core, 0, keepdims=False), "seq", 0)
+        counts, queries, keys.reshape(4 * KEYS, -1), values.reshape(4 * KEYS, -1),
+        w_key, w_value, d_context,
+    )
     d_query_weight, d_hidden, d_encoded, row_dots = backward(
-        d_queries,
-        mine,
-        theirs,
-        w_full.reshape(16, 2, 256, -1),
-        grad,
+        d_queries, normed, w_part, grad,
         jnp.broadcast_to(sums[:, 0][None], (8, tok_rows)),
-        tokens,
-        inverse,
-        query_gain.reshape(32, 1, 256),
+        tokens, inverse, gain,
     )
     return (
         context,

time: 286 us -> 167 us (0.58)
  waiting for transfers between devices: 96.1 us -> 0 us
  Pallas kernels: 105 us -> 155 us
  matrix products: 22.7 us -> 0 us
  local copies, waits for them, and re-layouts: 29.4 us -> 10.5 us
  between operations: 15.7 us -> 0.71 us
  other arithmetic: 11.6 us -> 0 us
  starting transfers between devices: 4.74 us -> 0 us
    all_gather x2 -> x0, waiting for transfers between devices: 75.2 us -> none  [the longest x1 55.8 us: shards(): w_full = lax.all_gather(w_query, ('section', 'seq'), axis=0, tiled=True)]
    pallas_call x1 -> x2, Pallas kernels: 73.3 us -> 143 us  [the longest x1 72.5 us: forward(): pl.pallas_call(forward_kernel, in_specs=[anywhere, anywhere, vmem, anywhe...]
    dot_general x6 -> x0, matrix products: 22.3 us -> none  [the longest x1 11.6 us: shards(): jnp.dot(normed, w_full, preferred_element_type=jnp.float32)]
    pallas_call x1, Pallas kernels: 31.6 us -> 12.3 us  [attend(): pl.pallas_call(attend_kernel, grid=(blocks,), in_specs=[pl.BlockSpec(memo...]
    unnamed x28 -> x17, local copies, waits for them, and re-layouts: 22.3 us -> 7.2 us
    ppermute x2 -> x0, waiting for transfers between devices: 10.2 us -> none  [swapped(): return lax.ppermute(value, axis, pairs)]
    reduce_scatter x1 -> x0, waiting for transfers between devices: 10.2 us -> none  [shards(): lax.psum_scatter(state_part.astype(jnp.bfloat16), 'tensor', scatter_dimen...]
    mul x1 -> x0, other arithmetic: 4.96 us -> none  [shards(): unit_full = hidden * inverse]
  transfers between devices with their start and end apart: 5 -> 0, of which waited for: 4 -> 0; matrix products, arithmetic and copies ran while one was open for 11% -> 0% of each run, Pallas kernels for 11% -> 0%
where the time goes in v2:
time: 167 us
  Pallas kernels  155 us (93%)
  local copies, waits for them, and re-layouts  10.5 us (6%)
    pallas_call x1, Pallas kernels, forward(): pl.pallas_call(forward_kernel, in_specs=[anywhere, anywhere, vmem, anywhe...  72.5 us
    pallas_call x1, Pallas kernels, backward(): pl.pallas_call(backward_kernel, in_specs=[vmem, anywhere, anywhere, vmem,...  70.6 us
    pallas_call x1, Pallas kernels, attend(): pl.pallas_call(attend_kernel, grid=(blocks,), in_specs=[pl.BlockSpec(memo...  12.3 us
    unnamed x17, local copies, waits for them, and re-layouts  7.2 us

profile of v2, /device:TPU:1, one launch (start us, length us, event | category | flops | bytes accessed | tf_op | source)
XLA Modules:
  0.0 166.6 jit_solution(10058222305912574285)
XLA Ops:
  0.6 1.3 reshape.31.egain_ref
  1.9 0.0 copy-start
  1.9 0.0 copy-start.1
  1.9 72.5 %shard_map.155 = (bf16[256,1024]{1,0:T(8,128)(2,1)}, bf16[16,256,1024]{2,1,0:T(8,128)(2,1)}, bf16[16,512,256]{2,1,0:T(8,128)(2,1)}, bf16[4,256,1024]{2,1,0:T(8,1...) custom-call(bf16[256,8192]{1,0:T(8,128)(2,1)} %tokens_ref.3, bf16[256,1024]{1,0:T(8,128)(2,1)} %w_ref.1, ...), custom_call_target="tpu_custom_call" | custom-call | flops 11324620800 | bytes 41943040 | tf_op jit(solution)/shard_map/pallas_call | solution.py:429
  74.4 0.0 copy-done
  74.4 0.0 copy-done.1
  74.4 0.0 copy-start.4
  74.4 1.0 copy-done.4
  75.5 12.3 %shard_map.156 = (bf16[256,1024]{1,0:T(8,128)(2,1)}, bf16[256,1024]{1,0:T(8,128)(2,1)S(1)}, bf16[4,256,896]{2,1,0:T(8,128)(2,1)S(1)}, f32[256,128]{1,0:T(8,128)S(1)}) custom-call(s32[4]{0:T(128)S(1)} %copy-done.1, bf16[256,1024]{1,0:T(8,128)(2,1)S(1)} %copy-done.4, bf16[1024,1024]{1,0:T(8,128)(2,1)} %bitcast.11, bf16[1024,1024]{1,0:T(8,128)(2,1)} %bitcast.12, ...), custom_call_target="tpu_custom_call" | custom-call | flops 4563402752 | bytes 14680064 | tf_op jit(solution)/shard_map/pallas_call | solution.py:76
  87.8 0.0 copy-start.2
  87.8 1.3 copy-done.2
  89.1 0.0 copy-start.3
  89.1 0.8 copy-done.3
  89.9 0.1 slice_reduce_fusion
  90.0 0.6 broadcast_in_dim.8.sums_ref
  90.6 70.6 %shard_map.157 = (f32[256,1024]{1,0:T(8,128)}, bf16[256,2048]{1,0:T(8,128)(2,1)}, bf16[256,896]{1,0:T(8,128)(2,1)}, f32[8,256]{1,0:T(8,128)}) custom-call(bf16[256,1024]{1,0:T(8,128)(2,1)} %copy-done.3, bf16[16,512,256]{2,1,0:T(8,128)(2,1)} %get-tuple-element.24.nrm_ref, bf16[16,256,1024]{2,1,0:T(8,128)(2,1)} %get-tuple-element.25.w_ref, ...), custom_call_target="tpu_custom_call" | custom-call | flops 8589934592 | bytes 20971520 | tf_op jit(solution)/shard_map/pallas_call | solution.py:754
  161.2 0.0 copy-start.5
  161.2 1.3 slice.7
  162.5 0.0 copy-start.6
  162.5 2.4 %copy.20 = bf16[256,2048]{1,0:T(8,128)(2,1)} copy(bf16[256,2048]{1,0:T(8,128)(2,1)} %get-tuple-element.39) | data formatting | bytes 2097152
  164.9 0.0 copy-done.5
  164.9 1.0 copy.21
  165.9 0.0 copy-done.6
  165.9 0.8 copy.22
Async XLA Ops:
  1.9 72.5 %copy-start = (bf16[256,1024]{1,0:T(8,128)(2,1)S(1)}, bf16[256,1024]{1,0:T(8,128)(2,1)}, u32[]{:S(2)}) copy-start(bf16[256,1024]{1,0:T(8,128)(2,1)} %do_ref.1) | copy-start | bytes 1572868
  1.9 72.5 %copy-start.1 = (s32[4]{0:T(128)S(1)}, s32[4]{0:T(128)}, u32[]{:S(2)}) copy-start(s32[4]{0:T(128)} %counts.1) | copy-start | bytes 52
  74.4 1.0 copy-start.4
  87.8 1.3 copy-start.2
  89.1 0.8 copy-start.3
  161.2 3.7 %copy-start.5 = (f32[256,1024]{1,0:T(8,128)S(1)}, f32[256,1024]{1,0:T(8,128)}, u32[]{:S(2)}) copy-start(f32[256,1024]{1,0:T(8,128)} %get-tuple-element.40) | copy-start | bytes 3145732
  162.5 3.3 %copy-start.6 = (bf16[256,896]{1,0:T(8,128)(2,1)S(1)}, bf16[256,896]{1,0:T(8,128)(2,1)}, u32[]{:S(2)}) copy-start(bf16[256,896]{1,0:T(8,128)(2,1)} %get-tuple-element.31) | copy-start | bytes 1376260

commit v3 on v2

--- a/solution.py
+++ b/solution.py
@@ -211,16 +211,14 @@
         block = piece(half, line, 0)
         cross[half, line] = (pass_on(block, dim, 1), pass_on(block, dim, 3))
 
-    def first_round(half):
+    def relays(half):
         dim = dims[half][0]
         near[half][0].wait_recv()
-        relay[half] = [pass_on(piece(half, 3, 0, 0), dim, 1)]
-        across(half, 3)
+        first = pass_on(piece(half, 3, 0, 0), dim, 1)
         near[half][1].wait_recv()
-        relay[half].append(pass_on(piece(half, 1, 0, 1), dim, 3))
-        across(half, 1)
-
-    def second_round(half):
+        relay[half] = (first, pass_on(piece(half, 1, 0, 1), dim, 3))
+
+    def relayed(half):
         relay[half][0].wait_recv()
         relay[half][1].wait_recv()
         across(half, 2)
@@ -262,8 +260,7 @@
         block = piece(half, 0, 0)
         near[half] = (pass_on(block, dims[half][0], 1), pass_on(block, dims[half][0], 3))
     c_near = send(near_ref, enc_in, at.partner())
-    for half in (0, 1):
-        across(half, 0)
+    across(1, 0)
 
     loads[1].wait()
 
@@ -295,8 +292,12 @@
         send(sp.at[far, 0:32], sr1.at[0], at.along("x", 1)),
         send(sp.at[far, 32:64], sr1.at[1], at.along("x", 3)),
     )
-    first_round(0)
-    first_round(1)
+    relays(0)
+    relays(1)
+    across(1, 3)
+    across(1, 1)
+    for line in (0, 3, 1):
+        across(0, line)
 
     @pl.loop(0, 16)
     def _(k):
@@ -317,8 +318,8 @@
         send(sp.at[up], sr2.at[0], at.along("x", 1)),
         send(sp.at[down], sr2.at[1], at.along("x", 3)),
     )
-    second_round(0)
-    second_round(1)
+    relayed(0)
+    crossed(1, 0)
 
     loads[3].wait()
     c_near.wait_recv()
@@ -326,8 +327,6 @@
     mean = jnp.sum(enc_rows * enc_rows, axis=-1, keepdims=True) * (1.0 / E)
     enc_normed = (enc_rows * lax.rsqrt(mean + EPSILON) * egain_ref[...]).astype(BF16)
     eq_s[...] = dot(enc_normed, equery[...]).astype(BF16)
-    for half in (0, 1):
-        crossed(half, 0)
 
     c_s2[0].wait_recv()
     c_s2[1].wait_recv()
@@ -362,6 +361,7 @@
         send(enc.at[at.x], enc.at[at.x], at.along("x", 1)),
         send(enc.at[at.x], enc.at[at.x], at.along("x", 3)),
     )
+    relayed(1)
     loads[5].wait()
     loads[6].wait()
 
@@ -377,11 +377,13 @@
 
     c_nrm.wait_recv()
     write(nrm, nrm_out)
+    crossed(0, 0)
     accumulate([(0, 0), (1, 0), (3, 0), (0, 1), (0, 3)], begin=True)
-    for line in (3, 1):
-        for half in (0, 1):
-            crossed(half, line)
+    crossed(1, 3)
+    crossed(1, 1)
     project(at.x)
+    crossed(0, 3)
+    crossed(0, 1)
     c_e1[0].wait_recv()
     c_e2 = [send(enc.at[down, 0:128], enc.at[down, 0:128], at.along("x", 1))]
     c_e1[1].wait_recv()
@@ -389,8 +391,8 @@
     project(down)
     project(up)
     accumulate([(1, 1), (1, 3), (3, 1), (3, 3)])
-    for half in (0, 1):
-        crossed(half, 2)
+    crossed(1, 2)
+    crossed(0, 2)
     landed(0, 0)
     landed(1, 0)
     accumulate([(2, 0), (0, 2)])
@@ -477,6 +479,7 @@
 
 
 LINES = (2, 1, 3, 0)
+Z_FIRST = 384
 
 
 def backward_kernel(
@@ -537,57 +540,88 @@
             prod[k, rows, :] = dot(dq_t[rows, :], nrm[k]).astype(BF16)
 
     dims = (("z", "y"), ("y", "z"))
-
-    def block(half, line, off, low=0, high=512):
+    spans = ((0, Z_FIRST), (Z_FIRST, 1024))
+    size = (Z_FIRST, 1024 - Z_FIRST)
+
+    def block(half, line, off, part=None):
         dy, dz = (line, off) if half == 0 else (off, line)
-        return prod.at[at.chunk(dy, dz), half * 512 + low : half * 512 + high]
-
-    c1 = {}
+        low, high = spans[half]
+        middle = (low + high) // 2
+        low, high = (low, high) if part is None else ((low, middle), (middle, high))[part]
+        return prod.at[at.chunk(dy, dz), low:high]
+
+    def first_slot(half, line, way):
+        return ra1.at[half, LINES.index(line), way, 0 : size[half] // 2]
+
+    def second_slot(half, line, way):
+        return ra2.at[half, LINES.index(line), way, 0 : size[half]]
+
+    def both(dim, one, other):
+        return send(*one, at.along(dim, 1)), send(*other, at.along(dim, 3))
+
+    c1, c2, d1, d2 = {}, {}, {}, {}
 
     def first_hop(half, line):
-        dim = dims[half][0]
-        slot = LINES.index(line)
-        c1[half, line] = (
-            send(block(half, line, 2, 0, 256), ra1.at[half, slot, 0], at.along(dim, 1)),
-            send(block(half, line, 2, 256, 512), ra1.at[half, slot, 1], at.along(dim, 3)),
-        )
-
-    product(2, 2)
-    first_hop(0, 2)
-    first_hop(1, 2)
-    for line in (1, 3, 0):
-        product(line, 2)
-        first_hop(0, line)
-        product(2, line)
-        first_hop(1, line)
-    for dy in (1, 3, 0):
-        for dz in (1, 3, 0):
-            product(dy, dz)
-
-    c_g1[0].wait_recv()
-    c_g1[1].wait_recv()
-    gs[0, 0:128] = (grad_ref[up, 0:128].astype(F32) + g1[0].astype(F32)).astype(BF16)
-    gs[0, 128:256] = grad_ref[up, 128:256]
-    gs[1, 0:128] = grad_ref[down, 0:128]
-    gs[1, 128:256] = (grad_ref[down, 128:256].astype(F32) + g1[1].astype(F32)).astype(BF16)
-    c_g2 = [
-        send(gs.at[0], g2.at[0], at.along("x", 1)),
-        send(gs.at[1], g2.at[1], at.along("x", 3)),
-    ]
-
-    c2 = {}
+        c1[half, line] = both(
+            dims[half][0],
+            (block(half, line, 2, 0), first_slot(half, line, 0)),
+            (block(half, line, 2, 1), first_slot(half, line, 1)),
+        )
 
     def second_hop(half, line):
-        dim = dims[half][0]
-        slot = LINES.index(line)
         for way, off in ((0, 1), (1, 3)):
             c1[half, line][way].wait_recv()
-            piece = block(half, line, off, 256 * way, 256 * way + 256)
-            added(piece, piece, ra1.at[half, slot, way])
-        c2[half, line] = (
-            send(block(half, line, 1), ra2.at[half, slot, 0], at.along(dim, 1)),
-            send(block(half, line, 3), ra2.at[half, slot, 1], at.along(dim, 3)),
-        )
+            piece = block(half, line, off, way)
+            added(piece, piece, first_slot(half, line, way))
+        c2[half, line] = both(
+            dims[half][0],
+            (block(half, line, 1), second_slot(half, line, 0)),
+            (block(half, line, 3), second_slot(half, line, 1)),
+        )
+
+    def gathered(half, line):
+        for way in (0, 1):
+            c2[half, line][way].wait_recv()
+        piece = block(half, line, 0)
+        total = piece[...].astype(F32) + second_slot(half, line, 0)[...].astype(F32)
+        piece[...] = (total + second_slot(half, line, 1)[...].astype(F32)).astype(BF16)
+
+    def turn_slot(half, way):
+        return rb1.at[half, way, 0 : size[half] // 2]
+
+    def last_slot(half, way):
+        return rb2.at[half, way, 0 : size[half]]
+
+    def turn(half):
+        d1[half] = both(
+            dims[half][1],
+            (block(half, 2, 0, 0), turn_slot(half, 0)),
+            (block(half, 2, 0, 1), turn_slot(half, 1)),
+        )
+
+    def turned(half):
+        for way, off in ((0, 1), (1, 3)):
+            d1[half][way].wait_recv()
+            piece = block(half, off, 0, way)
+            added(piece, piece, turn_slot(half, way))
+        d2[half] = both(
+            dims[half][1],
+            (block(half, 1, 0), last_slot(half, 0)),
+            (block(half, 3, 0), last_slot(half, 1)),
+        )
+
+    def result(half):
+        for way in (0, 1):
+            c2[half, 0][way].wait_recv()
+            d2[half][way].wait_recv()
+        extras = [second_slot(half, 0, 0), second_slot(half, 0, 1)]
+        extras += [last_slot(half, 0), last_slot(half, 1)]
+        for low in range(0, size[half], 128):
+            total = block(half, 0, 0)[low : low + 128].astype(F32)
+            for extra in extras:
+                total = total + extra[low : low + 128].astype(F32)
+            first = spans[half][0] + low
+            dw_ref[:, first : first + 128] = jnp.transpose(total)
 
     def partial(k):
         @pl.loop(0, 2)
@@ -596,32 +630,15 @@
             part[k, rows, :] = dot(dq2[rows, :], wc[k], LAST).astype(BF16)
 
     n1, n2 = [], []
-    loads[1].wait()
-    second_hop(0, 2)
-    second_hop(1, 2)
-    for m in range(4):
+
+    def far_partial(m):
         partial(far * 4 + m)
         n1.append(
-            (
-                send(part.at[far * 4 + m, 0:256], rn1.at[m, 0], at.along("x", 1)),
-                send(part.at[far * 4 + m, 256:512], rn1.at[m, 1], at.along("x", 3)),
-            )
-        )
-        if m > 0:
-            second_hop(0, LINES[m])
-            second_hop(1, LINES[m])
-
-    for copy in c_sums:
-        copy.wait_recv()
-    sums = sums_ref[...] + sums_in[0] + sums_in[1] + sums_in[2]
-    dots_ref[...] = sums * (1.0 / math.sqrt(width))
-    column[...] = jnp.transpose(jnp.broadcast_to(sums[0:1], (128, 256)))
-
-    for m in range(4):
-        partial(up * 4 + m)
-        partial(down * 4 + m)
-        partial(at.x * 4 + m)
-    for m in range(4):
+            both("x", (part.at[far * 4 + m, 0:256], rn1.at[m, 0]),
+                 (part.at[far * 4 + m, 256:512], rn1.at[m, 1]))
+        )
+
+    def near_partial(m):
         n1[m][0].wait_recv()
         piece = part.at[up * 4 + m, 0:256]
         added(piece, piece, rn1.at[m, 0])
@@ -629,24 +646,66 @@
         piece = part.at[down * 4 + m, 256:512]
         added(piece, piece, rn1.at[m, 1])
         n2.append(
-            (
-                send(part.at[up * 4 + m], rn2.at[m, 0], at.along("x", 1)),
-                send(part.at[down * 4 + m], rn2.at[m, 1], at.along("x", 3)),
-            )
-        )
-
+            both("x", (part.at[up * 4 + m], rn2.at[m, 0]), (part.at[down * 4 + m], rn2.at[m, 1]))
+        )
+
+    product(2, 2)
+    first_hop(1, 2)
+    first_hop(0, 2)
+    loads[1].wait()
+    far_partial(0)
+    for m, line in ((1, 1), (2, 3), (3, 0)):
+        product(2, line)
+        first_hop(1, line)
+        product(line, 2)
+        first_hop(0, line)
+        far_partial(m)
+    for dy, dz in ((1, 1), (3, 1), (1, 3), (3, 3)):
+        product(dy, dz)
+
+    c_g1[0].wait_recv()
+    c_g1[1].wait_recv()
+    gs[0, 0:128] = (grad_ref[up, 0:128].astype(F32) + g1[0].astype(F32)).astype(BF16)
+    gs[0, 128:256] = grad_ref[up, 128:256]
+    gs[1, 0:128] = grad_ref[down, 0:128]
+    gs[1, 128:256] = (grad_ref[down, 128:256].astype(F32) + g1[1].astype(F32)).astype(BF16)
+    c_g2 = both("x", (gs.at[0], g2.at[0]), (gs.at[1], g2.at[1]))
+
+    second_hop(1, 2)
+    second_hop(0, 2)
+    for dy, dz in ((1, 0), (3, 0), (0, 1), (0, 3), (0, 0)):
+        product(dy, dz)
+    second_hop(1, 1)
+    second_hop(0, 1)
+    for m in range(4):
+        partial(up * 4 + m)
+        partial(down * 4 + m)
+    second_hop(1, 3)
+    second_hop(0, 3)
+    second_hop(0, 0)
+    for m in range(4):
+        near_partial(m)
+
+    for copy in c_sums:
+        copy.wait_recv()
+    sums = sums_ref[...] + sums_in[0] + sums_in[1] + sums_in[2]
+    dots_ref[...] = sums * (1.0 / math.sqrt(width))
+    column[...] = jnp.transpose(jnp.broadcast_to(sums[0:1], (128, 256)))
+
+    for m in range(4):
+        partial(at.x * 4 + m)
+    gathered(0, 2)
+    turn(0)
     for copy in c_g2:
         copy.wait_recv()
     gfin[...] = (grad_ref[at.x].astype(F32) + g2[0].astype(F32) + g2[1].astype(F32)).astype(BF16)
     c_swap = send(gfin, gin, at.partner())
-
-    def gathered(half, line):
-        for way in (0, 1):
-            c2[half, line][way].wait_recv()
-        slot = LINES.index(line)
-        piece = block(half, line, 0)
-        total = piece[...].astype(F32) + ra2[half, slot, 0].astype(F32)
-        piece[...] = (total + ra2[half, slot, 1].astype(F32)).astype(BF16)
+    gathered(1, 2)
+    turn(1)
+    gathered(0, 1)
+    gathered(0, 3)
+    turned(0)
+    second_hop(1, 0)
 
     for load in loads[2:]:
         load.wait()
@@ -681,56 +740,23 @@
         c_sib.append(send(out_sib.at[m], in_sib.at[m], at.sibling()))
         finish(2 * m + at.core, summed(0))
 
-    d1, d2 = {}, {}
-
-    def turn(half):
-        dim = dims[half][1]
-        d1[half] = (
-            send(block(half, 2, 0, 0, 256), rb1.at[half, 0], at.along(dim, 1)),
-            send(block(half, 2, 0, 256, 512), rb1.at[half, 1], at.along(dim, 3)),
-        )
-
-    def turned(half):
-        dim = dims[half][1]
-        for way, off in ((0, 1), (1, 3)):
-            d1[half][way].wait_recv()
-            piece = block(half, off, 0, 256 * way, 256 * way + 256)
-            added(piece, piece, rb1.at[half, way])
-        d2[half] = (
-            send(block(half, 1, 0), rb2.at[half, 0], at.along(dim, 1)),
-            send(block(half, 3, 0), rb2.at[half, 1], at.along(dim, 3)),
-        )
-
-    def result(half):
-        for way in (0, 1):
-            c2[half, 0][way].wait_recv()
-            d2[half][way].wait_recv()
-        for low in (0, 256):
-            rows = slice(low, low + 256)
-            total = block(half, 0, 0)[rows].astype(F32)
-            for extra in (ra2.at[half, 3, 0], ra2.at[half, 3, 1], rb2.at[half, 0], rb2.at[half, 1]):
-                total = total + extra[rows].astype(F32)
-            first = half * 512 + low
-            dw_ref[:, first : first + 256] = jnp.transpose(total)
-
-    for half in (0, 1):
-        gathered(half, 2)
-        turn(half)
-    normed_sum(0)
-    for half in (0, 1):
-        gathered(half, 1)
-    normed_sum(1)
-    for half in (0, 1):
-        gathered(half, 3)
-    for half in (0, 1):
-        turned(half)
-    normed_sum(2)
-    for half in (0, 1):
-        result(half)
-    normed_sum(3)
-    for m in range(4):
+    def sibling_part(m):
         c_sib[m].wait_recv()
         finish(2 * m + 1 - at.core, in_sib[m].astype(F32))
+
+    normed_sum(0)
+    gathered(1, 1)
+    normed_sum(1)
+    sibling_part(0)
+    gathered(1, 3)
+    turned(1)
+    normed_sum(2)
+    sibling_part(1)
+    normed_sum(3)
+    sibling_part(2)
+    result(0)
+    result(1)
+    sibling_part(3)
     c_swap.wait_recv()
     de_ref[...] = gin[...]
     for copy in send.copies:
@@ -767,10 +793,10 @@
             buffer(16, 512, 256),
             buffer(16, 256, 1024),
             buffer(16, 1024, 256),
-            buffer(2, 4, 2, 256, 256),
-            buffer(2, 4, 2, 512, 256),
-            buffer(2, 2, 256, 256),
-            buffer(2, 2, 512, 256),
+            buffer(2, 4, 2, (1024 - Z_FIRST) // 2, 256),
+            buffer(2, 4, 2, 1024 - Z_FIRST, 256),
+            buffer(2, 2, (1024 - Z_FIRST) // 2, 256),
+            buffer(2, 2, 1024 - Z_FIRST, 256),
             buffer(16, 512, 256),
             buffer(4, 2, 256, 256),
             buffer(4, 2, 512, 256),

time: 167 us -> 152 us (0.910)
  Pallas kernels: 155 us -> 141 us
    pallas_call x1, Pallas kernels: 72.5 us -> 62.9 us  [forward(): pl.pallas_call(forward_kernel, in_specs=[anywhere, anywhere, vmem, anywhe...]
    pallas_call x1, Pallas kernels: 70.6 us -> 65.4 us  [backward(): pl.pallas_call(backward_kernel, in_specs=[vmem, anywhere, anywhere, vmem,...]
where the time goes in v3:
time: 152 us
  Pallas kernels  141 us (93%)
  local copies, waits for them, and re-layouts  10.5 us (7%)
    pallas_call x1, Pallas kernels, backward(): pl.pallas_call(backward_kernel, in_specs=[vmem, anywhere, anywhere, vmem,...  65.4 us
    pallas_call x1, Pallas kernels, forward(): pl.pallas_call(forward_kernel, in_specs=[anywhere, anywhere, vmem, anywhe...  62.9 us
    pallas_call x1, Pallas kernels, attend(): pl.pallas_call(attend_kernel, grid=(blocks,), in_specs=[pl.BlockSpec(memo...  12.3 us
    unnamed x17, local copies, waits for them, and re-layouts  7.2 us

profile of v3, /device:TPU:1, one launch (start us, length us, event | category | flops | bytes accessed | tf_op | source)
XLA Modules:
  0.0 151.9 jit_solution(7549920056660273574)
XLA Ops:
  0.6 1.3 reshape.31.egain_ref
  1.9 0.0 copy-start
  1.9 0.0 copy-start.1
  1.9 62.9 %shard_map.155 = (bf16[256,1024]{1,0:T(8,128)(2,1)}, bf16[16,256,1024]{2,1,0:T(8,128)(2,1)}, bf16[16,512,256]{2,1,0:T(8,128)(2,1)}, bf16[4,256,1024]{2,1,0:T(8,1...) custom-call(bf16[256,8192]{1,0:T(8,128)(2,1)} %tokens_ref.3, bf16[256,1024]{1,0:T(8,128)(2,1)} %w_ref.1, ...), custom_call_target="tpu_custom_call" | custom-call | flops 11324620800 | bytes 41943040 | tf_op jit(solution)/shard_map/pallas_call | solution.py:431
  64.8 0.0 copy-done
  64.8 0.0 copy-done.1
  64.8 0.0 copy-start.4
  64.8 1.0 copy-done.4
  65.8 12.3 %shard_map.156 = (bf16[256,1024]{1,0:T(8,128)(2,1)}, bf16[256,1024]{1,0:T(8,128)(2,1)S(1)}, bf16[4,256,896]{2,1,0:T(8,128)(2,1)S(1)}, f32[256,128]{1,0:T(8,128)S(1)}) custom-call(s32[4]{0:T(128)S(1)} %copy-done.1, bf16[256,1024]{1,0:T(8,128)(2,1)S(1)} %copy-done.4, bf16[1024,1024]{1,0:T(8,128)(2,1)} %bitcast.11, bf16[1024,1024]{1,0:T(8,128)(2,1)} %bitcast.12, ...), custom_call_target="tpu_custom_call" | custom-call | flops 4563402752 | bytes 14680064 | tf_op jit(solution)/shard_map/pallas_call | solution.py:76
  78.2 0.0 copy-start.2
  78.2 1.3 copy-done.2
  79.4 0.0 copy-start.3
  79.4 0.8 copy-done.3
  80.2 0.1 slice_reduce_fusion
  80.3 0.6 broadcast_in_dim.8.sums_ref
  80.9 65.4 %shard_map.157 = (f32[256,1024]{1,0:T(8,128)}, bf16[256,2048]{1,0:T(8,128)(2,1)}, bf16[256,896]{1,0:T(8,128)(2,1)}, f32[8,256]{1,0:T(8,128)}) custom-call(bf16[256,1024]{1,0:T(8,128)(2,1)} %copy-done.3, bf16[16,512,256]{2,1,0:T(8,128)(2,1)} %get-tuple-element.24.nrm_ref, bf16[16,256,1024]{2,1,0:T(8,128)(2,1)} %get-tuple-element.25.w_ref, ...), custom_call_target="tpu_custom_call" | custom-call | flops 8589934592 | bytes 20971520 | tf_op jit(solution)/shard_map/pallas_call | solution.py:780
  146.4 0.0 copy-start.5
  146.4 1.3 slice.7
  147.8 0.0 copy-start.6
  147.8 2.4 %copy.20 = bf16[256,2048]{1,0:T(8,128)(2,1)} copy(bf16[256,2048]{1,0:T(8,128)(2,1)} %get-tuple-element.39) | data formatting | bytes 2097152
  150.1 0.0 copy-done.5
  150.1 1.0 copy.21
  151.1 0.0 copy-done.6
  151.1 0.8 copy.22
Async XLA Ops:
  1.9 62.9 %copy-start = (bf16[256,1024]{1,0:T(8,128)(2,1)S(1)}, bf16[256,1024]{1,0:T(8,128)(2,1)}, u32[]{:S(2)}) copy-start(bf16[256,1024]{1,0:T(8,128)(2,1)} %do_ref.1) | copy-start | bytes 1572868
  1.9 62.9 %copy-start.1 = (s32[4]{0:T(128)S(1)}, s32[4]{0:T(128)}, u32[]{:S(2)}) copy-start(s32[4]{0:T(128)} %counts.1) | copy-start | bytes 52
  64.8 1.0 copy-start.4
  78.2 1.3 copy-start.2
  79.4 0.8 copy-start.3
  146.4 3.7 %copy-start.5 = (f32[256,1024]{1,0:T(8,128)S(1)}, f32[256,1024]{1,0:T(8,128)}, u32[]{:S(2)}) copy-start(f32[256,1024]{1,0:T(8,128)} %get-tuple-element.40) | copy-start | bytes 3145732
  147.8 3.3 %copy-start.6 = (bf16[256,896]{1,0:T(8,128)(2,1)S(1)}, bf16[256,896]{1,0:T(8,128)(2,1)}, u32[]{:S(2)}) copy-start(bf16[256,896]{1,0:T(8,128)(2,1)} %get-tuple-element.31) | copy-start | bytes 1376260

commit v4 on v3

--- a/solution.py
+++ b/solution.py
@@ -27,84 +27,6 @@
 
 def dot(a, b, dims=(((1,), (0,)), ((), ()))):
     return lax.dot_general(a, b, dims, preferred_element_type=F32)
-
-
-def attend_kernel(
-    counts, q_ref, k_ref, v_ref, wk_ref, wv_ref, do_ref,
-    ctx_ref, dq_ref, grad_ref, sums_ref,
-    score_s, dprob_s, weight_s, dscore_s, dk_s, dv_s,
-):
-    count = counts[pl.program_id(0)]
-    heads = q_ref.shape[1] // HD
-    valid = lax.broadcasted_iota(jnp.int32, (BLOCK, KEYS), 1) < count * RLEN
-    empty = jnp.where(count == 0, 1.0, 0.0).astype(F32)
-    scale = 1.0 / math.sqrt(HD)
-    spans = [slice(head * HD, (head + 1) * HD) for head in range(heads)]
-    for head, cols in enumerate(spans):
-        score_s[head] = dot(q_ref[:, cols], k_ref[:, cols], LAST) * scale
-        dprob_s[head] = dot(do_ref[:, cols], v_ref[:, cols], LAST)
-    for head in range(heads):
-        scores = score_s[head]
-        top = jnp.max(jnp.where(valid, scores, NEG_LARGE), axis=-1, keepdims=True)
-        weights = jnp.where(valid, jnp.exp(scores - top), 0.0)
-        probs = weights / (jnp.sum(weights, axis=-1, keepdims=True) + empty)
-        weight_s[head] = probs.astype(BF16)
-        d_probs = dprob_s[head]
-        inner = jnp.sum(probs * d_probs, axis=-1, keepdims=True)
-        dscore_s[head] = (probs * (d_probs - inner) * scale).astype(BF16)
-    total = jnp.zeros((BLOCK, HD), F32)
-    for head, cols in enumerate(spans):
-        ctx_ref[:, cols] = dot(weight_s[head], v_ref[:, cols]).astype(BF16)
-        dq = dot(dscore_s[head], k_ref[:, cols])
-        dq_ref[:, cols] = dq.astype(BF16)
-        total = total + dq * q_ref[:, cols].astype(F32)
-        dv_s[:, cols] = dot(weight_s[head], do_ref[:, cols], FIRST).astype(BF16)
-        dk_s[:, cols] = dot(dscore_s[head], q_ref[:, cols], FIRST).astype(BF16)
-    grad = dot(dk_s[...], wk_ref[...], LAST) + dot(dv_s[...], wv_ref[...], LAST)
-    grad_ref[0] = grad.astype(BF16)
-    sums_ref[...] = jnp.broadcast_to(jnp.sum(total, axis=-1, keepdims=True), (BLOCK, HD))
-
-
-def attend(counts, queries, keys, values, w_key, w_value, d_context):
-    blocks = counts.shape[0]
-    rows, width = queries.shape
-    heads = width // HD
-    row_block = pl.BlockSpec((BLOCK, width), lambda b: (b, 0))
-    key_block = pl.BlockSpec((KEYS, width), lambda b: (b, 0))
-    weight = pl.BlockSpec((E, width), lambda b: (0, 0))
-    flops = 2 * (4 * rows * 2 * E * width + 6 * rows * KEYS * width)
-    return pl.pallas_call(
-        attend_kernel,
-        grid=(blocks,),
-        in_specs=[
-            pl.BlockSpec(memory_space=pltpu.SMEM),
-            row_block,
-            key_block,
-            key_block,
-            weight,
-            weight,
-            row_block,
-        ],
-        out_specs=[
-            row_block,
-            row_block,
-            pl.BlockSpec((1, KEYS, E), lambda b: (b, 0, 0)),
-            pl.BlockSpec((BLOCK, HD), lambda b: (b, 0)),
-        ],
-        out_shape=[
-            jax.ShapeDtypeStruct((rows, width), BF16),
-            jax.ShapeDtypeStruct((rows, width), BF16),
-            jax.ShapeDtypeStruct((blocks, KEYS, E), BF16),
-            jax.ShapeDtypeStruct((rows, HD), F32),
-        ],
-        scratch_shapes=[pltpu.VMEM((heads, BLOCK, KEYS), F32)] * 2
-        + [pltpu.VMEM((heads, BLOCK, KEYS), BF16)] * 2
-        + [pltpu.VMEM((KEYS, width), BF16)] * 2,
-        compiler_params=pltpu.CompilerParams(vmem_limit_bytes=50 * 2**20),
-        cost_estimate=pl.CostEstimate(
-            flops=flops, bytes_accessed=14 * 2**20, transcendentals=rows * 8 * KEYS
-        ),
-    )(counts, queries, keys, values, w_key, w_value, d_context)
 
 
 class Place:
@@ -479,149 +401,184 @@
 
 
 LINES = (2, 1, 3, 0)
-Z_FIRST = 384
+GROUPS = ((0, 256, 96), (256, 1024, 288))
+LOADS = 16
+
+
+def halves(group):
+    first, stop, z_first = GROUPS[group]
+    return z_first, stop - first - z_first
 
 
 def backward_kernel(
-    dq_ref, nrm_ref, w_ref, grad_ref, sums_ref, tokens_ref, inverse_ref, gain_ref,
-    dw_ref, dh_ref, de_ref, dots_ref,
-    dq2, dq_t, nrm, wc, prod, ra1, ra2, rb1, rb2, part, rn1, rn2, out_sib, in_sib,
-    g1, gs, g2, gfin, gin, sums_in, tok, dh_s, column,
-    load_sem, dh_sem, send_sem, recv_sem,
+    counts, q_ref, k_ref, v_ref, do_ref, wk_ref, wv_ref, nrm_ref, w_ref, tokens_ref,
+    inverse_ref, gain_ref,
+    ctx_ref, dw_ref, dh_ref, de_ref, dots_ref,
+    qs, dos, ks, vs, wk, wv, ctx, score_s, dprob_s, weight_s, dscore_s, sum_s,
+    dq2, dq_t, nrm, wc, prod, dw_t, part, rn1, rn2, out_sib, in_sib,
+    grads, g1, gs, g2, gfin, gin, sums, sums_in, tok, column,
+    ra1_00, ra1_01, ra1_10, ra1_11, ra2_00, ra2_01, ra2_10, ra2_11,
+    rb1_00, rb1_01, rb1_10, rb1_11, rb2_00, rb2_01, rb2_10, rb2_11,
+    load_sem, out_sem, send_sem, recv_sem,
 ):
     at = Place()
     width = tokens_ref.shape[1]
     share = width // 4
-    loads = [
-        pltpu.make_async_copy(nrm_ref, nrm, load_sem.at[0]),
-        pltpu.make_async_copy(w_ref, wc, load_sem.at[1]),
+    ra1 = ((ra1_00, ra1_01), (ra1_10, ra1_11))
+    ra2 = ((ra2_00, ra2_01), (ra2_10, ra2_11))
+    rb1 = ((rb1_00, rb1_01), (rb1_10, rb1_11))
+    rb2 = ((rb2_00, rb2_01), (rb2_10, rb2_11))
+    pairs = [
+        (q_ref, qs), (do_ref, dos), (k_ref, ks), (v_ref, vs), (wk_ref, wk), (wv_ref, wv),
+        (nrm_ref, nrm), (w_ref, wc),
     ]
     for i in range(8):
         first = pl.multiple_of(at.x * share + i * 256, 256)
-        loads.append(
-            pltpu.make_async_copy(tokens_ref.at[:, pl.ds(first, 256)], tok.at[i], load_sem.at[2 + i])
-        )
+        pairs.append((tokens_ref.at[:, pl.ds(first, 256)], tok.at[i]))
+    loads = [pltpu.make_async_copy(src, dst, load_sem.at[i]) for i, (src, dst) in enumerate(pairs)]
     for load in loads:
         load.start()
-    greet(
-        [at.along("x", 1), at.along("x", 2), at.along("x", 3), at.along("y", 1), at.along("y", 3),
-         at.along("z", 1), at.along("z", 3), at.sibling()]
-    )
+    barrier = pltpu.get_barrier_semaphore()
+    friends = [at.along("x", 1), at.along("x", 2), at.along("x", 3), at.along("y", 1),
+               at.along("y", 3), at.along("z", 1), at.along("z", 3), at.sibling()]
+    for friend in friends:
+        pl.semaphore_signal(barrier, inc=1, device_id=friend, device_id_type=MESH)
 
     send = Sender(send_sem, recv_sem)
+    far, up, down = (at.x + 2) % 4, (at.x + 1) % 4, (at.x + 3) % 4
+    scale = 1.0 / math.sqrt(HD)
 
     def added(dst, first, second):
         dst[...] = (first[...].astype(F32) + second[...].astype(F32)).astype(BF16)
 
-    c_dq = send(dq_ref, dq2.at[256:512], at.sibling())
-    far = (at.x + 2) % 4
-    up, down = (at.x + 1) % 4, (at.x + 3) % 4
-    c_g1 = [
-        send(grad_ref.at[far, 0:128], g1.at[0], at.along("x", 1)),
-        send(grad_ref.at[far, 128:256], g1.at[1], at.along("x", 3)),
-    ]
-    c_sums = [send(sums_ref, sums_in.at[i], at.along("x", i + 1)) for i in range(3)]
-    dq2[0:256] = dq_ref[...]
-    for j in range(4):
-        dq_t[256 * j : 256 * j + 256, 0:256] = jnp.transpose(dq_ref[:, 256 * j : 256 * j + 256])
-    c_dq.wait_recv()
-    for j in range(4):
-        dq_t[256 * j : 256 * j + 256, 256:512] = jnp.transpose(
-            dq2[256:512, 256 * j : 256 * j + 256]
-        )
-    loads[0].wait()
-
-    def product(dy, dz):
+    def both(dim, one, other):
+        return send(*one, at.along(dim, 1)), send(*other, at.along(dim, 3))
+
+    def attention(b, group):
+        first, stop, _ = GROUPS[group]
+        spans = [slice(low, low + HD) for low in range(first, stop, HD)]
+        rows = pl.ds(pl.multiple_of(b * BLOCK, BLOCK), BLOCK)
+        count = counts[b]
+        valid = lax.broadcasted_iota(jnp.int32, (BLOCK, KEYS), 1) < count * RLEN
+        empty = jnp.where(count == 0, 1.0, 0.0).astype(F32)
+        for i, cols in enumerate(spans):
+            score_s[i] = dot(qs[rows, cols], ks[b, :, cols], LAST) * scale
+            dprob_s[i] = dot(dos[rows, cols], vs[b, :, cols], LAST)
+        for i in range(len(spans)):
+            scores = score_s[i]
+            top = jnp.max(jnp.where(valid, scores, NEG_LARGE), axis=-1, keepdims=True)
+            weights = jnp.where(valid, jnp.exp(scores - top), 0.0)
+            probs = weights / (jnp.sum(weights, axis=-1, keepdims=True) + empty)
+            weight_s[i] = probs.astype(BF16)
+            d_probs = dprob_s[i]
+            inner = jnp.sum(probs * d_probs, axis=-1, keepdims=True)
+            dscore_s[i] = (probs * (d_probs - inner) * scale).astype(BF16)
+        total = jnp.zeros((BLOCK, HD), F32)
+        for i, cols in enumerate(spans):
+            ctx[rows, cols] = dot(weight_s[i], vs[b, :, cols]).astype(BF16)
+            dq = dot(dscore_s[i], ks[b, :, cols])
+            dq2[rows, cols] = dq.astype(BF16)
+            total = total + dq * qs[rows, cols].astype(F32)
+            vs[b, :, cols] = dot(weight_s[i], dos[rows, cols], FIRST).astype(BF16)
+            ks[b, :, cols] = dot(dscore_s[i], qs[rows, cols], FIRST).astype(BF16)
+        sum_s[rows, :] = total if group == 0 else sum_s[rows, :] + total
+
+    def encoded_grad(b):
+        grad = dot(ks[b], wk[...], LAST) + dot(vs[b], wv[...], LAST)
+        grads[b] = grad.astype(BF16)
+
+    def share_dq(group):
+        first, stop, _ = GROUPS[group]
+        return send(dq2.at[0:256, first:stop], dq2.at[256:512, first:stop], at.sibling())
+
+    def transposed(group, rows):
+        first, stop, _ = GROUPS[group]
+        for low in range(first, stop, 256):
+            dq_t[low : low + 256, rows] = jnp.transpose(dq2[rows, low : low + 256])
+
+    def product(group, dy, dz):
         k = at.chunk(dy, dz)
-
-        @pl.loop(0, 4)
+        first, stop, _ = GROUPS[group]
+
+        @pl.loop(0, (stop - first) // 256)
         def _(i):
-            rows = pl.ds(pl.multiple_of(i * 256, 256), 256)
+            rows = pl.ds(pl.multiple_of(first + i * 256, 256), 256)
             prod[k, rows, :] = dot(dq_t[rows, :], nrm[k]).astype(BF16)
 
     dims = (("z", "y"), ("y", "z"))
-    spans = ((0, Z_FIRST), (Z_FIRST, 1024))
-    size = (Z_FIRST, 1024 - Z_FIRST)
-
-    def block(half, line, off, part=None):
+
+    def block(group, half, line, off, part=None):
         dy, dz = (line, off) if half == 0 else (off, line)
-        low, high = spans[half]
+        first, stop, z_first = GROUPS[group]
+        low, high = ((first, first + z_first), (first + z_first, stop))[half]
         middle = (low + high) // 2
         low, high = (low, high) if part is None else ((low, middle), (middle, high))[part]
         return prod.at[at.chunk(dy, dz), low:high]
 
-    def first_slot(half, line, way):
-        return ra1.at[half, LINES.index(line), way, 0 : size[half] // 2]
-
-    def second_slot(half, line, way):
-        return ra2.at[half, LINES.index(line), way, 0 : size[half]]
-
-    def both(dim, one, other):
-        return send(*one, at.along(dim, 1)), send(*other, at.along(dim, 3))
-
     c1, c2, d1, d2 = {}, {}, {}, {}
 
-    def first_hop(half, line):
-        c1[half, line] = both(
+    def first_hop(group, half, line):
+        slot = ra1[group][half].at[LINES.index(line)]
+        c1[group, half, line] = both(
             dims[half][0],
-            (block(half, line, 2, 0), first_slot(half, line, 0)),
-            (block(half, line, 2, 1), first_slot(half, line, 1)),
+            (block(group, half, line, 2, 0), slot.at[0]),
+            (block(group, half, line, 2, 1), slot.at[1]),
         )
 
-    def second_hop(half, line):
+    def second_hop(group, half, line):
         for way, off in ((0, 1), (1, 3)):
-            c1[half, line][way].wait_recv()
-            piece = block(half, line, off, way)
-            added(piece, piece, first_slot(half, line, way))
-        c2[half, line] = both(
+            c1[group, half, line][way].wait_recv()
+            piece = block(group, half, line, off, way)
+            added(piece, piece, ra1[group][half].at[LINES.index(line), way])
+        slot = ra2[group][half].at[LINES.index(line)]
+        c2[group, half, line] = both(
             dims[half][0],
-            (block(half, line, 1), second_slot(half, line, 0)),
-            (block(half, line, 3), second_slot(half, line, 1)),
+            (block(group, half, line, 1), slot.at[0]),
+            (block(group, half, line, 3), slot.at[1]),
         )
 
-    def gathered(half, line):
+    def gathered(group, half, line):
         for way in (0, 1):
-            c2[half, line][way].wait_recv()
-        piece = block(half, line, 0)
-        total = piece[...].astype(F32) + second_slot(half, line, 0)[...].astype(F32)
-        piece[...] = (total + second_slot(half, line, 1)[...].astype(F32)).astype(BF16)
-
-    def turn_slot(half, way):
-        return rb1.at[half, way, 0 : size[half] // 2]
-
-    def last_slot(half, way):
-        return rb2.at[half, way, 0 : size[half]]
-
-    def turn(half):
-        d1[half] = both(
+            c2[group, half, line][way].wait_recv()
+        slot = ra2[group][half].at[LINES.index(line)]
+        piece = block(group, half, line, 0)
+        total = piece[...].astype(F32) + slot[0].astype(F32) + slot[1].astype(F32)
+        piece[...] = total.astype(BF16)
+
+    def turn(group, half):
+        d1[group, half] = both(
             dims[half][1],
-            (block(half, 2, 0, 0), turn_slot(half, 0)),
-            (block(half, 2, 0, 1), turn_slot(half, 1)),
+            (block(group, half, 2, 0, 0), rb1[group][half].at[0]),
+            (block(group, half, 2, 0, 1), rb1[group][half].at[1]),
         )
 
-    def turned(half):
+    def turned(group, half):
         for way, off in ((0, 1), (1, 3)):
-            d1[half][way].wait_recv()
-            piece = block(half, off, 0, way)
-            added(piece, piece, turn_slot(half, way))
-        d2[half] = both(
+            d1[group, half][way].wait_recv()
+            piece = block(group, half, off, 0, way)
+            added(piece, piece, rb1[group][half].at[way])
+        d2[group, half] = both(
             dims[half][1],
-            (block(half, 1, 0), last_slot(half, 0)),
-            (block(half, 3, 0), last_slot(half, 1)),
+            (block(group, half, 1, 0), rb2[group][half].at[0]),
+            (block(group, half, 3, 0), rb2[group][half].at[1]),
         )
 
-    def result(half):
-        for way in (0, 1):
-            c2[half, 0][way].wait_recv()
-            d2[half][way].wait_recv()
-        extras = [second_slot(half, 0, 0), second_slot(half, 0, 1)]
-        extras += [last_slot(half, 0), last_slot(half, 1)]
-        for low in range(0, size[half], 128):
-            total = block(half, 0, 0)[low : low + 128].astype(F32)
-            for extra in extras:
-                total = total + extra[low : low + 128].astype(F32)
-            first = spans[half][0] + low
-            dw_ref[:, first : first + 128] = jnp.transpose(total)
+    def result(group):
+        first, stop, _ = GROUPS[group]
+        sizes = halves(group)
+        for half in (0, 1):
+            for way in (0, 1):
+                c2[group, half, 0][way].wait_recv()
+                d2[group, half][way].wait_recv()
+            own = block(group, half, 0, 0)
+            slot = ra2[group][half].at[LINES.index(0)]
+            total = own[...].astype(F32) + slot[0].astype(F32) + slot[1].astype(F32)
+            low = half * sizes[0]
+            dw_t[low : low + sizes[half]] = (
+                total + rb2[group][half][0].astype(F32) + rb2[group][half][1].astype(F32)
+            )
+        for low in range(0, stop - first, 128):
+            dw_ref[:, first + low : first + low + 128] = jnp.transpose(dw_t[low : low + 128])
 
     def partial(k):
         @pl.loop(0, 2)
@@ -649,81 +606,21 @@
             both("x", (part.at[up * 4 + m], rn2.at[m, 0]), (part.at[down * 4 + m], rn2.at[m, 1]))
         )
 
-    product(2, 2)
-    first_hop(1, 2)
-    first_hop(0, 2)
-    loads[1].wait()
-    far_partial(0)
-    for m, line in ((1, 1), (2, 3), (3, 0)):
-        product(2, line)
-        first_hop(1, line)
-        product(line, 2)
-        first_hop(0, line)
-        far_partial(m)
-    for dy, dz in ((1, 1), (3, 1), (1, 3), (3, 3)):
-        product(dy, dz)
-
-    c_g1[0].wait_recv()
-    c_g1[1].wait_recv()
-    gs[0, 0:128] = (grad_ref[up, 0:128].astype(F32) + g1[0].astype(F32)).astype(BF16)
-    gs[0, 128:256] = grad_ref[up, 128:256]
-    gs[1, 0:128] = grad_ref[down, 0:128]
-    gs[1, 128:256] = (grad_ref[down, 128:256].astype(F32) + g1[1].astype(F32)).astype(BF16)
-    c_g2 = both("x", (gs.at[0], g2.at[0]), (gs.at[1], g2.at[1]))
-
-    second_hop(1, 2)
-    second_hop(0, 2)
-    for dy, dz in ((1, 0), (3, 0), (0, 1), (0, 3), (0, 0)):
-        product(dy, dz)
-    second_hop(1, 1)
-    second_hop(0, 1)
-    for m in range(4):
-        partial(up * 4 + m)
-        partial(down * 4 + m)
-    second_hop(1, 3)
-    second_hop(0, 3)
-    second_hop(0, 0)
-    for m in range(4):
-        near_partial(m)
-
-    for copy in c_sums:
-        copy.wait_recv()
-    sums = sums_ref[...] + sums_in[0] + sums_in[1] + sums_in[2]
-    dots_ref[...] = sums * (1.0 / math.sqrt(width))
-    column[...] = jnp.transpose(jnp.broadcast_to(sums[0:1], (128, 256)))
-
-    for m in range(4):
-        partial(at.x * 4 + m)
-    gathered(0, 2)
-    turn(0)
-    for copy in c_g2:
-        copy.wait_recv()
-    gfin[...] = (grad_ref[at.x].astype(F32) + g2[0].astype(F32) + g2[1].astype(F32)).astype(BF16)
-    c_swap = send(gfin, gin, at.partner())
-    gathered(1, 2)
-    turn(1)
-    gathered(0, 1)
-    gathered(0, 3)
-    turned(0)
-    second_hop(1, 0)
-
-    for load in loads[2:]:
-        load.wait()
-    stores = []
+    outs = []
+
+    def write(src, dst):
+        copy = pltpu.make_async_copy(src, dst, out_sem.at[len(outs)])
+        copy.start()
+        outs.append(copy)
 
     def finish(i, d_normed):
         inverse = wide(inverse_ref[...])
         unit = tok[i].astype(F32) * inverse
-        rows = wide(column[...])
-        grads = d_normed * gain_ref[at.x * 8 + i]
-        result = inverse * (grads - unit * (rows * (1.0 / width)))
-        dh_s[i] = result.astype(BF16)
+        parts = d_normed * gain_ref[at.x * 8 + i]
+        result = inverse * (parts - unit * (wide(column[...]) * (1.0 / width)))
+        tok[i] = result.astype(BF16)
         first = pl.multiple_of(i * 256, 256)
-        store = pltpu.make_async_copy(
-            dh_s.at[i], dh_ref.at[:, pl.ds(first, 256)], dh_sem.at[len(stores)]
-        )
-        store.start()
-        stores.append(store)
+        write(tok.at[i], dh_ref.at[:, pl.ds(first, 256)])
 
     c_sib = []
 
@@ -744,32 +641,152 @@
         c_sib[m].wait_recv()
         finish(2 * m + 1 - at.core, in_sib[m].astype(F32))
 
+    for load in loads[:4]:
+        load.wait()
+
+    @pl.loop(0, 4)
+    def _(b):
+        attention(b, 0)
+
+    pl.semaphore_wait(barrier, len(friends))
+    c_dq = [share_dq(0)]
+    own, other = slice(0, 256), slice(256, 512)
+    transposed(0, own)
+    for load in loads[4:8]:
+        load.wait()
+    attention(far, 1)
+    encoded_grad(far)
+    c_g1 = both("x", (grads.at[far, 0:128], g1.at[0]), (grads.at[far, 128:256], g1.at[1]))
+    c_dq[0].wait_recv()
+    transposed(0, other)
+    product(0, 2, 2)
+    first_hop(0, 1, 2)
+    first_hop(0, 0, 2)
+    for line in (1, 3, 0):
+        product(0, 2, line)
+        first_hop(0, 1, line)
+        product(0, line, 2)
+        first_hop(0, 0, line)
+    attention(up, 1)
+    attention(down, 1)
+    for dy in (1, 3, 0):
+        for dz in (1, 3, 0):
+            product(0, dy, dz)
+    second_hop(0, 1, 2)
+    second_hop(0, 0, 2)
+    attention(at.x, 1)
+    c_dq.append(share_dq(1))
+    write(ctx, ctx_ref)
+    second_hop(0, 1, 1)
+    second_hop(0, 0, 1)
+    second_hop(0, 1, 3)
+    second_hop(0, 0, 3)
+    lanes = jnp.sum(jnp.transpose(sum_s[...]), axis=0, keepdims=True)
+    sums[...] = jnp.broadcast_to(lanes, (8, 256))
+    c_sums = [send(sums, sums_in.at[i], at.along("x", i + 1)) for i in range(3)]
+    transposed(1, own)
+    c_dq[1].wait_recv()
+    transposed(1, other)
+    product(1, 2, 2)
+    first_hop(1, 1, 2)
+    first_hop(1, 0, 2)
+    for line in (1, 3, 0):
+        product(1, 2, line)
+        first_hop(1, 1, line)
+        product(1, line, 2)
+        first_hop(1, 0, line)
+
+    encoded_grad(up)
+    encoded_grad(down)
+    c_g1[0].wait_recv()
+    c_g1[1].wait_recv()
+    gs[0, 0:128] = (grads[up, 0:128].astype(F32) + g1[0].astype(F32)).astype(BF16)
+    gs[0, 128:256] = grads[up, 128:256]
+    gs[1, 0:128] = grads[down, 0:128]
+    gs[1, 128:256] = (grads[down, 128:256].astype(F32) + g1[1].astype(F32)).astype(BF16)
+    c_g2 = both("x", (gs.at[0], g2.at[0]), (gs.at[1], g2.at[1]))
+    for m in range(4):
+        far_partial(m)
+
+    gathered(0, 0, 2)
+    turn(0, 0)
+    for dy in (1, 3, 0):
+        for dz in (1, 3, 0):
+            product(1, dy, dz)
+    second_hop(1, 1, 2)
+    second_hop(1, 0, 2)
+    gathered(0, 1, 2)
+    turn(0, 1)
+    for m in range(4):
+        partial(up * 4 + m)
+        partial(down * 4 + m)
+    second_hop(1, 1, 1)
+    second_hop(1, 0, 1)
+    second_hop(1, 1, 3)
+    second_hop(1, 0, 3)
+    encoded_grad(at.x)
+    for copy in c_g2:
+        copy.wait_recv()
+    gfin[...] = (grads[at.x].astype(F32) + g2[0].astype(F32) + g2[1].astype(F32)).astype(BF16)
+    c_swap = send(gfin, gin, at.partner())
+    gathered(0, 0, 1)
+    gathered(0, 0, 3)
+    turned(0, 0)
+    gathered(0, 1, 1)
+    gathered(0, 1, 3)
+    turned(0, 1)
+    for m in range(4):
+        near_partial(m)
+    second_hop(0, 0, 0)
+    second_hop(1, 0, 0)
+
+    for copy in c_sums:
+        copy.wait_recv()
+    whole = sums[...] + sums_in[0] + sums_in[1] + sums_in[2]
+    dots_ref[...] = whole[0:1] * (1.0 / math.sqrt(width))
+    column[...] = jnp.transpose(jnp.broadcast_to(whole[0:1], (128, 256)))
+    for load in loads[8:]:
+        load.wait()
+    for m in range(4):
+        partial(at.x * 4 + m)
+
+    gathered(1, 0, 2)
+    turn(1, 0)
+    gathered(1, 1, 2)
+    turn(1, 1)
+    second_hop(0, 1, 0)
     normed_sum(0)
-    gathered(1, 1)
+    gathered(1, 0, 1)
+    gathered(1, 0, 3)
+    turned(1, 0)
+    second_hop(1, 1, 0)
     normed_sum(1)
     sibling_part(0)
-    gathered(1, 3)
-    turned(1)
+    gathered(1, 1, 1)
+    gathered(1, 1, 3)
+    turned(1, 1)
     normed_sum(2)
     sibling_part(1)
+    result(0)
     normed_sum(3)
     sibling_part(2)
-    result(0)
     result(1)
     sibling_part(3)
     c_swap.wait_recv()
-    de_ref[...] = gin[...]
+    write(gin, de_ref)
     for copy in send.copies:
         copy.wait_send()
-    for store in stores:
-        store.wait()
-
-
-SENDS = 1 + 2 + 3 + 16 + 2 + 16 + 8 + 8 + 1 + 4 + 8
-
-
-def backward(d_queries, normed, w_all, grad, sums, tokens, inverse, gain):
-    rows, width = d_queries.shape
+    for copy in outs:
+        copy.wait()
+
+
+BACKWARD_SENDS = 2 + 2 + 2 + 8 + 8 + 3 + 1 + 4 + 2 * 40
+
+
+def backward(
+    counts, queries, keys, values, d_context, w_key, w_value, normed, w_all, tokens, inverse, gain
+):
+    rows, width = queries.shape
     full = tokens.shape[1]
     vmem = pl.BlockSpec(memory_space=pltpu.VMEM)
     anywhere = pl.BlockSpec(memory_space=pl.ANY)
@@ -777,52 +794,70 @@
     def buffer(*shape, kind=BF16):
         return pltpu.VMEM(shape, kind)
 
+    sizes = [size for group in range(2) for size in halves(group)]
     return pl.pallas_call(
         backward_kernel,
-        in_specs=[vmem, anywhere, anywhere, vmem, vmem, anywhere, vmem, vmem],
-        out_specs=[vmem, anywhere, vmem, vmem],
+        in_specs=[pl.BlockSpec(memory_space=pltpu.SMEM)] + [anywhere] * 9 + [vmem, vmem],
+        out_specs=[anywhere, vmem, anywhere, anywhere, vmem],
         out_shape=[
+            jax.ShapeDtypeStruct((rows, width), BF16),
             jax.ShapeDtypeStruct((256, width), F32),
             jax.ShapeDtypeStruct((rows, full // 4), BF16),
             jax.ShapeDtypeStruct((KEYS, E), BF16),
-            jax.ShapeDtypeStruct((8, rows), F32),
+            jax.ShapeDtypeStruct((1, rows), F32),
         ],
         scratch_shapes=[
+            buffer(rows, width),
+            buffer(rows, width),
+            buffer(4, KEYS, width),
+            buffer(4, KEYS, width),
+            buffer(E, width),
+            buffer(E, width),
+            buffer(rows, width),
+            buffer(6, BLOCK, KEYS, kind=F32),
+            buffer(6, BLOCK, KEYS, kind=F32),
+            buffer(6, BLOCK, KEYS),
+            buffer(6, BLOCK, KEYS),
+            buffer(rows, HD, kind=F32),
             buffer(512, 1024),
             buffer(1024, 512),
             buffer(16, 512, 256),
             buffer(16, 256, 1024),
             buffer(16, 1024, 256),
-            buffer(2, 4, 2, (1024 - Z_FIRST) // 2, 256),
-            buffer(2, 4, 2, 1024 - Z_FIRST, 256),
-            buffer(2, 2, (1024 - Z_FIRST) // 2, 256),
-            buffer(2, 2, 1024 - Z_FIRST, 256),
+            buffer(768, 256, kind=F32),
             buffer(16, 512, 256),
             buffer(4, 2, 256, 256),
             buffer(4, 2, 512, 256),
             buffer(4, 256, 256),
             buffer(4, 256, 256),
+            buffer(4, KEYS, E),
             buffer(2, 128, E),
             buffer(2, 256, E),
             buffer(2, 256, E),
             buffer(256, E),
             buffer(256, E),
+            buffer(8, 256, kind=F32),
             buffer(3, 8, 256, kind=F32),
             buffer(8, 256, 256),
-            buffer(8, 256, 256),
             buffer(256, 128, kind=F32),
+        ]
+        + [buffer(4, 2, size // 2, 256) for size in sizes]
+        + [buffer(4, 2, size, 256) for size in sizes]
+        + [buffer(2, size // 2, 256) for size in sizes]
+        + [buffer(2, size, 256) for size in sizes]
+        + [
+            pltpu.SemaphoreType.DMA((LOADS,)),
             pltpu.SemaphoreType.DMA((10,)),
-            pltpu.SemaphoreType.DMA((8,)),
-            pltpu.SemaphoreType.DMA((SENDS,)),
-            pltpu.SemaphoreType.DMA((SENDS,)),
+            pltpu.SemaphoreType.DMA((BACKWARD_SENDS,)),
+            pltpu.SemaphoreType.DMA((BACKWARD_SENDS,)),
         ],
         compiler_params=pltpu.CompilerParams(
-            collective_id=1, has_side_effects=True, vmem_limit_bytes=60 * 2**20
+            collective_id=1, has_side_effects=True, vmem_limit_bytes=62 * 2**20
         ),
         cost_estimate=pl.CostEstimate(
-            flops=4 * 512 * 1024 * 4096, bytes_accessed=20 * 2**20, transcendentals=0
+            flops=12 * 2**30, bytes_accessed=30 * 2**20, transcendentals=0
         ),
-    )(d_queries, normed, w_all, grad, sums, tokens, inverse, gain)
+    )(counts, queries, keys, values, d_context, w_key, w_value, normed, w_all, tokens, inverse, gain)
 
 
 def shards(
@@ -839,20 +874,14 @@
     counts,
     d_context,
 ):
-    tok_rows = tokens.shape[0]
     gain = query_gain.reshape(32, 1, 256)
     queries, w_part, normed, keys, values, inverse = forward(
         tokens, w_query, gain, state_kv, neighbours.reshape(KEYS, E), enc_gain.reshape(1, E),
         enc_query, enc_out, w_key, w_value,
     )
-    context, d_queries, grad, sums = attend(
-        counts, queries, keys.reshape(4 * KEYS, -1), values.reshape(4 * KEYS, -1),
-        w_key, w_value, d_context,
-    )
-    d_query_weight, d_hidden, d_encoded, row_dots = backward(
-        d_queries, normed, w_part, grad,
-        jnp.broadcast_to(sums[:, 0][None], (8, tok_rows)),
-        tokens, inverse, gain,
+    context, d_query_weight, d_hidden, d_encoded, row_dots = backward(
+        counts, queries, keys, values, d_context, w_key, w_value, normed, w_part, tokens, inverse,
+        gain,
     )
     return (
         context,

time: 152 us -> 150 us (0.987)
  local copies, waits for them, and re-layouts: 10.5 us -> 7.89 us
    unnamed x17 -> x11, local copies, waits for them, and re-layouts: 7.2 us -> 6.63 us
    pallas_call x2 -> x1, Pallas kernels: 77.8 us -> 77.9 us  [backward(): pl.pallas_call(backward_kernel, in_specs=[pl.BlockSpec(memory_space=pltpu...]
where the time goes in v4:
time: 150 us; the launch traced here: 149 us
  Pallas kernels  141 us (94%)
  local copies, waits for them, and re-layouts  7.89 us (5%)
    pallas_call x1, Pallas kernels, backward(): pl.pallas_call(backward_kernel, in_specs=[pl.BlockSpec(memory_space=pltpu...  77.9 us
    pallas_call x1, Pallas kernels, forward(): pl.pallas_call(forward_kernel, in_specs=[anywhere, anywhere, vmem, anywhe...  62.8 us
    unnamed x11, local copies, waits for them, and re-layouts  6.63 us

profile of v4, /device:TPU:1, one launch (start us, length us, event | category | flops | bytes accessed | tf_op | source)
XLA Modules:
  0.0 149.2 jit_solution(9477902440577492060)
XLA Ops:
  0.6 1.3 reshape.24.egain_ref
  1.9 62.8 %shard_map.155 = (bf16[256,1024]{1,0:T(8,128)(2,1)}, bf16[16,256,1024]{2,1,0:T(8,128)(2,1)}, bf16[16,512,256]{2,1,0:T(8,128)(2,1)}, bf16[4,256,1024]{2,1,0:T(8,1...) custom-call(bf16[256,8192]{1,0:T(8,128)(2,1)} %tokens_ref.3, bf16[256,1024]{1,0:T(8,128)(2,1)} %w_ref.1, ...), custom_call_target="tpu_custom_call" | custom-call | flops 11324620800 | bytes 41943040 | tf_op jit(solution)/shard_map/pallas_call | solution.py:353
  64.7 77.9 %shard_map.156 = (bf16[256,1024]{1,0:T(8,128)(2,1)}, f32[256,1024]{1,0:T(8,128)}, bf16[256,2048]{1,0:T(8,128)(2,1)}, bf16[256,896]{1,0:T(8,128)(2,1)}, f32[1,256]{1,0:T(1,128)}) custom-call(s32[4]{0:T(128)} %counts.1, bf16[256,1024]{1,0:T(8,128)(2,1)} %get-tuple-element.16.q_ref, bf16[4,256,1024]{2,1,0:T(8,128)(2,1)} %get-tuple-element.17.k_ref, ...), custom_call_target="tpu_custom_call" | custom-call | flops 12884901888 | bytes 31457280 | tf_op jit(solution)/shard_map/pallas_call | solution.py:798
  142.6 0.0 copy-start
  142.6 2.0 %copy.22 = bf16[256,1024]{1,0:T(8,128)(2,1)} copy(bf16[256,1024]{1,0:T(8,128)(2,1)} %get-tuple-element.32) | data formatting | bytes 1048576
  144.6 0.0 copy-start.1
  144.6 0.0 copy-start.2
  144.6 2.4 %copy.23 = bf16[256,2048]{1,0:T(8,128)(2,1)} copy(bf16[256,2048]{1,0:T(8,128)(2,1)} %get-tuple-element.33) | data formatting | bytes 2097152
  146.9 0.0 copy-done
  146.9 1.0 copy.24
  147.9 0.0 copy-done.1
  147.9 0.8 copy.25
  148.7 0.0 copy-done.2
  148.7 0.6 copy.26
Async XLA Ops:
  142.6 4.3 %copy-start = (f32[256,1024]{1,0:T(8,128)S(1)}, f32[256,1024]{1,0:T(8,128)}, u32[]{:S(2)}) copy-start(f32[256,1024]{1,0:T(8,128)} %get-tuple-element.34) | copy-start | bytes 3145732
  144.6 3.3 %copy-start.1 = (bf16[256,896]{1,0:T(8,128)(2,1)S(1)}, bf16[256,896]{1,0:T(8,128)(2,1)}, u32[]{:S(2)}) copy-start(bf16[256,896]{1,0:T(8,128)(2,1)} %get-tuple-element.25) | copy-start | bytes 1376260
  144.6 4.1 %copy-start.2 = (f32[1,256]{1,0:T(1,128)S(1)}, f32[1,256]{1,0:T(1,128)}, u32[]{:S(2)}) copy-start(f32[1,256]{1,0:T(1,128)} %get-tuple-element.26) | copy-start | bytes 3076

commit v5 on v4

--- a/solution.py
+++ b/solution.py
@@ -499,11 +499,7 @@
     def product(group, dy, dz):
         k = at.chunk(dy, dz)
         first, stop, _ = GROUPS[group]
-
-        @pl.loop(0, (stop - first) // 256)
-        def _(i):
-            rows = pl.ds(pl.multiple_of(first + i * 256, 256), 256)
-            prod[k, rows, :] = dot(dq_t[rows, :], nrm[k]).astype(BF16)
+        prod[k, first:stop] = dot(dq_t[first:stop], nrm[k]).astype(BF16)
 
     dims = (("z", "y"), ("y", "z"))
 
@@ -581,10 +577,7 @@
             dw_ref[:, first + low : first + low + 128] = jnp.transpose(dw_t[low : low + 128])
 
     def partial(k):
-        @pl.loop(0, 2)
-        def _(i):
-            rows = pl.ds(pl.multiple_of(i * 256, 256), 256)
-            part[k, rows, :] = dot(dq2[rows, :], wc[k], LAST).astype(BF16)
+        part[k] = dot(dq2[...], wc[k], LAST).astype(BF16)
 
     n1, n2 = [], []
 
@@ -668,19 +661,31 @@
         product(0, line, 2)
         first_hop(0, 0, line)
     attention(up, 1)
-    attention(down, 1)
-    for dy in (1, 3, 0):
-        for dz in (1, 3, 0):
-            product(0, dy, dz)
     second_hop(0, 1, 2)
     second_hop(0, 0, 2)
+    corners = ((1, 1), (3, 1), (1, 3), (3, 3))
+    rest = ((1, 0), (3, 0), (0, 1), (0, 3), (0, 0))
+    for dy, dz in corners:
+        product(0, dy, dz)
+    for line in (1, 3):
+        second_hop(0, 1, line)
+        second_hop(0, 0, line)
+    attention(down, 1)
+    encoded_grad(up)
+    encoded_grad(down)
+    c_g1[0].wait_recv()
+    c_g1[1].wait_recv()
+    gs[0, 0:128] = (grads[up, 0:128].astype(F32) + g1[0].astype(F32)).astype(BF16)
+    gs[0, 128:256] = grads[up, 128:256]
+    gs[1, 0:128] = grads[down, 0:128]
+    gs[1, 128:256] = (grads[down, 128:256].astype(F32) + g1[1].astype(F32)).astype(BF16)
+    c_g2 = both("x", (gs.at[0], g2.at[0]), (gs.at[1], g2.at[1]))
     attention(at.x, 1)
     c_dq.append(share_dq(1))
     write(ctx, ctx_ref)
-    second_hop(0, 1, 1)
-    second_hop(0, 0, 1)
-    second_hop(0, 1, 3)
-    second_hop(0, 0, 3)
+    for half in (0, 1):
+        gathered(0, half, 2)
+        turn(0, half)
     lanes = jnp.sum(jnp.transpose(sum_s[...]), axis=0, keepdims=True)
     sums[...] = jnp.broadcast_to(lanes, (8, 256))
     c_sums = [send(sums, sums_in.at[i], at.along("x", i + 1)) for i in range(3)]
@@ -695,50 +700,43 @@
         first_hop(1, 1, line)
         product(1, line, 2)
         first_hop(1, 0, line)
-
-    encoded_grad(up)
-    encoded_grad(down)
-    c_g1[0].wait_recv()
-    c_g1[1].wait_recv()
-    gs[0, 0:128] = (grads[up, 0:128].astype(F32) + g1[0].astype(F32)).astype(BF16)
-    gs[0, 128:256] = grads[up, 128:256]
-    gs[1, 0:128] = grads[down, 0:128]
-    gs[1, 128:256] = (grads[down, 128:256].astype(F32) + g1[1].astype(F32)).astype(BF16)
-    c_g2 = both("x", (gs.at[0], g2.at[0]), (gs.at[1], g2.at[1]))
+    for dy, dz in rest:
+        product(0, dy, dz)
+    for half in (0, 1):
+        gathered(0, half, 1)
+        gathered(0, half, 3)
+        turned(0, half)
+    second_hop(1, 0, 2)
     for m in range(4):
         far_partial(m)
-
-    gathered(0, 0, 2)
-    turn(0, 0)
-    for dy in (1, 3, 0):
-        for dz in (1, 3, 0):
-            product(1, dy, dz)
     second_hop(1, 1, 2)
-    second_hop(1, 0, 2)
-    gathered(0, 1, 2)
-    turn(0, 1)
+    for dy, dz in corners:
+        product(1, dy, dz)
+    for line in (1, 3):
+        second_hop(1, 0, line)
+        second_hop(1, 1, line)
     for m in range(4):
         partial(up * 4 + m)
         partial(down * 4 + m)
-    second_hop(1, 1, 1)
-    second_hop(1, 0, 1)
-    second_hop(1, 1, 3)
-    second_hop(1, 0, 3)
+        near_partial(m)
+    for dy, dz in rest:
+        product(1, dy, dz)
+    second_hop(0, 0, 0)
+    second_hop(1, 0, 0)
+    gathered(1, 0, 2)
+    turn(1, 0)
     encoded_grad(at.x)
     for copy in c_g2:
         copy.wait_recv()
     gfin[...] = (grads[at.x].astype(F32) + g2[0].astype(F32) + g2[1].astype(F32)).astype(BF16)
+    gathered(1, 1, 2)
+    turn(1, 1)
     c_swap = send(gfin, gin, at.partner())
-    gathered(0, 0, 1)
-    gathered(0, 0, 3)
-    turned(0, 0)
-    gathered(0, 1, 1)
-    gathered(0, 1, 3)
-    turned(0, 1)
-    for m in range(4):
-        near_partial(m)
-    second_hop(0, 0, 0)
-    second_hop(1, 0, 0)
+    second_hop(0, 1, 0)
+    gathered(1, 0, 1)
+    gathered(1, 0, 3)
+    turned(1, 0)
+    second_hop(1, 1, 0)
 
     for copy in c_sums:
         copy.wait_recv()
@@ -749,17 +747,7 @@
         load.wait()
     for m in range(4):
         partial(at.x * 4 + m)
-
-    gathered(1, 0, 2)
-    turn(1, 0)
-    gathered(1, 1, 2)
-    turn(1, 1)
-    second_hop(0, 1, 0)
     normed_sum(0)
-    gathered(1, 0, 1)
-    gathered(1, 0, 3)
-    turned(1, 0)
-    second_hop(1, 1, 0)
     normed_sum(1)
     sibling_part(0)
     gathered(1, 1, 1)
@@ -770,8 +758,8 @@
     result(0)
     normed_sum(3)
     sibling_part(2)
+    sibling_part(3)
     result(1)
-    sibling_part(3)
     c_swap.wait_recv()
     write(gin, de_ref)
     for copy in send.copies:

time: 150 us -> 144 us (0.960)
  Pallas kernels: 141 us -> 135 us
    pallas_call x1, Pallas kernels: 77.9 us -> 71.9 us  [backward(): pl.pallas_call(backward_kernel, in_specs=[pl.BlockSpec(memory_space=pltpu...]
where the time goes in v5:
time: 144 us; the launch traced here: 143 us
  Pallas kernels  135 us (94%)
  local copies, waits for them, and re-layouts  7.89 us (5%)
    pallas_call x1, Pallas kernels, backward(): pl.pallas_call(backward_kernel, in_specs=[pl.BlockSpec(memory_space=pltpu...  71.9 us
    pallas_call x1, Pallas kernels, forward(): pl.pallas_call(forward_kernel, in_specs=[anywhere, anywhere, vmem, anywhe...  62.8 us
    unnamed x11, local copies, waits for them, and re-layouts  6.63 us

profile of v5, /device:TPU:1, one launch (start us, length us, event | category | flops | bytes accessed | tf_op | source)
XLA Modules:
  0.0 143.2 jit_solution(2530499088398536824)
XLA Ops:
  0.6 1.3 reshape.24.egain_ref
  1.9 62.8 %shard_map.155 = (bf16[256,1024]{1,0:T(8,128)(2,1)}, bf16[16,256,1024]{2,1,0:T(8,128)(2,1)}, bf16[16,512,256]{2,1,0:T(8,128)(2,1)}, bf16[4,256,1024]{2,1,0:T(8,1...) custom-call(bf16[256,8192]{1,0:T(8,128)(2,1)} %tokens_ref.3, bf16[256,1024]{1,0:T(8,128)(2,1)} %w_ref.1, ...), custom_call_target="tpu_custom_call" | custom-call | flops 11324620800 | bytes 41943040 | tf_op jit(solution)/shard_map/pallas_call | solution.py:353
  64.7 71.9 %shard_map.156 = (bf16[256,1024]{1,0:T(8,128)(2,1)}, f32[256,1024]{1,0:T(8,128)}, bf16[256,2048]{1,0:T(8,128)(2,1)}, bf16[256,896]{1,0:T(8,128)(2,1)}, f32[1,256]{1,0:T(1,128)}) custom-call(s32[4]{0:T(128)} %counts.1, bf16[256,1024]{1,0:T(8,128)(2,1)} %get-tuple-element.16.q_ref, bf16[4,256,1024]{2,1,0:T(8,128)(2,1)} %get-tuple-element.17.k_ref, ...), custom_call_target="tpu_custom_call" | custom-call | flops 12884901888 | bytes 31457280 | tf_op jit(solution)/shard_map/pallas_call | solution.py:786
  136.6 0.0 copy-start
  136.6 2.0 %copy.22 = bf16[256,1024]{1,0:T(8,128)(2,1)} copy(bf16[256,1024]{1,0:T(8,128)(2,1)} %get-tuple-element.32) | data formatting | bytes 1048576
  138.6 0.0 copy-start.1
  138.6 0.0 copy-start.2
  138.6 2.4 %copy.23 = bf16[256,2048]{1,0:T(8,128)(2,1)} copy(bf16[256,2048]{1,0:T(8,128)(2,1)} %get-tuple-element.33) | data formatting | bytes 2097152
  140.9 0.0 copy-done
  140.9 1.0 copy.24
  141.9 0.0 copy-done.1
  141.9 0.8 copy.25
  142.7 0.0 copy-done.2
  142.7 0.6 copy.26
Async XLA Ops:
  136.6 4.3 %copy-start = (f32[256,1024]{1,0:T(8,128)S(1)}, f32[256,1024]{1,0:T(8,128)}, u32[]{:S(2)}) copy-start(f32[256,1024]{1,0:T(8,128)} %get-tuple-element.34) | copy-start | bytes 3145732
  138.6 3.3 %copy-start.1 = (bf16[256,896]{1,0:T(8,128)(2,1)S(1)}, bf16[256,896]{1,0:T(8,128)(2,1)}, u32[]{:S(2)}) copy-start(bf16[256,896]{1,0:T(8,128)(2,1)} %get-tuple-element.25) | copy-start | bytes 1376260
  138.6 4.1 %copy-start.2 = (f32[1,256]{1,0:T(1,128)S(1)}, f32[1,256]{1,0:T(1,128)}, u32[]{:S(2)}) copy-start(f32[1,256]{1,0:T(1,128)} %get-tuple-element.26) | copy-start | bytes 3076

commit v6 on v5

--- a/solution.py
+++ b/solution.py
@@ -247,7 +247,7 @@
     c_near.wait_recv()
     enc_rows = enc_in[...].astype(F32)
     mean = jnp.sum(enc_rows * enc_rows, axis=-1, keepdims=True) * (1.0 / E)
-    enc_normed = (enc_rows * lax.rsqrt(mean + EPSILON) * egain_ref[...]).astype(BF16)
+    enc_normed = (enc_rows * lax.rsqrt(mean + EPSILON) * egain_ref[...].reshape(1, E)).astype(BF16)
     eq_s[...] = dot(enc_normed, equery[...]).astype(BF16)
 
     c_s2[0].wait_recv()
@@ -436,7 +436,7 @@
         first = pl.multiple_of(at.x * share + i * 256, 256)
         pairs.append((tokens_ref.at[:, pl.ds(first, 256)], tok.at[i]))
     loads = [pltpu.make_async_copy(src, dst, load_sem.at[i]) for i, (src, dst) in enumerate(pairs)]
-    for load in loads:
+    for load in loads[:4]:
         load.start()
     barrier = pltpu.get_barrier_semaphore()
     friends = [at.along("x", 1), at.along("x", 2), at.along("x", 3), at.along("y", 1),
@@ -636,6 +636,8 @@
 
     for load in loads[:4]:
         load.wait()
+    for load in loads[4:]:
+        load.start()
 
     @pl.loop(0, 4)
     def _(b):
@@ -848,6 +850,36 @@
     )(counts, queries, keys, values, d_context, w_key, w_value, normed, w_all, tokens, inverse, gain)
 
 
+def results_kernel(*refs):
+    count = (len(refs) - 1) // 2
+    sem = refs[-1]
+    copies = []
+    for source, target in zip(refs[:count], refs[count : 2 * count]):
+        pieces = min(4, source.shape[0])
+        rows = source.shape[0] // pieces
+        for i in range(pieces):
+            piece = pl.ds(i * rows, rows)
+            copies.append(
+                pltpu.make_async_copy(source.at[piece], target.at[piece], sem.at[len(copies)])
+            )
+    for copy in copies:
+        copy.start()
+    for copy in copies:
+        copy.wait()
+
+
+def results(*arrays):
+    anywhere = pl.BlockSpec(memory_space=pl.ANY)
+    return pl.pallas_call(
+        results_kernel,
+        in_specs=[anywhere] * len(arrays),
+        out_specs=[anywhere] * len(arrays),
+        out_shape=[jax.ShapeDtypeStruct(array.shape, array.dtype) for array in arrays],
+        scratch_shapes=[pltpu.SemaphoreType.DMA((4 * len(arrays),))],
+        compiler_params=pltpu.CompilerParams(vmem_limit_bytes=62 * 2**20),
+    )(*arrays)
+
+
 def shards(
     tokens,
     w_query,
@@ -864,12 +896,15 @@
 ):
     gain = query_gain.reshape(32, 1, 256)
     queries, w_part, normed, keys, values, inverse = forward(
-        tokens, w_query, gain, state_kv, neighbours.reshape(KEYS, E), enc_gain.reshape(1, E),
+        tokens, w_query, gain, state_kv, neighbours.reshape(KEYS, E), enc_gain,
         enc_query, enc_out, w_key, w_value,
     )
     context, d_query_weight, d_hidden, d_encoded, row_dots = backward(
         counts, queries, keys, values, d_context, w_key, w_value, normed, w_part, tokens, inverse,
         gain,
+    )
+    context, d_query_weight, d_hidden, d_encoded, row_dots = results(
+        context, d_query_weight, d_hidden, d_encoded, row_dots
     )
     return (
         context,

time: 144 us -> 231 us (1.60)
  Pallas kernels: 135 us -> 230 us
  local copies, waits for them, and re-layouts: 7.89 us -> 0 us
    pallas_call x0 -> x1, Pallas kernels: none -> 94.6 us  [results(): pl.pallas_call(results_kernel, in_specs=[anywhere] * len(arrays), out_spe...]
    unnamed x11 -> x0, local copies, waits for them, and re-layouts: 6.63 us -> none
where the time goes in v6:
time: 231 us
  Pallas kernels  230 us (100%)
    pallas_call x1, Pallas kernels, results(): pl.pallas_call(results_kernel, in_specs=[anywhere] * len(arrays), out_spe...  94.6 us
    pallas_call x1, Pallas kernels, backward(): pl.pallas_call(backward_kernel, in_specs=[pl.BlockSpec(memory_space=pltpu...  72.9 us
    pallas_call x1, Pallas kernels, forward(): pl.pallas_call(forward_kernel, in_specs=[anywhere, anywhere, vmem, anywhe...  62.9 us

profile of v6, /device:TPU:1, one launch (start us, length us, event | category | flops | bytes accessed | tf_op | source)
XLA Modules:
  0.0 231.3 jit_solution(7894230838713053944)
XLA Ops:
  0.6 62.9 %shard_map.155 = (bf16[256,1024]{1,0:T(8,128)(2,1)}, bf16[16,256,1024]{2,1,0:T(8,128)(2,1)}, bf16[16,512,256]{2,1,0:T(8,128)(2,1)}, bf16[4,256,1024]{2,1,0:T(8,1...) custom-call(bf16[256,8192]{1,0:T(8,128)(2,1)} %tokens_ref.3, bf16[256,1024]{1,0:T(8,128)(2,1)} %w_ref.1, ...), custom_call_target="tpu_custom_call" | custom-call | flops 11324620800 | bytes 41943040 | tf_op jit(solution)/shard_map/pallas_call | solution.py:353
  63.5 72.9 %shard_map.156 = (bf16[256,1024]{1,0:T(8,128)(2,1)}, f32[256,1024]{1,0:T(8,128)}, bf16[256,2048]{1,0:T(8,128)(2,1)}, bf16[256,896]{1,0:T(8,128)(2,1)}, f32[1,256]{1,0:T(1,128)}) custom-call(s32[4]{0:T(128)} %counts.1, bf16[256,1024]{1,0:T(8,128)(2,1)} %get-tuple-element.21.q_ref, bf16[4,256,1024]{2,1,0:T(8,128)(2,1)} %get-tuple-element.22.k_ref, ...), custom_call_target="tpu_custom_call" | custom-call | flops 12884901888 | bytes 31457280 | tf_op jit(solution)/shard_map/pallas_call | solution.py:788
  136.5 94.6 %shard_map.157 = (bf16[256,1024]{1,0:T(8,128)(2,1)}, f32[256,1024]{1,0:T(8,128)}, bf16[256,2048]{1,0:T(8,128)(2,1)}, bf16[256,896]{1,0:T(8,128)(2,1)}, f32[1,256]{1,0:T(1,128)}) custom-call(bf16[256,1024]{1,0:T(8,128)(2,1)} %get-tuple-element.27.refs_0_, f32[256,1024]{1,0:T(8,128)} %get-tuple-element.28.refs_1_, ...), custom_call_target="tpu_custom_call" | custom-call | tf_op jit(solution)/shard_map/pallas_call | solution.py:873

commit v7 on v5

--- a/solution.py
+++ b/solution.py
@@ -247,7 +247,7 @@
     c_near.wait_recv()
     enc_rows = enc_in[...].astype(F32)
     mean = jnp.sum(enc_rows * enc_rows, axis=-1, keepdims=True) * (1.0 / E)
-    enc_normed = (enc_rows * lax.rsqrt(mean + EPSILON) * egain_ref[...]).astype(BF16)
+    enc_normed = (enc_rows * lax.rsqrt(mean + EPSILON) * egain_ref[...].reshape(1, E)).astype(BF16)
     eq_s[...] = dot(enc_normed, equery[...]).astype(BF16)
 
     c_s2[0].wait_recv()
@@ -401,7 +401,7 @@
 
 
 LINES = (2, 1, 3, 0)
-GROUPS = ((0, 256, 96), (256, 1024, 288))
+GROUPS = ((0, 384, 160), (384, 1024, 224))
 LOADS = 16
 
 
@@ -436,7 +436,7 @@
         first = pl.multiple_of(at.x * share + i * 256, 256)
         pairs.append((tokens_ref.at[:, pl.ds(first, 256)], tok.at[i]))
     loads = [pltpu.make_async_copy(src, dst, load_sem.at[i]) for i, (src, dst) in enumerate(pairs)]
-    for load in loads:
+    for load in loads[:4]:
         load.start()
     barrier = pltpu.get_barrier_semaphore()
     friends = [at.along("x", 1), at.along("x", 2), at.along("x", 3), at.along("y", 1),
@@ -493,8 +493,8 @@
 
     def transposed(group, rows):
         first, stop, _ = GROUPS[group]
-        for low in range(first, stop, 256):
-            dq_t[low : low + 256, rows] = jnp.transpose(dq2[rows, low : low + 256])
+        for low in range(first, stop, 128):
+            dq_t[low : low + 128, rows] = jnp.transpose(dq2[rows, low : low + 128])
 
     def product(group, dy, dz):
         k = at.chunk(dy, dz)
@@ -636,6 +636,8 @@
 
     for load in loads[:4]:
         load.wait()
+    for load in loads[4:]:
+        load.start()
 
     @pl.loop(0, 4)
     def _(b):
@@ -661,15 +663,6 @@
         product(0, line, 2)
         first_hop(0, 0, line)
     attention(up, 1)
-    second_hop(0, 1, 2)
-    second_hop(0, 0, 2)
-    corners = ((1, 1), (3, 1), (1, 3), (3, 3))
-    rest = ((1, 0), (3, 0), (0, 1), (0, 3), (0, 0))
-    for dy, dz in corners:
-        product(0, dy, dz)
-    for line in (1, 3):
-        second_hop(0, 1, line)
-        second_hop(0, 0, line)
     attention(down, 1)
     encoded_grad(up)
     encoded_grad(down)
@@ -680,9 +673,18 @@
     gs[1, 0:128] = grads[down, 0:128]
     gs[1, 128:256] = (grads[down, 128:256].astype(F32) + g1[1].astype(F32)).astype(BF16)
     c_g2 = both("x", (gs.at[0], g2.at[0]), (gs.at[1], g2.at[1]))
+    second_hop(0, 1, 2)
+    second_hop(0, 0, 2)
     attention(at.x, 1)
     c_dq.append(share_dq(1))
     write(ctx, ctx_ref)
+    corners = ((1, 1), (3, 1), (1, 3), (3, 3))
+    rest = ((1, 0), (3, 0), (0, 1), (0, 3), (0, 0))
+    for dy, dz in corners:
+        product(0, dy, dz)
+    for line in (1, 3):
+        second_hop(0, 1, line)
+        second_hop(0, 0, line)
     for half in (0, 1):
         gathered(0, half, 2)
         turn(0, half)
@@ -695,11 +697,13 @@
     product(1, 2, 2)
     first_hop(1, 1, 2)
     first_hop(1, 0, 2)
-    for line in (1, 3, 0):
+    for m, line in enumerate((1, 3, 0)):
         product(1, 2, line)
         first_hop(1, 1, line)
         product(1, line, 2)
         first_hop(1, 0, line)
+        far_partial(m)
+    far_partial(3)
     for dy, dz in rest:
         product(0, dy, dz)
     for half in (0, 1):
@@ -707,14 +711,17 @@
         gathered(0, half, 3)
         turned(0, half)
     second_hop(1, 0, 2)
-    for m in range(4):
-        far_partial(m)
     second_hop(1, 1, 2)
     for dy, dz in corners:
         product(1, dy, dz)
     for line in (1, 3):
         second_hop(1, 0, line)
         second_hop(1, 1, line)
+    encoded_grad(at.x)
+    for copy in c_g2:
+        copy.wait_recv()
+    gfin[...] = (grads[at.x].astype(F32) + g2[0].astype(F32) + g2[1].astype(F32)).astype(BF16)
+    c_swap = send(gfin, gin, at.partner())
     for m in range(4):
         partial(up * 4 + m)
         partial(down * 4 + m)
@@ -725,13 +732,8 @@
     second_hop(1, 0, 0)
     gathered(1, 0, 2)
     turn(1, 0)
-    encoded_grad(at.x)
-    for copy in c_g2:
-        copy.wait_recv()
-    gfin[...] = (grads[at.x].astype(F32) + g2[0].astype(F32) + g2[1].astype(F32)).astype(BF16)
     gathered(1, 1, 2)
     turn(1, 1)
-    c_swap = send(gfin, gin, at.partner())
     second_hop(0, 1, 0)
     gathered(1, 0, 1)
     gathered(1, 0, 3)
@@ -848,6 +850,28 @@
     )(counts, queries, keys, values, d_context, w_key, w_value, normed, w_all, tokens, inverse, gain)
 
 
+def results_kernel(*refs):
+    count = len(refs) // 2
+    for source, target in zip(refs[:count], refs[count:]):
+        target[...] = source[...]
+
+
+def results(*arrays):
+    steps = 4
+    specs = [
+        pl.BlockSpec((array.shape[0] // steps, array.shape[1]), lambda i: (i, 0))
+        for array in arrays
+    ]
+    return pl.pallas_call(
+        results_kernel,
+        grid=(steps,),
+        in_specs=specs,
+        out_specs=specs,
+        out_shape=[jax.ShapeDtypeStruct(array.shape, array.dtype) for array in arrays],
+        compiler_params=pltpu.CompilerParams(vmem_limit_bytes=62 * 2**20),
+    )(*arrays)
+
+
 def shards(
     tokens,
     w_query,
@@ -864,12 +888,15 @@
 ):
     gain = query_gain.reshape(32, 1, 256)
     queries, w_part, normed, keys, values, inverse = forward(
-        tokens, w_query, gain, state_kv, neighbours.reshape(KEYS, E), enc_gain.reshape(1, E),
+        tokens, w_query, gain, state_kv, neighbours.reshape(KEYS, E), enc_gain,
         enc_query, enc_out, w_key, w_value,
     )
     context, d_query_weight, d_hidden, d_encoded, row_dots = backward(
         counts, queries, keys, values, d_context, w_key, w_value, normed, w_part, tokens, inverse,
         gain,
+    )
+    context, d_query_weight, d_hidden, d_encoded = results(
+        context, d_query_weight, d_hidden, d_encoded
     )
     return (
         context,

time: 144 us -> 140 us (0.972)
  local copies, waits for them, and re-layouts: 7.89 us -> 0.57 us
  Pallas kernels: 135 us -> 139 us
    unnamed x11 -> x3, local copies, waits for them, and re-layouts: 6.63 us -> 0.57 us
    pallas_call x0 -> x1, Pallas kernels: none -> 4.11 us  [results(): pl.pallas_call(results_kernel, grid=(steps,), in_specs=specs, out_specs=s...]
where the time goes in v7:
time: 140 us
  Pallas kernels  139 us (99%)
    pallas_call x1, Pallas kernels, backward(): pl.pallas_call(backward_kernel, in_specs=[pl.BlockSpec(memory_space=pltpu...  71.6 us
    pallas_call x1, Pallas kernels, forward(): pl.pallas_call(forward_kernel, in_specs=[anywhere, anywhere, vmem, anywhe...  62.9 us
    pallas_call x1, Pallas kernels, results(): pl.pallas_call(results_kernel, grid=(steps,), in_specs=specs, out_specs=s...  4.11 us

profile of v7, /device:TPU:1, one launch (start us, length us, event | category | flops | bytes accessed | tf_op | source)
XLA Modules:
  0.0 139.9 jit_solution(12203210913877369069)
XLA Ops:
  0.6 62.9 %shard_map.155 = (bf16[256,1024]{1,0:T(8,128)(2,1)}, bf16[16,256,1024]{2,1,0:T(8,128)(2,1)}, bf16[16,512,256]{2,1,0:T(8,128)(2,1)}, bf16[4,256,1024]{2,1,0:T(8,1...) custom-call(bf16[256,8192]{1,0:T(8,128)(2,1)} %tokens_ref.3, bf16[256,1024]{1,0:T(8,128)(2,1)} %w_ref.1, ...), custom_call_target="tpu_custom_call" | custom-call | flops 11324620800 | bytes 41943040 | tf_op jit(solution)/shard_map/pallas_call | solution.py:353
  63.5 71.6 %shard_map.156 = (bf16[256,1024]{1,0:T(8,128)(2,1)}, f32[256,1024]{1,0:T(8,128)}, bf16[256,2048]{1,0:T(8,128)(2,1)}, bf16[256,896]{1,0:T(8,128)(2,1)}, f32[1,256]{1,0:T(1,128)}) custom-call(s32[4]{0:T(128)} %counts.1, bf16[256,1024]{1,0:T(8,128)(2,1)} %get-tuple-element.20.q_ref, bf16[4,256,1024]{2,1,0:T(8,128)(2,1)} %get-tuple-element.21.k_ref, ...), custom_call_target="tpu_custom_call" | custom-call | flops 12884901888 | bytes 31457280 | tf_op jit(solution)/shard_map/pallas_call | solution.py:788
  135.2 0.0 copy-start
  135.2 4.1 %shard_map.157 = (bf16[256,1024]{1,0:T(8,128)(2,1)}, f32[256,1024]{1,0:T(8,128)}, bf16[256,2048]{1,0:T(8,128)(2,1)}, bf16[256,896]{1,0:T(8,128)(2,1)}) custom-call(bf16[256,1024]{1,0:T(8,128)(2,1)} %get-tuple-element.26.refs_0_, f32[256,1024]{1,0:T(8,128)} %get-tuple-element.27.refs_1_, bf16[256,2048]{1,0:T(8,128)(2,1)} %get-tuple-element.28.refs_2_, ...), custom_call_target="tpu_custom_call" | custom-call | tf_op jit(solution)/shard_map/pallas_call | solution.py:865
  139.3 0.0 copy-done
  139.3 0.6 copy.18
Async XLA Ops:
  135.2 4.1 %copy-start = (f32[1,256]{1,0:T(1,128)S(1)}, f32[1,256]{1,0:T(1,128)}, u32[]{:S(2)}) copy-start(f32[1,256]{1,0:T(1,128)} %get-tuple-element.34) | copy-start | bytes 3076

commit v8 on v7

--- a/solution.py
+++ b/solution.py
@@ -415,7 +415,7 @@
     inverse_ref, gain_ref,
     ctx_ref, dw_ref, dh_ref, de_ref, dots_ref,
     qs, dos, ks, vs, wk, wv, ctx, score_s, dprob_s, weight_s, dscore_s, sum_s,
-    dq2, dq_t, nrm, wc, prod, dw_t, part, rn1, rn2, out_sib, in_sib,
+    dq2, dq_t, nrm, wc, prod, dw_t, dw_s, part, rn1, rn2, out_sib, in_sib,
     grads, g1, gs, g2, gfin, gin, sums, sums_in, tok, column,
     ra1_00, ra1_01, ra1_10, ra1_11, ra2_00, ra2_01, ra2_10, ra2_11,
     rb1_00, rb1_01, rb1_10, rb1_11, rb2_00, rb2_01, rb2_10, rb2_11,
@@ -574,7 +574,8 @@
                 total + rb2[group][half][0].astype(F32) + rb2[group][half][1].astype(F32)
             )
         for low in range(0, stop - first, 128):
-            dw_ref[:, first + low : first + low + 128] = jnp.transpose(dw_t[low : low + 128])
+            dw_s[:, first + low : first + low + 128] = jnp.transpose(dw_t[low : low + 128])
+        write(dw_s.at[:, first:stop], dw_ref.at[:, first:stop])
 
     def partial(k):
         part[k] = dot(dq2[...], wc[k], LAST).astype(BF16)
@@ -588,7 +589,9 @@
                  (part.at[far * 4 + m, 256:512], rn1.at[m, 1]))
         )
 
-    def near_partial(m):
+    def summed_partial(m):
+        partial(up * 4 + m)
+        partial(down * 4 + m)
         n1[m][0].wait_recv()
         piece = part.at[up * 4 + m, 0:256]
         added(piece, piece, rn1.at[m, 0])
@@ -657,11 +660,14 @@
     product(0, 2, 2)
     first_hop(0, 1, 2)
     first_hop(0, 0, 2)
-    for line in (1, 3, 0):
+
+    def leading(line):
         product(0, 2, line)
         first_hop(0, 1, line)
         product(0, line, 2)
         first_hop(0, 0, line)
+
+    leading(1)
     attention(up, 1)
     attention(down, 1)
     encoded_grad(up)
@@ -673,6 +679,8 @@
     gs[1, 0:128] = grads[down, 0:128]
     gs[1, 128:256] = (grads[down, 128:256].astype(F32) + g1[1].astype(F32)).astype(BF16)
     c_g2 = both("x", (gs.at[0], g2.at[0]), (gs.at[1], g2.at[1]))
+    leading(3)
+    leading(0)
     second_hop(0, 1, 2)
     second_hop(0, 0, 2)
     attention(at.x, 1)
@@ -717,28 +725,22 @@
     for line in (1, 3):
         second_hop(1, 0, line)
         second_hop(1, 1, line)
+    summed_partial(0)
     encoded_grad(at.x)
     for copy in c_g2:
         copy.wait_recv()
     gfin[...] = (grads[at.x].astype(F32) + g2[0].astype(F32) + g2[1].astype(F32)).astype(BF16)
     c_swap = send(gfin, gin, at.partner())
-    for m in range(4):
-        partial(up * 4 + m)
-        partial(down * 4 + m)
-        near_partial(m)
+    for m in range(1, 4):
+        summed_partial(m)
     for dy, dz in rest:
         product(1, dy, dz)
-    second_hop(0, 0, 0)
-    second_hop(1, 0, 0)
     gathered(1, 0, 2)
     turn(1, 0)
     gathered(1, 1, 2)
     turn(1, 1)
+    second_hop(0, 0, 0)
     second_hop(0, 1, 0)
-    gathered(1, 0, 1)
-    gathered(1, 0, 3)
-    turned(1, 0)
-    second_hop(1, 1, 0)
 
     for copy in c_sums:
         copy.wait_recv()
@@ -750,20 +752,25 @@
     for m in range(4):
         partial(at.x * 4 + m)
     normed_sum(0)
-    normed_sum(1)
-    sibling_part(0)
+    gathered(1, 0, 1)
+    gathered(1, 0, 3)
+    turned(1, 0)
+    second_hop(1, 1, 0)
     gathered(1, 1, 1)
     gathered(1, 1, 3)
     turned(1, 1)
+    second_hop(1, 0, 0)
+    normed_sum(1)
+    sibling_part(0)
     normed_sum(2)
     sibling_part(1)
     result(0)
-    normed_sum(3)
-    sibling_part(2)
-    sibling_part(3)
-    result(1)
     c_swap.wait_recv()
     write(gin, de_ref)
+    sibling_part(2)
+    normed_sum(3)
+    result(1)
+    sibling_part(3)
     for copy in send.copies:
         copy.wait_send()
     for copy in outs:
@@ -788,7 +795,7 @@
     return pl.pallas_call(
         backward_kernel,
         in_specs=[pl.BlockSpec(memory_space=pltpu.SMEM)] + [anywhere] * 9 + [vmem, vmem],
-        out_specs=[anywhere, vmem, anywhere, anywhere, vmem],
+        out_specs=[anywhere] * 4 + [vmem],
         out_shape=[
             jax.ShapeDtypeStruct((rows, width), BF16),
             jax.ShapeDtypeStruct((256, width), F32),
@@ -815,6 +822,7 @@
             buffer(16, 256, 1024),
             buffer(16, 1024, 256),
             buffer(768, 256, kind=F32),
+            buffer(256, width, kind=F32),
             buffer(16, 512, 256),
             buffer(4, 2, 256, 256),
             buffer(4, 2, 512, 256),
@@ -837,7 +845,7 @@
         + [buffer(2, size, 256) for size in sizes]
         + [
             pltpu.SemaphoreType.DMA((LOADS,)),
-            pltpu.SemaphoreType.DMA((10,)),
+            pltpu.SemaphoreType.DMA((12,)),
             pltpu.SemaphoreType.DMA((BACKWARD_SENDS,)),
             pltpu.SemaphoreType.DMA((BACKWARD_SENDS,)),
         ],
@@ -851,23 +859,38 @@
 
 
 def results_kernel(*refs):
-    count = len(refs) // 2
-    for source, target in zip(refs[:count], refs[count:]):
-        target[...] = source[...]
+    count = (len(refs) - 2) // 3
+    in_sem, out_sem = refs[-2:]
+    coming, going = [], []
+    for source, target, held in zip(refs, refs[count:], refs[2 * count : 3 * count]):
+        pieces = min(2, source.shape[0])
+        rows = source.shape[0] // pieces
+        for i in range(pieces):
+            piece, index = pl.ds(i * rows, rows), len(coming)
+            coming.append(
+                pltpu.make_async_copy(source.at[piece], held.at[piece], in_sem.at[index])
+            )
+            going.append(
+                pltpu.make_async_copy(held.at[piece], target.at[piece], out_sem.at[index])
+            )
+    for copy in coming:
+        copy.start()
+    for arrived, copy in zip(coming, going):
+        arrived.wait()
+        copy.start()
+    for copy in going:
+        copy.wait()
 
 
 def results(*arrays):
-    steps = 4
-    specs = [
-        pl.BlockSpec((array.shape[0] // steps, array.shape[1]), lambda i: (i, 0))
-        for array in arrays
-    ]
+    anywhere = pl.BlockSpec(memory_space=pl.ANY)
     return pl.pallas_call(
         results_kernel,
-        grid=(steps,),
-        in_specs=specs,
-        out_specs=specs,
+        in_specs=[anywhere] * len(arrays),
+        out_specs=[anywhere] * len(arrays),
         out_shape=[jax.ShapeDtypeStruct(array.shape, array.dtype) for array in arrays],
+        scratch_shapes=[pltpu.VMEM(array.shape, array.dtype) for array in arrays]
+        + [pltpu.SemaphoreType.DMA((2 * len(arrays),))] * 2,
         compiler_params=pltpu.CompilerParams(vmem_limit_bytes=62 * 2**20),
     )(*arrays)
 
@@ -895,8 +918,8 @@
         counts, queries, keys, values, d_context, w_key, w_value, normed, w_part, tokens, inverse,
         gain,
     )
-    context, d_query_weight, d_hidden, d_encoded = results(
-        context, d_query_weight, d_hidden, d_encoded
+    context, d_query_weight, d_hidden, d_encoded, row_dots = results(
+        context, d_query_weight, d_hidden, d_encoded, row_dots
     )
     return (
         context,

time: 140 us -> 139 us (level)
  Pallas kernels: 139 us -> 137 us
where the time goes in v8:
time: 139 us; the launch traced here: 138 us
  Pallas kernels  137 us (99%)
    pallas_call x1, Pallas kernels, backward(): pl.pallas_call(backward_kernel, in_specs=[pl.BlockSpec(memory_space=pltpu...  71 us
    pallas_call x1, Pallas kernels, forward(): pl.pallas_call(forward_kernel, in_specs=[anywhere, anywhere, vmem, anywhe...  62.9 us
    pallas_call x1, Pallas kernels, results(): pl.pallas_call(results_kernel, in_specs=[anywhere] * len(arrays), out_spe...  2.83 us

profile of v8, /device:TPU:1, one launch (start us, length us, event | category | flops | bytes accessed | tf_op | source)
XLA Modules:
  0.0 137.5 jit_solution(16691635334326955942)
XLA Ops:
  0.6 62.9 %shard_map.155 = (bf16[256,1024]{1,0:T(8,128)(2,1)}, bf16[16,256,1024]{2,1,0:T(8,128)(2,1)}, bf16[16,512,256]{2,1,0:T(8,128)(2,1)}, bf16[4,256,1024]{2,1,0:T(8,1...) custom-call(bf16[256,8192]{1,0:T(8,128)(2,1)} %tokens_ref.3, bf16[256,1024]{1,0:T(8,128)(2,1)} %w_ref.1, ...), custom_call_target="tpu_custom_call" | custom-call | flops 11324620800 | bytes 41943040 | tf_op jit(solution)/shard_map/pallas_call | solution.py:353
  63.5 71.0 %shard_map.156 = (bf16[256,1024]{1,0:T(8,128)(2,1)}, f32[256,1024]{1,0:T(8,128)}, bf16[256,2048]{1,0:T(8,128)(2,1)}, bf16[256,896]{1,0:T(8,128)(2,1)}, f32[1,256]{1,0:T(1,128)}) custom-call(s32[4]{0:T(128)} %counts.1, bf16[256,1024]{1,0:T(8,128)(2,1)} %get-tuple-element.21.q_ref, bf16[4,256,1024]{2,1,0:T(8,128)(2,1)} %get-tuple-element.22.k_ref, ...), custom_call_target="tpu_custom_call" | custom-call | flops 12884901888 | bytes 31457280 | tf_op jit(solution)/shard_map/pallas_call | solution.py:795
  134.5 2.8 %shard_map.157 = (bf16[256,1024]{1,0:T(8,128)(2,1)}, f32[256,1024]{1,0:T(8,128)}, bf16[256,2048]{1,0:T(8,128)(2,1)}, bf16[256,896]{1,0:T(8,128)(2,1)}, f32[1,256]{1,0:T(1,128)}) custom-call(bf16[256,1024]{1,0:T(8,128)(2,1)} %get-tuple-element.27.refs_0_, f32[256,1024]{1,0:T(8,128)} %get-tuple-element.28.refs_1_, ...), custom_call_target="tpu_custom_call" | custom-call | tf_op jit(solution)/shard_map/pallas_call | solution.py:887

commit v9 on v8

--- a/solution.py
+++ b/solution.py
@@ -327,18 +327,26 @@
     accumulate([(2, 1), (2, 3), (1, 2), (3, 2)])
     landed(0, 2)
     landed(1, 2)
-    accumulate([(2, 2)])
-    q_send[...] = acc[256:512].astype(BF16)
-    c_q = send(q_send, q_in, at.sibling())
-    c_q.wait_recv()
-    q_ref[...] = (acc[0:256] + q_in[...].astype(F32)).astype(BF16)
+    final = at.chunk(2, 2)
+    write(wc.at[final], w_out.at[final])
+    c_q = []
+    parts = (slice(0, 512), slice(512, 1024))
+    for cols in parts:
+        total = acc[256:512, cols] + dot(nrm[final, 256:512], wc[final, :, cols])
+        q_send[:, cols] = total.astype(BF16)
+        c_q.append(send(q_send.at[:, cols], q_in.at[:, cols], at.sibling()))
+    for cols in parts:
+        acc[0:256, cols] = acc[0:256, cols] + dot(nrm[final, 0:256], wc[final, :, cols])
+    for cols, copy in zip(parts, c_q):
+        copy.wait_recv()
+        q_ref[:, cols] = (acc[0:256, cols] + q_in[:, cols].astype(F32)).astype(BF16)
     for copy in send.copies:
         copy.wait_send()
     for copy in outs:
         copy.wait()
 
 
-FORWARD_SENDS = 4 + 1 + 4 + 2 * 6 + 2 * 2 + 16 + 2 + 2 + 1 + 2 + 2 + 1
+FORWARD_SENDS = 4 + 1 + 4 + 2 * 6 + 2 * 2 + 16 + 2 + 2 + 1 + 2 + 2 + 2
 
 
 def forward(tokens, w_query, gain, state_kv, near, enc_gain, enc_query, enc_out, w_key, w_value):
@@ -402,7 +410,7 @@
 
 LINES = (2, 1, 3, 0)
 GROUPS = ((0, 384, 160), (384, 1024, 224))
-LOADS = 16
+LOADS = 20
 
 
 def halves(group):
@@ -428,10 +436,12 @@
     ra2 = ((ra2_00, ra2_01), (ra2_10, ra2_11))
     rb1 = ((rb1_00, rb1_01), (rb1_10, rb1_11))
     rb2 = ((rb2_00, rb2_01), (rb2_10, rb2_11))
-    pairs = [
-        (q_ref, qs), (do_ref, dos), (k_ref, ks), (v_ref, vs), (wk_ref, wk), (wv_ref, wv),
-        (nrm_ref, nrm), (w_ref, wc),
-    ]
+    pairs = []
+    for first, stop, _ in GROUPS:
+        cols = slice(first, stop)
+        pairs += [(source.at[:, cols], target.at[:, cols]) for source, target in ((q_ref, qs), (do_ref, dos))]
+        pairs += [(source.at[:, :, cols], target.at[:, :, cols]) for source, target in ((k_ref, ks), (v_ref, vs))]
+    pairs += [(wk_ref, wk), (wv_ref, wv), (nrm_ref, nrm), (w_ref, wc)]
     for i in range(8):
         first = pl.multiple_of(at.x * share + i * 256, 256)
         pairs.append((tokens_ref.at[:, pl.ds(first, 256)], tok.at[i]))
@@ -650,7 +660,7 @@
     c_dq = [share_dq(0)]
     own, other = slice(0, 256), slice(256, 512)
     transposed(0, own)
-    for load in loads[4:8]:
+    for load in loads[4:12]:
         load.wait()
     attention(far, 1)
     encoded_grad(far)
@@ -747,7 +757,7 @@
     whole = sums[...] + sums_in[0] + sums_in[1] + sums_in[2]
     dots_ref[...] = whole[0:1] * (1.0 / math.sqrt(width))
     column[...] = jnp.transpose(jnp.broadcast_to(whole[0:1], (128, 256)))
-    for load in loads[8:]:
+    for load in loads[12:]:
         load.wait()
     for m in range(4):
         partial(at.x * 4 + m)

time: 139 us -> 138 us (level)
  no operation moved by 1% of the time
where the time goes in v9:
time: 138 us; the launch traced here: 137 us
  Pallas kernels  136 us (99%)
    pallas_call x1, Pallas kernels, backward(): pl.pallas_call(backward_kernel, in_specs=[pl.BlockSpec(memory_space=pltpu...  70.8 us
    pallas_call x1, Pallas kernels, forward(): pl.pallas_call(forward_kernel, in_specs=[anywhere, anywhere, vmem, anywhe...  62.1 us
    pallas_call x1, Pallas kernels, results(): pl.pallas_call(results_kernel, in_specs=[anywhere] * len(arrays), out_spe...  2.83 us

profile of v9, /device:TPU:1, one launch (start us, length us, event | category | flops | bytes accessed | tf_op | source)
XLA Modules:
  0.0 136.6 jit_solution(1547322333405474560)
XLA Ops:
  0.6 62.1 %shard_map.155 = (bf16[256,1024]{1,0:T(8,128)(2,1)}, bf16[16,256,1024]{2,1,0:T(8,128)(2,1)}, bf16[16,512,256]{2,1,0:T(8,128)(2,1)}, bf16[4,256,1024]{2,1,0:T(8,1...) custom-call(bf16[256,8192]{1,0:T(8,128)(2,1)} %tokens_ref.3, bf16[256,1024]{1,0:T(8,128)(2,1)} %w_ref.1, ...), custom_call_target="tpu_custom_call" | custom-call | flops 11324620800 | bytes 41943040 | tf_op jit(solution)/shard_map/pallas_call | solution.py:361
  62.7 70.8 %shard_map.156 = (bf16[256,1024]{1,0:T(8,128)(2,1)}, f32[256,1024]{1,0:T(8,128)}, bf16[256,2048]{1,0:T(8,128)(2,1)}, bf16[256,896]{1,0:T(8,128)(2,1)}, f32[1,256]{1,0:T(1,128)}) custom-call(s32[4]{0:T(128)} %counts.1, bf16[256,1024]{1,0:T(8,128)(2,1)} %get-tuple-element.21.q_ref, bf16[4,256,1024]{2,1,0:T(8,128)(2,1)} %get-tuple-element.22.k_ref, ...), custom_call_target="tpu_custom_call" | custom-call | flops 12884901888 | bytes 31457280 | tf_op jit(solution)/shard_map/pallas_call | solution.py:805
  133.6 2.8 %shard_map.157 = (bf16[256,1024]{1,0:T(8,128)(2,1)}, f32[256,1024]{1,0:T(8,128)}, bf16[256,2048]{1,0:T(8,128)(2,1)}, bf16[256,896]{1,0:T(8,128)(2,1)}, f32[1,256]{1,0:T(1,128)}) custom-call(bf16[256,1024]{1,0:T(8,128)(2,1)} %get-tuple-element.27.refs_0_, f32[256,1024]{1,0:T(8,128)} %get-tuple-element.28.refs_1_, ...), custom_call_target="tpu_custom_call" | custom-call | tf_op jit(solution)/shard_map/pallas_call | solution.py:897

commit v10 on v9

--- a/solution.py
+++ b/solution.py
@@ -409,7 +409,7 @@
 
 
 LINES = (2, 1, 3, 0)
-GROUPS = ((0, 384, 160), (384, 1024, 224))
+GROUPS = ((0, 384, 192), (384, 1024, 224))
 LOADS = 20
 
 

time: 138 us -> 137 us (level)
  no operation moved by 1% of the time
where the time goes in v10:
time: 137 us
  Pallas kernels  136 us (99%)
    pallas_call x1, Pallas kernels, backward(): pl.pallas_call(backward_kernel, in_specs=[pl.BlockSpec(memory_space=pltpu...  71.1 us
    pallas_call x1, Pallas kernels, forward(): pl.pallas_call(forward_kernel, in_specs=[anywhere, anywhere, vmem, anywhe...  62.1 us
    pallas_call x1, Pallas kernels, results(): pl.pallas_call(results_kernel, in_specs=[anywhere] * len(arrays), out_spe...  2.83 us

profile of v10, /device:TPU:1, one launch (start us, length us, event | category | flops | bytes accessed | tf_op | source)
XLA Modules:
  0.0 136.8 jit_solution(15764609844638360041)
XLA Ops:
  0.6 62.1 %shard_map.155 = (bf16[256,1024]{1,0:T(8,128)(2,1)}, bf16[16,256,1024]{2,1,0:T(8,128)(2,1)}, bf16[16,512,256]{2,1,0:T(8,128)(2,1)}, bf16[4,256,1024]{2,1,0:T(8,1...) custom-call(bf16[256,8192]{1,0:T(8,128)(2,1)} %tokens_ref.3, bf16[256,1024]{1,0:T(8,128)(2,1)} %w_ref.1, ...), custom_call_target="tpu_custom_call" | custom-call | flops 11324620800 | bytes 41943040 | tf_op jit(solution)/shard_map/pallas_call | solution.py:361
  62.7 71.1 %shard_map.156 = (bf16[256,1024]{1,0:T(8,128)(2,1)}, f32[256,1024]{1,0:T(8,128)}, bf16[256,2048]{1,0:T(8,128)(2,1)}, bf16[256,896]{1,0:T(8,128)(2,1)}, f32[1,256]{1,0:T(1,128)}) custom-call(s32[4]{0:T(128)} %counts.1, bf16[256,1024]{1,0:T(8,128)(2,1)} %get-tuple-element.21.q_ref, bf16[4,256,1024]{2,1,0:T(8,128)(2,1)} %get-tuple-element.22.k_ref, ...), custom_call_target="tpu_custom_call" | custom-call | flops 12884901888 | bytes 31457280 | tf_op jit(solution)/shard_map/pallas_call | solution.py:805
  133.8 2.8 %shard_map.157 = (bf16[256,1024]{1,0:T(8,128)(2,1)}, f32[256,1024]{1,0:T(8,128)}, bf16[256,2048]{1,0:T(8,128)(2,1)}, bf16[256,896]{1,0:T(8,128)(2,1)}, f32[1,256]{1,0:T(1,128)}) custom-call(bf16[256,1024]{1,0:T(8,128)(2,1)} %get-tuple-element.27.refs_0_, f32[256,1024]{1,0:T(8,128)} %get-tuple-element.28.refs_1_, ...), custom_call_target="tpu_custom_call" | custom-call | tf_op jit(solution)/shard_map/pallas_call | solution.py:897
